TPU v7x, 32 devices: a whole 2x2x4 slice. The times are simulated.
32 devices in a mesh: groups: 2 (over y), blk: 4 (over z), fsdp: 2 (over x), sub: 2 (over core).
Axes of the slice: x: 2, y: 2, z: 4, core: 2. Of those that a mesh axis runs over, the one named last changes fastest.
Arguments:
- grad_out: bfloat16 [2048, 8192], P(('groups', 'blk'), 'sub'), parts along dimension 0, may hold values from -6 to 6
- inputs: bfloat16 [2048, 8192], P(('groups', 'blk'), ('fsdp', 'sub')), parts along dimension 0, may hold values from -6 to 6
- gate_act: bfloat16 [2048, 14336], P(('groups', 'blk'), ('fsdp', 'sub')), parts along dimension 0, may hold values from -6 to 6
- w_down: bfloat16 [14336, 8192], P(('fsdp', 'sub'), 'blk'), may hold values from -0.0625 to 0.0625
- proj_in: bfloat16 [8192, 64], P(('fsdp', 'sub')), may hold values from -0.0625 to 0.0625
- proj_out: bfloat16 [14336, 64], P(('fsdp', 'sub')), may hold values from -0.046875 to 0.046875
- queries: bfloat16 [8, 16, 4096], P(('groups', 'blk'), 'fsdp', 'sub'), parts along dimension 0, may hold values from -0.015625 to 0.015625
- example_of: int32 [2048], P(('groups', 'blk')), parts along dimension 0, may hold values from 0 to 7, as said below
Outputs:
- sketches: bfloat16 [64, 4096], P(('groups', 'blk'), 'sub'), parts along dimension 0
- scores: float32 [64, 4, 16], P(('groups', 'blk'), None, ('fsdp', 'sub')), parts along dimension 0
There are 2 independent parts, one for each index of `groups`. A program takes and returns all parts, laid end to end along the dimension named above; an argument that names none is the same for every part. Nothing has to cross between parts.
Inputs may be any that keep to these rules, and one draw needn't show every extreme that they name: `example_of`: within each aligned block of 256 tokens the numbers never fall and each of 0 to 7 appears.
All inputs are finite; a program needn't handle non-finite values.
Results may differ from a plain program's by a relative error of at most 0.0032.
Values may be sent and summed in bfloat16 or wider, within the bound.
No kernel may reach another device: no remote copies, remote signals or barrier semaphores. Data moves between devices by JAX's collectives and lax.ppermute only.
A program may use at most 192 MiB of HBM per device.

v0:
```python
import jax
import jax.numpy as jnp
from jax import lax
from jax.sharding import PartitionSpec as P

R = 64
EX_DEV = 8


def from_behind(block, axis, distance):
    devices = range(lax.axis_size(axis))
    route = [((i - distance) % len(devices), i) for i in devices]
    return lax.ppermute(block, axis, route)


def forward_step(block):
    return from_behind(block, "blk", 1)


def local(grad_out, inputs, gate_act, w_down, proj_in, proj_out, queries, example_of):
    tok_rows = grad_out.shape[0]
    full_grads = lax.all_gather(grad_out, "sub", axis=1, tiled=True)
    part_in = jnp.dot(inputs, proj_in, preferred_element_type=jnp.float32)
    proj32 = proj_out.astype(jnp.float32)
    hidden_grad = lax.dot_general(
        full_grads,
        lax.all_gather(w_down, "blk", axis=1, tiled=True),
        (((1,), (1,)), ((), ())),
        preferred_element_type=jnp.float32,
    )
    part_out = jnp.dot(
        hidden_grad * gate_act.astype(jnp.float32), proj32, precision=lax.Precision.HIGHEST
    )
    left_proj, up_proj = lax.psum((part_in, part_out), ("fsdp", "sub"))
    half_rank = R // 2
    left_half = lax.dynamic_slice_in_dim(left_proj, lax.axis_index("sub") * half_rank, half_rank, 1)
    onehot = (example_of[:, None] == jnp.arange(EX_DEV, dtype=jnp.int32)[None, :]).astype(
        jnp.float32
    )
    weighted = (onehot[:, :, None] * left_half[:, None, :]).reshape(tok_rows, EX_DEV * half_rank)
    full_sketch = jnp.dot(weighted.T, up_proj, precision=lax.Precision.HIGHEST)
    sketch_bf = full_sketch.reshape(EX_DEV, half_rank * R).astype(jnp.bfloat16)
    nblk = lax.axis_size("blk")
    here = lax.axis_index("blk")
    own_block = queries[0]

    def score(block):
        return lax.dot_general(
            sketch_bf, block, (((1,), (1,)), ((), ())), preferred_element_type=jnp.float32
        )

    def place(table, block, source):
        return lax.dynamic_update_slice(
            table, score(block)[:, None, :], (jnp.int32(0), source, jnp.int32(0))
        )

    table = jnp.zeros((EX_DEV, nblk, own_block.shape[0]), jnp.float32)
    table = place(table, own_block, here)

    def one_turn(step, carry):
        block, acc = carry
        block = forward_step(block)
        return (block, place(acc, block, (here - step) % nblk))

    own_block, table = lax.fori_loop(1, nblk, one_turn, (own_block, table))
    scores = lax.psum_scatter(table, "sub", scatter_dimension=2, tiled=True)
    return (sketch_bf, scores)


def solution(mesh):
    in_specs = (
        P(("groups", "blk"), "sub"),
        P(("groups", "blk"), ("fsdp", "sub")),
        P(("groups", "blk"), ("fsdp", "sub")),
        P(("fsdp", "sub"), "blk"),
        P(("fsdp", "sub"), None),
        P(("fsdp", "sub"), None),
        P(("groups", "blk"), "fsdp", "sub"),
        P(("groups", "blk")),
    )
    out_specs = (P(("groups", "blk"), "sub"), P(("groups", "blk"), None, ("fsdp", "sub")))
    return jax.shard_map(local, mesh=mesh, in_specs=in_specs, out_specs=out_specs, check_vma=False)
```

profile of v0, /device:TPU:0, one launch (start us, length us, event | category | flops | bytes accessed | tf_op | source)
XLA Modules:
  0.0 1094.8 jit_solution(8071187166289558350)
XLA Ops:
  7.2 0.0 copy-start
  7.2 0.0 all-gather.3.cloned.1.call-start
  7.2 0.8 copy.32
  8.1 0.0 all-gather.3.cloned.1.call-update
  8.1 0.0 copy-start.4
  8.1 0.0 copy-start.6
  8.1 0.0 all-gather.5.cloned.1.call-start
  8.2 0.7 all-gather.5.cloned.1.call-update
  8.9 0.0 all-reduce.4.cloned.1.call-start
  8.9 0.0 copy-done
  8.9 0.2 copy-done.4
  9.1 1.1 fusion.4
  10.2 0.0 copy-start.3
  10.2 15.8 %all-gather.3.cloned.1.call-done = bf16[256,8192]{1,0:T(8,128)(2,1)} async-done(((bf16[256,4096]{1,0:T(8,128)(2,1)}), bf16[256,8192]{1,0:T(8,128)(2,1)}) %all-gather.3.cloned.1.call-update) | async-done | bytes 4194320 | tf_op jit(solution)/shard_map/all_gather | solution.py:22
  26.0 977.2 %all-gather.5.cloned.1.call-done = bf16[3584,8192]{1,0:T(8,128)(2,1)} async-done(((bf16[3584,2048]{1,0:T(8,128)(2,1)}), bf16[3584,8192]{1,0:T(8,128)(2,1)}) %all-gather.5.cloned.1.call-update) | async-done | bytes 58720272 | tf_op jit(solution)/shard_map/all_gather | solution.py:27
  1003.1 0.0 copy-done.6
  1003.2 0.0 copy-start.1
  1003.2 26.6 %convolution_multiply_fusion = f32[256,3584]{1,0:T(8,128)} fusion(bf16[256,8192]{1,0:T(8,128)(2,1)} %all-gather.3.cloned.1.call-done, bf16[3584,8192]{1,0:T(8,128)(2,1)} %all-gather.5.cloned.1.call-done, bf16[256,3584]{1,0:T(8,128)(2,1)S(1)} %copy-done.6), kind=kOutput, calls=%fused_computation.2 | convolution fusion | flops 15034220544 | bytes 68419584 | tf_op jit(solution)/shard_map/dot_general | solution.py:25
  1029.7 0.0 copy-done.3
  1029.7 0.0 copy-start.5
  1029.7 0.0 copy-start.7
  1029.7 4.7 fusion.5
  1034.4 0.0 all-reduce.4.cloned.1.call-update
  1034.4 0.0 copy-done.5
  1034.5 0.0 copy-done.7
  1034.5 0.6 dynamic-slice
  1035.8 28.5 %all-reduce.4.cloned.1.call-done = (f32[256,64]{0,1:T(8,128)}, f32[256,64]{0,1:T(8,128)}) async-done(((f32[256,64]{0,1:T(8,128)}, f32[256,64]{0,1:T(8,128)}), (f32[256,64]{0,1:T(8,128)}, f32[256,64]{0,1:T(8,128)})) %all-reduce.4.cloned.1.call-update) | async-done | bytes 131088 | tf_op jit(solution)/shard_map/psum | solution.py:34
  1064.3 0.8 constant_dynamic-slice_fusion.1
  1065.1 1.2 convolution_convert_fusion
  1066.3 0.1 copy.14
  1066.4 0.1 convert_element_type.21
  1066.6 0.1 fusion.1
  1066.7 17.5 %while.17 = (s32[]{:T(128)}, bf16[8,2048]{1,0:T(8,128)(2,1)S(1)}, f32[8,4,8]{2,0,1:T(8,128)S(1)}, bf16[8,2048]{1,0:T(8,128)(2,1)S(1)}, s32[]{:T(128)}, /*index=5*/s32[]{:T(128)}, s32[]{:T(128)}, s32[]{:T(128)}, s32[]{:T(128)}) while((s32[]{:T(128)}, bf16[8,2048]{1,0:T(8,128)(2,1)S(1)}, f32[8,4,8]{2,0,1:T(8,128)S(1)}, ...), condition=%wide.region_3.4_spmd, body=%wide.region_2.3_spmd.sunk | while | flops 262161 | bytes 266532 | solution.py:65
  1066.7 1.5 collective-permute-start
  1068.2 4.2 collective-permute-done
  1072.4 0.1 fusion.22
  1072.5 0.0 collective-permute-start
  1072.5 5.7 collective-permute-done
  1078.3 0.1 fusion.22
  1078.4 0.0 collective-permute-start
  1078.4 5.7 collective-permute-done
  1084.1 0.1 fusion.22
  1084.2 0.0 copy-start.2
  1084.2 0.1 copy.15
  1084.3 3.4 all-reduce
  1087.7 0.6 constant_dynamic-slice_fusion
  1088.3 0.0 copy-done.2
  1088.3 0.0 copy-done.1
  (6 shorter events, 0.0 us)
Async XLA Ops:
  7.2 1.8 copy-start
  7.2 18.8 %all-gather.3.cloned.1.call-start = ((), (), s32[]{:S(2)}) async-start(), calls=%async_computation | async-start | bytes 6291456 | tf_op jit(solution)/shard_map/all_gather | solution.py:22
  8.1 1.0 copy-start.4
  8.1 995.0 %copy-start.6 = (bf16[256,3584]{1,0:T(8,128)(2,1)S(1)}, bf16[256,3584]{1,0:T(8,128)(2,1)}, u32[]{:S(2)}) copy-start(bf16[256,3584]{1,0:T(8,128)(2,1)} %param.12) | copy-start | bytes 5505028
  8.1 995.0 %all-gather.5.cloned.1.call-start = ((), (), s32[]{:S(2)}) async-start(), calls=%async_computation.1 | async-start | bytes 73400320 | tf_op jit(solution)/shard_map/all_gather | solution.py:27
  8.9 1055.4 %all-reduce.4.cloned.1.call-start = ((), (), s32[]{:S(2)}) async-start(), calls=%async_computation.2 | async-start | bytes 262144 | tf_op jit(solution)/shard_map/psum | solution.py:34
  10.2 1019.5 %copy-start.3 = (bf16[3584,64]{0,1:T(8,128)(2,1)S(1)}, bf16[3584,64]{0,1:T(8,128)(2,1)}, u32[]{:S(2)}) copy-start(bf16[3584,64]{0,1:T(8,128)(2,1)} %param.15) | copy-start | bytes 1376260
  1003.2 85.1 %copy-start.1 = (bf16[256,2048]{1,0:T(8,128)(2,1)S(1)}, bf16[256,2048]{1,0:T(8,128)(2,1)}, u32[]{:S(2)}) copy-start(bf16[256,2048]{1,0:T(8,128)(2,1)} %param.11) | copy-start | bytes 3145732
  1029.7 4.7 copy-start.5
  1029.7 4.7 copy-start.7
  1066.7 5.7 collective-permute-start
  1072.5 5.7 collective-permute-start
  1078.4 5.7 collective-permute-start
  1084.2 4.0 copy-start.2
Sparse Core Ops, SparseCore 0:
  9.6 16.3 all-gather.2
  27.5 975.5 all-gather.4
  1034.6 29.6 all-reduce.3
where the time goes:
time: 1100 us; the launch traced here: 1090 us
  waiting for transfers between devices  1040 us (95%)
  matrix products  34 us (3%)
  between operations  14.5 us (1%)
    all_gather x1, waiting for transfers between devices, local(): lax.all_gather(w_down, 'blk', axis=1, tiled=True)  977 us
    psum x1, waiting for transfers between devices, local(): left_proj, up_proj = lax.psum((part_in, part_out), ('fsdp', 'sub'))  28.5 us
    dot_general x1, matrix products, local(): lax.dot_general(full_grads, lax.all_gather(w_down, 'blk', axis=1, tiled=T...  26.6 us
  transfers between devices with their start and end apart: 6, of which 6 were waited for; matrix products, arithmetic and copies ran while one was open for 0% of the time, Pallas kernels for 0%

commit v1 on v0

v1 whole, which is shorter than its diff:
```python
import jax
import jax.numpy as jnp
from jax import lax
from jax.sharding import PartitionSpec as P

R = 64
EX_DEV = 8
CHUNKS = 2
F32 = jnp.float32
BF16 = jnp.bfloat16


def line_right(block):
    n = lax.axis_size("blk")
    return lax.ppermute(block, "blk", [(i, i + 1) for i in range(n - 1)])


def line_left(block):
    n = lax.axis_size("blk")
    return lax.ppermute(block, "blk", [(i + 1, i) for i in range(n - 1)])


def shifted(block, axis, distance):
    n = lax.axis_size(axis)
    return lax.ppermute(block, axis, [(i, (i + distance) % n) for i in range(n)])


def gathered(block, axis):
    n = lax.axis_size(axis)
    if n == 1:
        return block[None]
    here = lax.axis_index(axis)
    got = [block] + [shifted(block, axis, e) for e in range(1, n)]
    return jnp.stack([lax.select_n((here - i) % n, *got) for i in range(n)])


def summed(block, axes):
    for axis in axes:
        n = lax.axis_size(axis)
        step = 1
        while step < n:
            block = block + lax.ppermute(block, axis, [(i, i ^ step) for i in range(n)])
            step *= 2
    return block


def local(grad_out, inputs, gate_act, w_down, proj_in, proj_out, queries, example_of):
    n = lax.axis_size("blk")
    cores = lax.axis_size("sub")
    n_f = lax.axis_size("fsdp")
    z, x, core = lax.axis_index("blk"), lax.axis_index("fsdp"), lax.axis_index("sub")
    tok = grad_out.shape[0]
    hid, dblk = w_down.shape
    group = n // cores
    rows = tok // n_f
    half = tok // 2
    part = half // CHUNKS
    proj32 = proj_out.astype(F32)

    def project(block):
        return jnp.dot(block, proj32, precision=lax.Precision.HIGH)

    def features(p):
        mine = lax.dynamic_slice(grad_out, (x * rows, ((z + p) % group) * dblk), (rows, dblk))
        route = []
        for zs in range(n):
            for cs in range(cores):
                zd = cs * group + (zs + p) % group
                route.append((zs * cores + cs, zd * cores + zs // group))
        got = lax.ppermute(mine, ("blk", "sub"), route)
        whole = gathered(got, "fsdp").reshape(tok, dblk)
        return gathered(whole, "sub")

    order = list(range(1, group)) + [0]
    grads = {p: features(p) for p in order}

    hidden = {
        p: lax.dot_general(
            grads[p].reshape(cores * tok, dblk),
            w_down,
            (((1,), (1,)), ((), ())),
            preferred_element_type=F32,
        ).reshape(cores, tok, hid)
        for p in order
    }

    def hidden_of(distance, start, size):
        which = ((z - distance) % n) // group
        return lax.dynamic_slice(hidden[distance % group], (which, start, 0), (1, size, hid))[0]

    gates = {k: [] for k in range(1, n)}
    up_second = []
    for c in range(CHUNKS):
        own = gate_act[c * part : (c + 1) * part]
        from_left, from_right = [line_right(own)], [line_left(own)]
        for s in range(1, n):
            start = half + c * part
            mine = hidden_of(s, start, part)
            payload = from_left[-1].astype(F32) + jnp.where(z < s, mine, 0.0)
            from_left.append(line_right(payload.astype(BF16)))
            mine = hidden_of(n - s, start, part)
            payload = from_right[-1].astype(F32) + jnp.where(z + s >= n, mine, 0.0)
            from_right.append(line_left(payload.astype(BF16)))
        for k in range(1, n):
            gates[k].append(jnp.where(z >= k, from_left[k - 1], from_right[n - 1 - k]))
        total = hidden_of(0, start, part) + from_left[-1].astype(F32) + from_right[-1].astype(F32)
        up = project(total * gate_act[start : start + part].astype(F32))
        up_second.append(summed(up, ("sub", "fsdp")))

    up_first = project(hidden_of(0, 0, half) * gate_act[:half].astype(F32))
    for k in range(1, n):
        gate = jnp.concatenate(gates[k])
        up = project(hidden_of(k, 0, half) * gate.astype(F32))
        up_first = up_first + shifted(up, "blk", -k)
    up_first = summed(up_first, ("sub", "fsdp"))
    up_proj = jnp.concatenate([up_first] + up_second)

    left_proj = summed(
        jnp.dot(inputs, proj_in, preferred_element_type=F32), ("sub", "fsdp")
    )
    onehot = (example_of[:, None] == jnp.arange(EX_DEV, dtype=jnp.int32)[None, :]).astype(F32)
    weighted = (onehot[:, :, None] * left_proj[:, None, :]).reshape(tok, EX_DEV * R)
    full_sketch = lax.dot_general(
        weighted, up_proj, (((0,), (0,)), ((), ())), precision=lax.Precision.HIGHEST
    )
    sketch = full_sketch.reshape(EX_DEV, R * R).astype(BF16)
    width = R * R // cores
    sketch_part = lax.dynamic_slice(sketch, (0, core * width), (EX_DEV, width))

    own_q = queries[0].reshape(cores, -1, width)
    got_q = [lax.dynamic_index_in_dim(own_q, core, 0, keepdims=False)]
    for e in range(1, cores):
        got_q.append(
            shifted(lax.dynamic_index_in_dim(own_q, (core + e) % cores, 0, keepdims=False), "sub", e)
        )
    own_q = jnp.concatenate([lax.select_n((core - i) % cores, *got_q) for i in range(cores)], axis=1)
    all_q = gathered(own_q, "blk")
    scores = lax.dot_general(
        sketch, all_q, (((1,), (2,)), ((), ())), preferred_element_type=F32
    )
    return sketch_part, scores


def solution(mesh):
    in_specs = (
        P(("groups", "blk"), "sub"),
        P(("groups", "blk"), ("fsdp", "sub")),
        P(("groups", "blk"), ("fsdp", "sub")),
        P(("fsdp", "sub"), "blk"),
        P(("fsdp", "sub"), None),
        P(("fsdp", "sub"), None),
        P(("groups", "blk"), "fsdp", "sub"),
        P(("groups", "blk")),
    )
    out_specs = (P(("groups", "blk"), "sub"), P(("groups", "blk"), None, ("fsdp", "sub")))
    return jax.shard_map(local, mesh=mesh, in_specs=in_specs, out_specs=out_specs, check_vma=False)
```

time: 1100 us -> 182 us (0.17)
  waiting for transfers between devices: 1040 us -> 40.6 us
  starting transfers between devices: 1.62 us -> 95.1 us
  between operations: 14.5 us -> 1.73 us
    all_gather x2 -> x0, waiting for transfers between devices: 993 us -> none  [the longest x1 977 us: local(): lax.all_gather(w_down, 'blk', axis=1, tiled=True)]
    ppermute x3 -> x37, starting transfers between devices: 1.5 us -> 95.1 us  [the longest x11 42.3 us: shifted(): lax.ppermute(block, axis, [(i, (i + distance) % n) for i in range(n)])]
    psum x1 -> x0, waiting for transfers between devices: 28.5 us -> none  [local(): left_proj, up_proj = lax.psum((part_in, part_out), ('fsdp', 'sub'))]
    ppermute x3 -> x37, waiting for transfers between devices: 15.7 us -> 40.6 us  [the longest x8 15.8 us: line_left(): return lax.ppermute(block, 'blk', [(i + 1, i) for i in range(n - 1)])]
    dot_general x8 -> x11, matrix products: 34 us -> 29.8 us  [the longest x2 23.1 us: local(): lax.dot_general(grads[p].reshape(cores * tok, dblk), w_down, (((1,), (1,)...]
  transfers between devices with their start and end apart: 6 -> 37, of which waited for: 6 -> 13; matrix products, arithmetic and copies ran while one was open for 0% -> 21% of each run, Pallas kernels for 0% -> 0%
where the time goes in v1:
time: 182 us
  starting transfers between devices  95.1 us (52%)
  waiting for transfers between devices  40.6 us (22%)
  matrix products  29.8 us (16%)
  other arithmetic  9.52 us (5%)
  local copies, waits for them, and re-layouts  4.76 us (3%)
    ppermute x11, starting transfers between devices, shifted(): lax.ppermute(block, axis, [(i, (i + distance) % n) for i in range(n)])  42.3 us
    ppermute x8, starting transfers between devices, line_right(): return lax.ppermute(block, 'blk', [(i, i + 1) for i in range(n - 1)])  32 us
    dot_general x2, matrix products, local(): lax.dot_general(grads[p].reshape(cores * tok, dblk), w_down, (((1,), (1,)...  23.1 us
    ppermute x8, waiting for transfers between devices, line_left(): return lax.ppermute(block, 'blk', [(i + 1, i) for i in range(n - 1)])  15.8 us
    ppermute x8, waiting for transfers between devices, line_right(): return lax.ppermute(block, 'blk', [(i, i + 1) for i in range(n - 1)])  10.8 us
    ppermute x8, starting transfers between devices, line_left(): return lax.ppermute(block, 'blk', [(i + 1, i) for i in range(n - 1)])  10.5 us
    ppermute x11, waiting for transfers between devices, shifted(): lax.ppermute(block, axis, [(i, (i + distance) % n) for i in range(n)])  6.43 us
    ppermute x8, starting transfers between devices, summed(): block = block + lax.ppermute(block, axis, [(i, i ^ step) for i in range(n)])  5.49 us
  transfers between devices with their start and end apart: 37, of which 13 were waited for; matrix products, arithmetic and copies ran while one was open for 21% of the time, Pallas kernels for 0%

profile of v1, /device:TPU:0, one launch (start us, length us, event | category | flops | bytes accessed | tf_op | source)
XLA Modules:
  0.0 181.6 jit_solution(4160484604977881672)
XLA Ops:
  0.7 2.5 %fusion.84 = (bf16[128,2048]{1,0:T(8,128)(2,1)}, bf16[128,2048]{1,0:T(8,128)(2,1)}) fusion(bf16[256,4096]{1,0:T(8,128)(2,1)} %param.8, s32[]{:T(128)S(6)} %select_n.482, s32[]{:T(128)S(6)} %select_n.484, s32[]{:T(128)S(6)} %select_n.499), kind=kLoop, calls=%fused_computation.130 | loop fusion | bytes 2097164 | tf_op jit(solution)/shard_map/dynamic_slice | solution.py:64
  3.2 1.8 %collective-permute-start.2 = (bf16[128,2048]{1,0:T(8,128)(2,1)}, bf16[128,2048]{1,0:T(8,128)(2,1)S(1)}, u32[]{:S(2)}, u32[]{:S(2)}) collective-permute-start(bf16[128,2048]{1,0:T(8,128)(2,1)} %get-tuple-element.16), channel_id=1, source_target_pairs={{0,0},{1,8},{4,4},{5,12},{8,1},{9,9},{12,5},{13,13},{2,2},{3,10},{... | collective-permute-start | bytes 1572872 | tf_op jit(solution)/shard_map/ppermute | solution.py:70
  5.0 3.0 %collective-permute-start.5 = (bf16[128,2048]{1,0:T(8,128)(2,1)}, bf16[128,2048]{1,0:T(8,128)(2,1)}, u32[]{:S(2)}, u32[]{:S(2)}) collective-permute-start(bf16[128,2048]{1,0:T(8,128)(2,1)} %get-tuple-element.17), channel_id=1, source_target_pairs={{0,4},{1,12},{4,0},{5,8},{8,5},{9,13},{12,1},{13,9},{2,6},{3,14},{... | collective-permute-start | bytes 1572872 | tf_op jit(solution)/shard_map/ppermute | solution.py:70
  8.0 1.0 fusion.85
  9.0 1.9 %collective-permute-start.12 = (bf16[64,3584]{1,0:T(8,128)(2,1)}, bf16[64,3584]{1,0:T(8,128)(2,1)S(1)}, u32[]{:S(2)}, u32[]{:S(2)}) collective-permute-start(bf16[64,3584]{1,0:T(8,128)(2,1)} %get-tuple-element.21), channel_id=1, source_target_pairs={{0,4},{4,8},{8,12},{1,5},{5,9},{9,13},{2,6},{6,10},{10,14},{3,7},{... | collective-permute-start | bytes 1376264 | tf_op jit(solution)/shard_map/ppermute | solution.py:15
  11.0 2.8 %collective-permute-start.33 = (bf16[4,2048]{1,0:T(4,128)(2,1)S(1)}, bf16[4,2048]{1,0:T(4,128)(2,1)S(1)}, u32[]{:S(2)}, u32[]{:S(2)}) collective-permute-start(bf16[4,2048]{1,0:T(4,128)(2,1)S(1)} %dynamic-slice_bitcast_fusion), channel_id=1, source_target_pairs={{0,1},{1,0},{2,3},{3,2},{4,5},{5,4},{6,7},{7,6},{8,9},{9,8},{10,11... | collective-permute-start | bytes 49160 | tf_op jit(solution)/shard_map/ppermute | solution.py:25
  13.8 1.4 fusion.86
  15.5 5.3 %collective-permute-done.5 = bf16[128,2048]{1,0:T(8,128)(2,1)} collective-permute-done((bf16[128,2048]{1,0:T(8,128)(2,1)}, bf16[128,2048]{1,0:T(8,128)(2,1)}, u32[]{:S(2)}, u32[]{:S(2)}) %collective-permute-start.5) | collective-permute-done | bytes 524320 | tf_op jit(solution)/shard_map/ppermute | solution.py:70
  20.8 2.3 %collective-permute-start.6 = (bf16[128,2048]{1,0:T(8,128)(2,1)}, bf16[128,2048]{1,0:T(8,128)(2,1)S(1)}, u32[]{:S(2)}, u32[]{:S(2)}) collective-permute-start(bf16[128,2048]{1,0:T(8,128)(2,1)} %collective-permute-done.5), channel_id=1, source_target_pairs={{0,2},{2,0},{1,3},{3,1},{4,6},{6,4},{5,7},{7,5},{8,10},{10,8},{9,1... | collective-permute-start | bytes 1572872 | tf_op jit(solution)/shard_map/ppermute | solution.py:25
  23.1 1.0 collective-permute-start.34
  24.2 18.4 %collective-permute-start.35 = (bf16[4,4096]{1,0:T(4,128)(2,1)S(1)}, bf16[4,4096]{1,0:T(4,128)(2,1)S(1)}, u32[]{:S(2)}, u32[]{:S(2)}) collective-permute-start(bf16[4,4096]{1,0:T(4,128)(2,1)S(1)} %pad_maximum_fusion.4), channel_id=1, source_target_pairs={{0,8},{4,12},{8,0},{12,4},{1,9},{5,13},{9,1},{13,5},{2,10},{6,14},... | collective-permute-start | bytes 98312 | tf_op jit(solution)/shard_map/ppermute | solution.py:25
  42.6 2.8 %collective-permute-start.36 = (bf16[4,4096]{1,0:T(4,128)(2,1)S(1)}, bf16[4,4096]{1,0:T(4,128)(2,1)S(1)}, u32[]{:S(2)}, u32[]{:S(2)}) collective-permute-start(bf16[4,4096]{1,0:T(4,128)(2,1)S(1)} %pad_maximum_fusion.4), channel_id=1, source_target_pairs={{0,12},{4,0},{8,4},{12,8},{1,13},{5,1},{9,5},{13,9},{2,14},{6,2},{... | collective-permute-start | bytes 98312 | tf_op jit(solution)/shard_map/ppermute | solution.py:25
  45.4 1.1 select_bitcast_fusion.5
  46.6 1.3 collective-permute-start.13
  48.1 1.5 collective-permute-start.3
  49.8 0.7 select_bitcast_fusion.11
  50.5 4.9 %collective-permute-start.8 = (bf16[64,3584]{1,0:T(8,128)(2,1)S(1)}, bf16[64,3584]{1,0:T(8,128)(2,1)S(1)}, u32[]{:S(2)}, u32[]{:S(2)}) collective-permute-start(bf16[64,3584]{1,0:T(8,128)(2,1)S(1)} %copy-done.13), channel_id=1, source_target_pairs={{0,4},{4,8},{8,12},{1,5},{5,9},{9,13},{2,6},{6,10},{10,14},{3,7},{... | collective-permute-start | bytes 1376264 | tf_op jit(solution)/shard_map/ppermute | solution.py:15
  55.4 0.6 add.210
  56.0 6.4 %collective-permute-done.3 = bf16[128,2048]{1,0:T(8,128)(2,1)S(1)} collective-permute-done((bf16[128,2048]{1,0:T(8,128)(2,1)S(1)}, bf16[128,2048]{1,0:T(8,128)(2,1)S(1)}, u32[]{:S(2)}, u32[]{:S(2)}) %collective-permute-start.3) | collective-permute-done | bytes 524320 | tf_op jit(solution)/shard_map/ppermute | solution.py:25
  62.4 1.3 collective-permute-start.9
  64.0 1.2 select_bitcast_fusion.1
  65.2 11.5 %fusion = f32[2,256,3584]{2,1,0:T(8,128)S(1)} fusion(bf16[3584,2048]{1,0:T(8,128)(2,1)} %param.11, bf16[1,256,2048]{2,1,0:T(8,128)(2,1)} %get-tuple-element.19, bf16[1,256,2048]{2,1,0:T(8,128)(2,1)S(1)} %get-tuple-element.18), kind=kOutput, calls=%fused_computation | convolution fusion | flops 7517241344 | bytes 24117248 | tf_op jit(solution)/shard_map/dot_general | solution.py:78
  77.1 1.6 fusion.46
  78.7 1.3 collective-permute-start.10
  80.0 1.3 collective-permute-start.14
  81.3 6.7 %collective-permute-start.17 = (bf16[64,3584]{1,0:T(8,128)(2,1)}, bf16[64,3584]{1,0:T(8,128)(2,1)S(1)}, u32[]{:S(2)}, u32[]{:S(2)}) collective-permute-start(bf16[64,3584]{1,0:T(8,128)(2,1)} %get-tuple-element.10), channel_id=1, source_target_pairs={{0,4},{4,8},{8,12},{1,5},{5,9},{9,13},{2,6},{6,10},{10,14},{3,7},{... | collective-permute-start | bytes 1376264 | tf_op jit(solution)/shard_map/ppermute | solution.py:15
  88.0 5.6 %collective-permute-start.18 = (bf16[64,3584]{1,0:T(8,128)(2,1)}, bf16[64,3584]{1,0:T(8,128)(2,1)}, u32[]{:S(2)}, u32[]{:S(2)}) collective-permute-start(bf16[64,3584]{1,0:T(8,128)(2,1)} %get-tuple-element.11), channel_id=1, source_target_pairs={{0,4},{4,8},{8,12},{1,5},{5,9},{9,13},{2,6},{6,10},{10,14},{3,7},{... | collective-permute-start | bytes 1376264 | tf_op jit(solution)/shard_map/ppermute | solution.py:15
  93.7 1.5 select_bitcast_fusion.3
  95.2 11.6 %fusion.2 = f32[2,256,3584]{2,1,0:T(8,128)S(1)} fusion(bf16[3584,2048]{1,0:T(8,128)(2,1)} %param.11, bf16[1,256,2048]{2,1,0:T(8,128)(2,1)} %get-tuple-element.15, bf16[1,256,2048]{2,1,0:T(8,128)(2,1)} %get-tuple-element.14), kind=kOutput, calls=%fused_computation.2 | convolution fusion | flops 7517241344 | bytes 24117248 | tf_op jit(solution)/shard_map/dot_general | solution.py:78
  106.9 1.3 collective-permute-done.18
  108.1 1.5 fusion.44
  109.6 1.4 collective-permute-start.15
  111.0 1.3 collective-permute-start.11
  112.5 0.8 fusion.11
  113.3 7.7 %collective-permute-start.19 = (f32[128,64]{0,1:T(8,128)S(1)}, f32[128,64]{0,1:T(8,128)S(1)}, u32[]{:S(2)}, u32[]{:S(2)}) collective-permute-start(f32[128,64]{0,1:T(8,128)S(1)} %fusion.11), channel_id=1, source_target_pairs={{0,8},{4,12},{8,0},{12,4},{1,9},{5,13},{9,1},{13,5},{2,10},{6,14},... | collective-permute-start | bytes 98312 | tf_op jit(solution)/shard_map/ppermute | solution.py:25
  120.9 4.1 %collective-permute-start.21 = (bf16[64,3584]{1,0:T(8,128)(2,1)S(1)}, bf16[64,3584]{1,0:T(8,128)(2,1)S(1)}, u32[]{:S(2)}, u32[]{:S(2)}) collective-permute-start(bf16[64,3584]{1,0:T(8,128)(2,1)S(1)} %get-tuple-element.7), channel_id=1, source_target_pairs={{0,4},{4,8},{8,12},{1,5},{5,9},{9,13},{2,6},{6,10},{10,14},{3,7},{... | collective-permute-start | bytes 1376264 | tf_op jit(solution)/shard_map/ppermute | solution.py:15
  125.1 1.9 %collective-permute-start.20 = (bf16[64,3584]{1,0:T(8,128)(2,1)S(1)}, bf16[64,3584]{1,0:T(8,128)(2,1)S(1)}, u32[]{:S(2)}, u32[]{:S(2)}) collective-permute-start(bf16[64,3584]{1,0:T(8,128)(2,1)S(1)} %get-tuple-element.6), channel_id=1, source_target_pairs={{0,4},{4,8},{8,12},{1,5},{5,9},{9,13},{2,6},{6,10},{10,14},{3,7},{... | collective-permute-start | bytes 1376264 | tf_op jit(solution)/shard_map/ppermute | solution.py:15
  127.1 8.2 %collective-permute-done.11 = bf16[64,3584]{1,0:T(8,128)(2,1)S(1)} collective-permute-done((bf16[64,3584]{1,0:T(8,128)(2,1)S(1)}, bf16[64,3584]{1,0:T(8,128)(2,1)S(1)}, u32[]{:S(2)}, u32[]{:S(2)}) %collective-permute-start.11) | collective-permute-done | bytes 458784 | tf_op jit(solution)/shard_map/ppermute | solution.py:20
  135.4 0.8 fusion.12
  136.1 3.0 %collective-permute-start.16 = (f32[128,64]{0,1:T(8,128)S(1)}, f32[128,64]{0,1:T(8,128)S(1)}, u32[]{:S(2)}, u32[]{:S(2)}) collective-permute-start(f32[128,64]{0,1:T(8,128)S(1)} %fusion.12), channel_id=1, source_target_pairs={{0,12},{4,0},{8,4},{12,8},{1,13},{5,1},{9,5},{13,9},{2,14},{6,2},{... | collective-permute-start | bytes 98312 | tf_op jit(solution)/shard_map/ppermute | solution.py:25
  139.2 5.1 %collective-permute-done.20 = bf16[64,3584]{1,0:T(8,128)(2,1)S(1)} collective-permute-done((bf16[64,3584]{1,0:T(8,128)(2,1)S(1)}, bf16[64,3584]{1,0:T(8,128)(2,1)S(1)}, u32[]{:S(2)}, u32[]{:S(2)}) %collective-permute-start.20) | collective-permute-done | bytes 458784 | tf_op jit(solution)/shard_map/ppermute | solution.py:15
  144.4 0.8 fusion.10
  145.2 2.5 %collective-permute-start.22 = (f32[128,64]{0,1:T(8,128)S(1)}, f32[128,64]{0,1:T(8,128)S(1)}, u32[]{:S(2)}, u32[]{:S(2)}) collective-permute-start(f32[128,64]{0,1:T(8,128)S(1)} %fusion.10), channel_id=1, source_target_pairs={{0,4},{4,8},{8,12},{12,0},{1,5},{5,9},{9,13},{13,1},{2,6},{6,10},{... | collective-permute-start | bytes 98312 | tf_op jit(solution)/shard_map/ppermute | solution.py:25
  147.7 0.5 fusion.38
  148.2 2.2 %collective-permute-start.25 = (bf16[64,3584]{1,0:T(8,128)(2,1)S(1)}, bf16[64,3584]{1,0:T(8,128)(2,1)S(1)}, u32[]{:S(2)}, u32[]{:S(2)}) collective-permute-start(bf16[64,3584]{1,0:T(8,128)(2,1)S(1)} %get-tuple-element.2), channel_id=1, source_target_pairs={{0,4},{4,8},{8,12},{1,5},{5,9},{9,13},{2,6},{6,10},{10,14},{3,7},{... | collective-permute-start | bytes 1376264 | tf_op jit(solution)/shard_map/ppermute | solution.py:15
  150.4 1.3 collective-permute-start.26
  151.7 0.8 fusion.13
  152.5 1.6 collective-permute-start.1
  154.1 4.6 %collective-permute-start.29 = (bf16[64,3584]{1,0:T(8,128)(2,1)S(1)}, bf16[64,3584]{1,0:T(8,128)(2,1)S(1)}, u32[]{:S(2)}, u32[]{:S(2)}) collective-permute-start(bf16[64,3584]{1,0:T(8,128)(2,1)S(1)} %get-tuple-element.3), channel_id=1, source_target_pairs={{0,4},{4,8},{8,12},{1,5},{5,9},{9,13},{2,6},{6,10},{10,14},{3,7},{... | collective-permute-start | bytes 1376264 | tf_op jit(solution)/shard_map/ppermute | solution.py:15
  158.7 1.3 collective-permute-start.30
  160.0 1.3 collective-permute-done.25
  161.3 3.4 %collective-permute-done.26 = bf16[64,3584]{1,0:T(8,128)(2,1)S(1)} collective-permute-done((bf16[64,3584]{1,0:T(8,128)(2,1)S(1)}, bf16[64,3584]{1,0:T(8,128)(2,1)S(1)}, u32[]{:S(2)}, u32[]{:S(2)}) %collective-permute-start.26) | collective-permute-done | bytes 458784 | tf_op jit(solution)/shard_map/ppermute | solution.py:20
  164.7 0.4 fusion.41
  165.2 3.2 %collective-permute-done.29 = bf16[64,3584]{1,0:T(8,128)(2,1)S(1)} collective-permute-done((bf16[64,3584]{1,0:T(8,128)(2,1)S(1)}, bf16[64,3584]{1,0:T(8,128)(2,1)S(1)}, u32[]{:S(2)}, u32[]{:S(2)}) %collective-permute-start.29) | collective-permute-done | bytes 458784 | tf_op jit(solution)/shard_map/ppermute | solution.py:15
  168.4 3.8 %collective-permute-done.30 = bf16[64,3584]{1,0:T(8,128)(2,1)S(1)} collective-permute-done((bf16[64,3584]{1,0:T(8,128)(2,1)S(1)}, bf16[64,3584]{1,0:T(8,128)(2,1)S(1)}, u32[]{:S(2)}, u32[]{:S(2)}) %collective-permute-start.30) | collective-permute-done | bytes 458784 | tf_op jit(solution)/shard_map/ppermute | solution.py:20
  172.2 0.4 fusion.35
  172.9 1.6 collective-permute-start.24
  174.4 0.6 collective-permute-start.28
  175.0 1.6 collective-permute-start.32
  176.9 1.6 collective-permute-done.28
  178.4 0.6 collective-permute-done.32
  179.0 0.6 convolution_convert_fusion
  180.2 0.6 constant_dynamic-slice_fusion
  180.8 0.8 fusion.62
  (111 shorter events, 2.5 us)
Async XLA Ops:
  0.6 13.2 %copy-start = (bf16[256,2048]{1,0:T(8,128)(2,1)S(1)}, bf16[256,2048]{1,0:T(8,128)(2,1)}, u32[]{:S(2)}) copy-start(bf16[256,2048]{1,0:T(8,128)(2,1)} %param.9) | copy-start | bytes 3145732
  0.6 7.4 %copy-start.3 = (bf16[256,3584]{1,0:T(8,128)(2,1)S(1)}, bf16[256,3584]{1,0:T(8,128)(2,1)}, u32[]{:S(2)}) copy-start(bf16[256,3584]{1,0:T(8,128)(2,1)} %param.10) | copy-start | bytes 5505028
  0.7 10.3 %copy-start.24 = (bf16[1,8,2048]{2,1,0:T(8,128)(2,1)S(1)}, bf16[1,8,2048]{2,1,0:T(8,128)(2,1)}, u32[]{:S(2)}) copy-start(bf16[1,8,2048]{2,1,0:T(8,128)(2,1)} %param.14) | copy-start | bytes 98308
  3.2 12.0 %copy-start.25 = (s32[256]{0:T(256)S(1)}, s32[256]{0:T(256)}, u32[]{:S(2)}) copy-start(s32[256]{0:T(256)} %param.15) | copy-start | bytes 3076
  3.2 44.9 %collective-permute-start.2 = (bf16[128,2048]{1,0:T(8,128)(2,1)}, bf16[128,2048]{1,0:T(8,128)(2,1)S(1)}, u32[]{:S(2)}, u32[]{:S(2)}) collective-permute-start(bf16[128,2048]{1,0:T(8,128)(2,1)} %get-tuple-element.16), channel_id=1, source_target_pairs={{0,0},{1,8},{4,4},{5,12},{8,1},{9,9},{12,5},{13,13},{2,2},{3,10},{... | collective-permute-start | bytes 1572872 | tf_op jit(solution)/shard_map/ppermute | solution.py:70
  5.0 15.8 %collective-permute-start.5 = (bf16[128,2048]{1,0:T(8,128)(2,1)}, bf16[128,2048]{1,0:T(8,128)(2,1)}, u32[]{:S(2)}, u32[]{:S(2)}) collective-permute-start(bf16[128,2048]{1,0:T(8,128)(2,1)} %get-tuple-element.17), channel_id=1, source_target_pairs={{0,4},{1,12},{4,0},{5,8},{8,5},{9,13},{12,1},{13,9},{2,6},{3,14},{... | collective-permute-start | bytes 1572872 | tf_op jit(solution)/shard_map/ppermute | solution.py:70
  9.0 67.6 %collective-permute-start.12 = (bf16[64,3584]{1,0:T(8,128)(2,1)}, bf16[64,3584]{1,0:T(8,128)(2,1)S(1)}, u32[]{:S(2)}, u32[]{:S(2)}) collective-permute-start(bf16[64,3584]{1,0:T(8,128)(2,1)} %get-tuple-element.21), channel_id=1, source_target_pairs={{0,4},{4,8},{8,12},{1,5},{5,9},{9,13},{2,6},{6,10},{10,14},{3,7},{... | collective-permute-start | bytes 1376264 | tf_op jit(solution)/shard_map/ppermute | solution.py:15
  11.0 12.0 %collective-permute-start.33 = (bf16[4,2048]{1,0:T(4,128)(2,1)S(1)}, bf16[4,2048]{1,0:T(4,128)(2,1)S(1)}, u32[]{:S(2)}, u32[]{:S(2)}) collective-permute-start(bf16[4,2048]{1,0:T(4,128)(2,1)S(1)} %dynamic-slice_bitcast_fusion), channel_id=1, source_target_pairs={{0,1},{1,0},{2,3},{3,2},{4,5},{5,4},{6,7},{7,6},{8,9},{9,8},{10,11... | collective-permute-start | bytes 49160 | tf_op jit(solution)/shard_map/ppermute | solution.py:25
  20.8 21.7 %collective-permute-start.6 = (bf16[128,2048]{1,0:T(8,128)(2,1)}, bf16[128,2048]{1,0:T(8,128)(2,1)S(1)}, u32[]{:S(2)}, u32[]{:S(2)}) collective-permute-start(bf16[128,2048]{1,0:T(8,128)(2,1)} %collective-permute-done.5), channel_id=1, source_target_pairs={{0,2},{2,0},{1,3},{3,1},{4,6},{6,4},{5,7},{7,5},{8,10},{10,8},{9,1... | collective-permute-start | bytes 1572872 | tf_op jit(solution)/shard_map/ppermute | solution.py:25
  23.1 27.4 %copy-start.13 = (bf16[64,3584]{1,0:T(8,128)(2,1)S(1)}, bf16[64,3584]{1,0:T(8,128)(2,1)}, u32[]{:S(2)}) copy-start(bf16[64,3584]{1,0:T(8,128)(2,1)} %get-tuple-element.20) | copy-start | bytes 1376260
  23.1 23.5 %collective-permute-start.34 = (bf16[4,4096]{1,0:T(4,128)(2,1)S(1)}, bf16[4,4096]{1,0:T(4,128)(2,1)S(1)}, u32[]{:S(2)}, u32[]{:S(2)}) collective-permute-start(bf16[4,4096]{1,0:T(4,128)(2,1)S(1)} %pad_maximum_fusion.4), channel_id=1, source_target_pairs={{0,4},{4,8},{8,12},{12,0},{1,5},{5,9},{9,13},{13,1},{2,6},{6,10},{... | collective-permute-start | bytes 98312 | tf_op jit(solution)/shard_map/ppermute | solution.py:25
  24.2 23.8 %collective-permute-start.35 = (bf16[4,4096]{1,0:T(4,128)(2,1)S(1)}, bf16[4,4096]{1,0:T(4,128)(2,1)S(1)}, u32[]{:S(2)}, u32[]{:S(2)}) collective-permute-start(bf16[4,4096]{1,0:T(4,128)(2,1)S(1)} %pad_maximum_fusion.4), channel_id=1, source_target_pairs={{0,8},{4,12},{8,0},{12,4},{1,9},{5,13},{9,1},{13,5},{2,10},{6,14},... | collective-permute-start | bytes 98312 | tf_op jit(solution)/shard_map/ppermute | solution.py:25
  42.6 7.0 %collective-permute-start.36 = (bf16[4,4096]{1,0:T(4,128)(2,1)S(1)}, bf16[4,4096]{1,0:T(4,128)(2,1)S(1)}, u32[]{:S(2)}, u32[]{:S(2)}) collective-permute-start(bf16[4,4096]{1,0:T(4,128)(2,1)S(1)} %pad_maximum_fusion.4), channel_id=1, source_target_pairs={{0,12},{4,0},{8,4},{12,8},{1,13},{5,1},{9,5},{13,9},{2,14},{6,2},{... | collective-permute-start | bytes 98312 | tf_op jit(solution)/shard_map/ppermute | solution.py:25
  46.6 17.2 %copy-start.15 = (bf16[4,4096]{1,0:T(4,128)(2,1)}, bf16[4,4096]{1,0:T(4,128)(2,1)S(1)}, u32[]{:S(2)}) copy-start(bf16[4,4096]{1,0:T(4,128)(2,1)S(1)} %collective-permute-done.34) | copy-start | bytes 98308
  46.6 30.1 %collective-permute-start.13 = (bf16[64,3584]{1,0:T(8,128)(2,1)}, bf16[64,3584]{1,0:T(8,128)(2,1)S(1)}, u32[]{:S(2)}, u32[]{:S(2)}) collective-permute-start(bf16[64,3584]{1,0:T(8,128)(2,1)} %get-tuple-element.21), channel_id=1, source_target_pairs={{4,0},{8,4},{12,8},{5,1},{9,5},{13,9},{6,2},{10,6},{14,10},{7,3},{... | collective-permute-start | bytes 1376264 | tf_op jit(solution)/shard_map/ppermute | solution.py:20
  48.0 15.9 %copy-start.17 = (bf16[4,4096]{1,0:T(4,128)(2,1)}, bf16[4,4096]{1,0:T(4,128)(2,1)S(1)}, u32[]{:S(2)}) copy-start(bf16[4,4096]{1,0:T(4,128)(2,1)S(1)} %collective-permute-done.35) | copy-start | bytes 98308
  48.0 2.5 %collective-permute-start = (f32[256,64]{0,1:T(8,128)S(1)}, f32[256,64]{0,1:T(8,128)S(1)}, u32[]{:S(2)}, u32[]{:S(2)}) collective-permute-start(f32[256,64]{0,1:T(8,128)S(1)} %fusion.86), channel_id=1, source_target_pairs={{0,1},{1,0},{2,3},{3,2},{4,5},{5,4},{6,7},{7,6},{8,9},{9,8},{10,11... | collective-permute-start | bytes 196616 | tf_op jit(solution)/shard_map/ppermute | solution.py:42
  48.1 14.3 %collective-permute-start.3 = (bf16[128,2048]{1,0:T(8,128)(2,1)S(1)}, bf16[128,2048]{1,0:T(8,128)(2,1)S(1)}, u32[]{:S(2)}, u32[]{:S(2)}) collective-permute-start(bf16[128,2048]{1,0:T(8,128)(2,1)S(1)} %collective-permute-done.2), channel_id=1, source_target_pairs={{0,2},{2,0},{1,3},{3,1},{4,6},{6,4},{5,7},{7,5},{8,10},{10,8},{9,1... | collective-permute-start | bytes 1572872 | tf_op jit(solution)/shard_map/ppermute | solution.py:25
  49.6 14.3 %copy-start.19 = (bf16[4,4096]{1,0:T(4,128)(2,1)}, bf16[4,4096]{1,0:T(4,128)(2,1)S(1)}, u32[]{:S(2)}) copy-start(bf16[4,4096]{1,0:T(4,128)(2,1)S(1)} %collective-permute-done.36) | copy-start | bytes 98308
  49.6 14.3 %collective-permute-start.7 = (bf16[256,2048]{1,0:T(8,128)(2,1)S(1)}, bf16[256,2048]{1,0:T(8,128)(2,1)S(1)}, u32[]{:S(2)}, u32[]{:S(2)}) collective-permute-start(bf16[256,2048]{1,0:T(8,128)(2,1)S(1)} %bitcast.125), channel_id=1, source_target_pairs={{0,1},{1,0},{2,3},{3,2},{4,5},{5,4},{6,7},{7,6},{8,9},{9,8},{10,11... | collective-permute-start | bytes 3145736 | tf_op jit(solution)/shard_map/ppermute | solution.py:25
  50.5 26.3 %collective-permute-start.8 = (bf16[64,3584]{1,0:T(8,128)(2,1)S(1)}, bf16[64,3584]{1,0:T(8,128)(2,1)S(1)}, u32[]{:S(2)}, u32[]{:S(2)}) collective-permute-start(bf16[64,3584]{1,0:T(8,128)(2,1)S(1)} %copy-done.13), channel_id=1, source_target_pairs={{0,4},{4,8},{8,12},{1,5},{5,9},{9,13},{2,6},{6,10},{10,14},{3,7},{... | collective-permute-start | bytes 1376264 | tf_op jit(solution)/shard_map/ppermute | solution.py:15
  62.4 14.7 %collective-permute-start.9 = (bf16[64,3584]{1,0:T(8,128)(2,1)S(1)}, bf16[64,3584]{1,0:T(8,128)(2,1)S(1)}, u32[]{:S(2)}, u32[]{:S(2)}) collective-permute-start(bf16[64,3584]{1,0:T(8,128)(2,1)S(1)} %copy-done.13), channel_id=1, source_target_pairs={{4,0},{8,4},{12,8},{5,1},{9,5},{13,9},{6,2},{10,6},{14,10},{7,3},{... | collective-permute-start | bytes 1376264 | tf_op jit(solution)/shard_map/ppermute | solution.py:20
  63.9 29.8 %collective-permute-start.4 = (bf16[256,2048]{1,0:T(8,128)(2,1)S(1)}, bf16[256,2048]{1,0:T(8,128)(2,1)S(1)}, u32[]{:S(2)}, u32[]{:S(2)}) collective-permute-start(bf16[256,2048]{1,0:T(8,128)(2,1)S(1)} %bitcast.126), channel_id=1, source_target_pairs={{0,1},{1,0},{2,3},{3,2},{4,5},{5,4},{6,7},{7,6},{8,9},{9,8},{10,11... | collective-permute-start | bytes 3145736 | tf_op jit(solution)/shard_map/ppermute | solution.py:25
  76.7 2.0 %copy-start.5 = (bf16[64,3584]{1,0:T(8,128)(2,1)}, bf16[64,3584]{1,0:T(8,128)(2,1)S(1)}, u32[]{:S(2)}) copy-start(bf16[64,3584]{1,0:T(8,128)(2,1)S(1)} %collective-permute-done.12) | copy-start | bytes 1376260
  76.7 1.9 %copy-start.7 = (bf16[64,3584]{1,0:T(8,128)(2,1)}, bf16[64,3584]{1,0:T(8,128)(2,1)S(1)}, u32[]{:S(2)}) copy-start(bf16[64,3584]{1,0:T(8,128)(2,1)S(1)} %collective-permute-done.13) | copy-start | bytes 1376260
  76.7 1.9 %copy-start.11 = (bf16[64,3584]{1,0:T(8,128)(2,1)}, bf16[64,3584]{1,0:T(8,128)(2,1)S(1)}, u32[]{:S(2)}) copy-start(bf16[64,3584]{1,0:T(8,128)(2,1)S(1)} %collective-permute-done.8) | copy-start | bytes 1376260
  77.1 1.6 copy-start.9
  78.7 28.1 %collective-permute-start.10 = (bf16[64,3584]{1,0:T(8,128)(2,1)}, bf16[64,3584]{1,0:T(8,128)(2,1)S(1)}, u32[]{:S(2)}, u32[]{:S(2)}) collective-permute-start(bf16[64,3584]{1,0:T(8,128)(2,1)} %get-tuple-element.13), channel_id=1, source_target_pairs={{4,0},{8,4},{12,8},{5,1},{9,5},{13,9},{6,2},{10,6},{14,10},{7,3},{... | collective-permute-start | bytes 1376264 | tf_op jit(solution)/shard_map/ppermute | solution.py:20
  80.0 26.9 %collective-permute-start.14 = (bf16[64,3584]{1,0:T(8,128)(2,1)}, bf16[64,3584]{1,0:T(8,128)(2,1)S(1)}, u32[]{:S(2)}, u32[]{:S(2)}) collective-permute-start(bf16[64,3584]{1,0:T(8,128)(2,1)} %get-tuple-element.12), channel_id=1, source_target_pairs={{4,0},{8,4},{12,8},{5,1},{9,5},{13,9},{6,2},{10,6},{14,10},{7,3},{... | collective-permute-start | bytes 1376264 | tf_op jit(solution)/shard_map/ppermute | solution.py:20
  81.3 25.6 %collective-permute-start.17 = (bf16[64,3584]{1,0:T(8,128)(2,1)}, bf16[64,3584]{1,0:T(8,128)(2,1)S(1)}, u32[]{:S(2)}, u32[]{:S(2)}) collective-permute-start(bf16[64,3584]{1,0:T(8,128)(2,1)} %get-tuple-element.10), channel_id=1, source_target_pairs={{0,4},{4,8},{8,12},{1,5},{5,9},{9,13},{2,6},{6,10},{10,14},{3,7},{... | collective-permute-start | bytes 1376264 | tf_op jit(solution)/shard_map/ppermute | solution.py:15
  88.0 20.1 %collective-permute-start.18 = (bf16[64,3584]{1,0:T(8,128)(2,1)}, bf16[64,3584]{1,0:T(8,128)(2,1)}, u32[]{:S(2)}, u32[]{:S(2)}) collective-permute-start(bf16[64,3584]{1,0:T(8,128)(2,1)} %get-tuple-element.11), channel_id=1, source_target_pairs={{0,4},{4,8},{8,12},{1,5},{5,9},{9,13},{2,6},{6,10},{10,14},{3,7},{... | collective-permute-start | bytes 1376264 | tf_op jit(solution)/shard_map/ppermute | solution.py:15
  109.6 2.9 %copy-start.2 = (bf16[3584,64]{0,1:T(8,128)(2,1)S(1)}, bf16[3584,64]{0,1:T(8,128)(2,1)}, u32[]{:S(2)}) copy-start(bf16[3584,64]{0,1:T(8,128)(2,1)} %param.13) | copy-start | bytes 1376260
  109.6 17.4 %collective-permute-start.15 = (bf16[64,3584]{1,0:T(8,128)(2,1)S(1)}, bf16[64,3584]{1,0:T(8,128)(2,1)S(1)}, u32[]{:S(2)}, u32[]{:S(2)}) collective-permute-start(bf16[64,3584]{1,0:T(8,128)(2,1)S(1)} %get-tuple-element.8), channel_id=1, source_target_pairs={{4,0},{8,4},{12,8},{5,1},{9,5},{13,9},{6,2},{10,6},{14,10},{7,3},{... | collective-permute-start | bytes 1376264 | tf_op jit(solution)/shard_map/ppermute | solution.py:20
  111.0 24.3 %collective-permute-start.11 = (bf16[64,3584]{1,0:T(8,128)(2,1)S(1)}, bf16[64,3584]{1,0:T(8,128)(2,1)S(1)}, u32[]{:S(2)}, u32[]{:S(2)}) collective-permute-start(bf16[64,3584]{1,0:T(8,128)(2,1)S(1)} %get-tuple-element.9), channel_id=1, source_target_pairs={{4,0},{8,4},{12,8},{5,1},{9,5},{13,9},{6,2},{10,6},{14,10},{7,3},{... | collective-permute-start | bytes 1376264 | tf_op jit(solution)/shard_map/ppermute | solution.py:20
  112.4 14.6 %copy-start.6 = (bf16[64,3584]{1,0:T(8,128)(2,1)S(1)}, bf16[64,3584]{1,0:T(8,128)(2,1)}, u32[]{:S(2)}) copy-start(bf16[64,3584]{1,0:T(8,128)(2,1)} %copy-done.5) | copy-start | bytes 1376260
  112.5 22.8 %copy-start.12 = (bf16[64,3584]{1,0:T(8,128)(2,1)S(1)}, bf16[64,3584]{1,0:T(8,128)(2,1)}, u32[]{:S(2)}) copy-start(bf16[64,3584]{1,0:T(8,128)(2,1)} %copy-done.11) | copy-start | bytes 1376260
  113.3 39.2 %collective-permute-start.19 = (f32[128,64]{0,1:T(8,128)S(1)}, f32[128,64]{0,1:T(8,128)S(1)}, u32[]{:S(2)}, u32[]{:S(2)}) collective-permute-start(f32[128,64]{0,1:T(8,128)S(1)} %fusion.11), channel_id=1, source_target_pairs={{0,8},{4,12},{8,0},{12,4},{1,9},{5,13},{9,1},{13,5},{2,10},{6,14},... | collective-permute-start | bytes 98312 | tf_op jit(solution)/shard_map/ppermute | solution.py:25
  120.9 18.2 %collective-permute-start.21 = (bf16[64,3584]{1,0:T(8,128)(2,1)S(1)}, bf16[64,3584]{1,0:T(8,128)(2,1)S(1)}, u32[]{:S(2)}, u32[]{:S(2)}) collective-permute-start(bf16[64,3584]{1,0:T(8,128)(2,1)S(1)} %get-tuple-element.7), channel_id=1, source_target_pairs={{0,4},{4,8},{8,12},{1,5},{5,9},{9,13},{2,6},{6,10},{10,14},{3,7},{... | collective-permute-start | bytes 1376264 | tf_op jit(solution)/shard_map/ppermute | solution.py:15
  125.1 19.2 %collective-permute-start.20 = (bf16[64,3584]{1,0:T(8,128)(2,1)S(1)}, bf16[64,3584]{1,0:T(8,128)(2,1)S(1)}, u32[]{:S(2)}, u32[]{:S(2)}) collective-permute-start(bf16[64,3584]{1,0:T(8,128)(2,1)S(1)} %get-tuple-element.6), channel_id=1, source_target_pairs={{0,4},{4,8},{8,12},{1,5},{5,9},{9,13},{2,6},{6,10},{10,14},{3,7},{... | collective-permute-start | bytes 1376264 | tf_op jit(solution)/shard_map/ppermute | solution.py:15
  127.1 12.1 %copy-start.8 = (bf16[64,3584]{1,0:T(8,128)(2,1)S(1)}, bf16[64,3584]{1,0:T(8,128)(2,1)}, u32[]{:S(2)}) copy-start(bf16[64,3584]{1,0:T(8,128)(2,1)} %copy-done.7) | copy-start | bytes 1376260
  135.3 9.0 %copy-start.10 = (bf16[64,3584]{1,0:T(8,128)(2,1)S(1)}, bf16[64,3584]{1,0:T(8,128)(2,1)}, u32[]{:S(2)}) copy-start(bf16[64,3584]{1,0:T(8,128)(2,1)} %copy-done.9) | copy-start | bytes 1376260
  136.1 18.0 %collective-permute-start.16 = (f32[128,64]{0,1:T(8,128)S(1)}, f32[128,64]{0,1:T(8,128)S(1)}, u32[]{:S(2)}, u32[]{:S(2)}) collective-permute-start(f32[128,64]{0,1:T(8,128)S(1)} %fusion.12), channel_id=1, source_target_pairs={{0,12},{4,0},{8,4},{12,8},{1,13},{5,1},{9,5},{13,9},{2,14},{6,2},{... | collective-permute-start | bytes 98312 | tf_op jit(solution)/shard_map/ppermute | solution.py:25
  145.2 6.6 %copy-start.4 = (bf16[256,3584]{1,0:T(8,128)(2,1)S(1)}, bf16[256,3584]{1,0:T(8,128)(2,1)}, u32[]{:S(2)}) copy-start(bf16[256,3584]{1,0:T(8,128)(2,1)} %param.10) | copy-start | bytes 5505028
  145.2 13.5 %collective-permute-start.22 = (f32[128,64]{0,1:T(8,128)S(1)}, f32[128,64]{0,1:T(8,128)S(1)}, u32[]{:S(2)}, u32[]{:S(2)}) collective-permute-start(f32[128,64]{0,1:T(8,128)S(1)} %fusion.10), channel_id=1, source_target_pairs={{0,4},{4,8},{8,12},{12,0},{1,5},{5,9},{9,13},{13,1},{2,6},{6,10},{... | collective-permute-start | bytes 98312 | tf_op jit(solution)/shard_map/ppermute | solution.py:25
  148.2 4.3 %copy-start.14 = (f32[256,64]{0,1:T(8,128)S(1)}, f32[256,64]{0,1:T(8,128)}, u32[]{:S(2)}) copy-start(f32[256,64]{0,1:T(8,128)} %add.210) | copy-start | bytes 196612
  148.2 13.1 %collective-permute-start.25 = (bf16[64,3584]{1,0:T(8,128)(2,1)S(1)}, bf16[64,3584]{1,0:T(8,128)(2,1)S(1)}, u32[]{:S(2)}, u32[]{:S(2)}) collective-permute-start(bf16[64,3584]{1,0:T(8,128)(2,1)S(1)} %get-tuple-element.2), channel_id=1, source_target_pairs={{0,4},{4,8},{8,12},{1,5},{5,9},{9,13},{2,6},{6,10},{10,14},{3,7},{... | collective-permute-start | bytes 1376264 | tf_op jit(solution)/shard_map/ppermute | solution.py:15
  150.4 14.3 %collective-permute-start.26 = (bf16[64,3584]{1,0:T(8,128)(2,1)S(1)}, bf16[64,3584]{1,0:T(8,128)(2,1)S(1)}, u32[]{:S(2)}, u32[]{:S(2)}) collective-permute-start(bf16[64,3584]{1,0:T(8,128)(2,1)S(1)} %get-tuple-element.4), channel_id=1, source_target_pairs={{4,0},{8,4},{12,8},{5,1},{9,5},{13,9},{6,2},{10,6},{14,10},{7,3},{... | collective-permute-start | bytes 1376264 | tf_op jit(solution)/shard_map/ppermute | solution.py:20
  152.5 20.3 %collective-permute-start.1 = (f32[256,64]{0,1:T(8,128)S(1)}, f32[256,64]{0,1:T(8,128)S(1)}, u32[]{:S(2)}, u32[]{:S(2)}) collective-permute-start(f32[256,64]{0,1:T(8,128)S(1)} %copy-done.14), channel_id=1, source_target_pairs={{0,2},{2,0},{1,3},{3,1},{4,6},{6,4},{5,7},{7,5},{8,10},{10,8},{9,1... | collective-permute-start | bytes 196616 | tf_op jit(solution)/shard_map/ppermute | solution.py:42
  154.1 14.3 %collective-permute-start.29 = (bf16[64,3584]{1,0:T(8,128)(2,1)S(1)}, bf16[64,3584]{1,0:T(8,128)(2,1)S(1)}, u32[]{:S(2)}, u32[]{:S(2)}) collective-permute-start(bf16[64,3584]{1,0:T(8,128)(2,1)S(1)} %get-tuple-element.3), channel_id=1, source_target_pairs={{0,4},{4,8},{8,12},{1,5},{5,9},{9,13},{2,6},{6,10},{10,14},{3,7},{... | collective-permute-start | bytes 1376264 | tf_op jit(solution)/shard_map/ppermute | solution.py:15
  158.7 13.5 %collective-permute-start.30 = (bf16[64,3584]{1,0:T(8,128)(2,1)S(1)}, bf16[64,3584]{1,0:T(8,128)(2,1)S(1)}, u32[]{:S(2)}, u32[]{:S(2)}) collective-permute-start(bf16[64,3584]{1,0:T(8,128)(2,1)S(1)} %get-tuple-element.5), channel_id=1, source_target_pairs={{4,0},{8,4},{12,8},{5,1},{9,5},{13,9},{6,2},{10,6},{14,10},{7,3},{... | collective-permute-start | bytes 1376264 | tf_op jit(solution)/shard_map/ppermute | solution.py:20
  160.0 12.7 %copy-start.16 = (bf16[4,4096]{1,0:T(4,128)(2,1)S(1)}, bf16[4,4096]{1,0:T(4,128)(2,1)}, u32[]{:S(2)}) copy-start(bf16[4,4096]{1,0:T(4,128)(2,1)} %copy-done.15) | copy-start | bytes 98308
  160.0 12.7 %copy-start.18 = (bf16[4,4096]{1,0:T(4,128)(2,1)S(1)}, bf16[4,4096]{1,0:T(4,128)(2,1)}, u32[]{:S(2)}) copy-start(bf16[4,4096]{1,0:T(4,128)(2,1)} %copy-done.17) | copy-start | bytes 98308
  160.0 12.7 %copy-start.20 = (bf16[4,4096]{1,0:T(4,128)(2,1)S(1)}, bf16[4,4096]{1,0:T(4,128)(2,1)}, u32[]{:S(2)}) copy-start(bf16[4,4096]{1,0:T(4,128)(2,1)} %copy-done.19) | copy-start | bytes 98308
  161.3 11.6 %collective-permute-start.23 = (f32[128,64]{0,1:T(8,128)S(1)}, f32[128,64]{0,1:T(8,128)S(1)}, u32[]{:S(2)}, u32[]{:S(2)}) collective-permute-start(f32[128,64]{0,1:T(8,128)S(1)} %add_add_fusion), channel_id=1, source_target_pairs={{0,1},{1,0},{2,3},{3,2},{4,5},{5,4},{6,7},{7,6},{8,9},{9,8},{10,11... | collective-permute-start | bytes 98312 | tf_op jit(solution)/shard_map/ppermute | solution.py:42
  165.1 9.3 %collective-permute-start.27 = (f32[64,64]{0,1:T(8,128)S(1)}, f32[64,64]{0,1:T(8,128)S(1)}, u32[]{:S(2)}, u32[]{:S(2)}) collective-permute-start(f32[64,64]{0,1:T(8,128)S(1)} %fusion.41), channel_id=1, source_target_pairs={{0,1},{1,0},{2,3},{3,2},{4,5},{5,4},{6,7},{7,6},{8,9},{9,8},{10,11... | collective-permute-start | bytes 49160 | tf_op jit(solution)/shard_map/ppermute | solution.py:42
  172.2 9.5 %copy-start.1 = (bf16[256,2048]{1,0:T(8,128)(2,1)S(1)}, bf16[256,2048]{1,0:T(8,128)(2,1)}, u32[]{:S(2)}) copy-start(bf16[256,2048]{1,0:T(8,128)(2,1)} %param.9) | copy-start | bytes 3145732
  172.6 8.2 %copy-start.21 = (bf16[1,4,4096]{2,1,0:T(4,128)(2,1)S(1)}, bf16[1,4,4096]{2,1,0:T(4,128)(2,1)}, u32[]{:S(2)}) copy-start(bf16[1,4,4096]{2,1,0:T(4,128)(2,1)} %get-tuple-element.26) | copy-start | bytes 98308
  172.6 8.2 %copy-start.22 = (bf16[1,4,4096]{2,1,0:T(4,128)(2,1)S(1)}, bf16[1,4,4096]{2,1,0:T(4,128)(2,1)}, u32[]{:S(2)}) copy-start(bf16[1,4,4096]{2,1,0:T(4,128)(2,1)} %get-tuple-element.27) | copy-start | bytes 98308
  172.6 8.2 %copy-start.23 = (bf16[1,4,4096]{2,1,0:T(4,128)(2,1)S(1)}, bf16[1,4,4096]{2,1,0:T(4,128)(2,1)}, u32[]{:S(2)}) copy-start(bf16[1,4,4096]{2,1,0:T(4,128)(2,1)} %get-tuple-element.28) | copy-start | bytes 98308
  172.7 2.4 %collective-permute-start.31 = (f32[64,64]{0,1:T(8,128)S(1)}, f32[64,64]{0,1:T(8,128)S(1)}, u32[]{:S(2)}, u32[]{:S(2)}) collective-permute-start(f32[64,64]{0,1:T(8,128)S(1)} %fusion.35), channel_id=1, source_target_pairs={{0,1},{1,0},{2,3},{3,2},{4,5},{5,4},{6,7},{7,6},{8,9},{9,8},{10,11... | collective-permute-start | bytes 49160 | tf_op jit(solution)/shard_map/ppermute | solution.py:42
  172.9 4.0 %collective-permute-start.24 = (f32[128,64]{0,1:T(8,128)S(1)}, f32[128,64]{0,1:T(8,128)S(1)}, u32[]{:S(2)}, u32[]{:S(2)}) collective-permute-start(f32[128,64]{0,1:T(8,128)S(1)} %add.242), channel_id=1, source_target_pairs={{0,2},{2,0},{1,3},{3,1},{4,6},{6,4},{5,7},{7,5},{8,10},{10,8},{9,1... | collective-permute-start | bytes 98312 | tf_op jit(solution)/shard_map/ppermute | solution.py:42
  174.4 4.0 %collective-permute-start.28 = (f32[64,64]{0,1:T(8,128)S(1)}, f32[64,64]{0,1:T(8,128)S(1)}, u32[]{:S(2)}, u32[]{:S(2)}) collective-permute-start(f32[64,64]{0,1:T(8,128)S(1)} %add.249), channel_id=1, source_target_pairs={{0,2},{2,0},{1,3},{3,1},{4,6},{6,4},{5,7},{7,5},{8,10},{10,8},{9,1... | collective-permute-start | bytes 49160 | tf_op jit(solution)/shard_map/ppermute | solution.py:42
  175.0 4.0 %collective-permute-start.32 = (f32[64,64]{0,1:T(8,128)S(1)}, f32[64,64]{0,1:T(8,128)S(1)}, u32[]{:S(2)}, u32[]{:S(2)}) collective-permute-start(f32[64,64]{0,1:T(8,128)S(1)} %add.255), channel_id=1, source_target_pairs={{0,2},{2,0},{1,3},{3,1},{4,6},{6,4},{5,7},{7,5},{8,10},{10,8},{9,1... | collective-permute-start | bytes 49160 | tf_op jit(solution)/shard_map/ppermute | solution.py:42

commit v2 on v1

v2 whole, which is shorter than its diff:
```python
import jax
import jax.numpy as jnp
from jax import lax
from jax.experimental import pallas as pl
from jax.experimental.pallas import tpu as pltpu
from jax.sharding import PartitionSpec as P

R = 64
EX_DEV = 8
LANES = 128
CHUNKS = 2
FIRST_LIMIT = 56
PAYLOAD_LIMIT = 12
F32 = jnp.float32
BF16 = jnp.bfloat16
ROWS_ROWS = (((1,), (1,)), ((), ()))
ANYWHERE = pl.BlockSpec(memory_space=pl.ANY)


def line_right(block):
    n = lax.axis_size("blk")
    return lax.ppermute(block, "blk", [(i, i + 1) for i in range(n - 1)])


def line_left(block):
    n = lax.axis_size("blk")
    return lax.ppermute(block, "blk", [(i + 1, i) for i in range(n - 1)])


def onward(block, reverse):
    n, n_f = lax.axis_size("blk"), lax.axis_size("fsdp")
    route = []
    for z in range(n):
        for x in range(n_f):
            to = z + (1 if (x % 2 == 0) != reverse else -1)
            route.append((z * n_f + x, to * n_f + x if 0 <= to < n else z * n_f + (x ^ 1)))
    return lax.ppermute(block, ("blk", "fsdp"), route)


def shifted(block, axis, distance):
    n = lax.axis_size(axis)
    return lax.ppermute(block, axis, [(i, (i + distance) % n) for i in range(n)])


def gathered(block, axis):
    n = lax.axis_size(axis)
    if n == 1:
        return block[None]
    here = lax.axis_index(axis)
    got = [block] + [shifted(block, axis, e) for e in range(1, n)]
    return jnp.stack([lax.select_n((here - i) % n, *got) for i in range(n)])


def summed(block, axes):
    for axis in axes:
        n = lax.axis_size(axis)
        step = 1
        while step < n:
            block = block + lax.ppermute(block, axis, [(i, i ^ step) for i in range(n)])
            step *= 2
    return block


def block_of(size, most):
    return max(b for b in range(LANES, most + 1, LANES) if size % b == 0)


def split(block):
    high = block.astype(BF16)
    return high, (block - high.astype(F32)).astype(BF16)


SHORT = pl.CostEstimate(flops=1000, bytes_accessed=1000, transcendentals=0)


def cost(microseconds):
    return pl.CostEstimate(
        flops=1000, bytes_accessed=3_690_000 * microseconds, transcendentals=0
    )


def stack_kernel(*refs):
    out_ref = refs[-1]
    for i, ref in enumerate(refs[:-2]):
        out_ref[i] = ref[...]


def hidden_grad(blocks, w_down, start, rows, after):
    depth = blocks[0].shape[1]
    stacked = pl.pallas_call(
        stack_kernel,
        grid=(1,),
        in_specs=[pl.BlockSpec((rows, depth), lambda i: (start // rows, 0))] * len(blocks)
        + [ANYWHERE],
        out_specs=pl.BlockSpec((len(blocks), rows, depth), lambda i: (0, 0, 0)),
        out_shape=jax.ShapeDtypeStruct((len(blocks), rows, depth), BF16),
        compiler_params=pltpu.CompilerParams(vmem_limit_bytes=16 << 20),
        cost_estimate=cost(1),
        name="stack",
    )(*blocks, after)
    out = lax.dot_general(
        stacked.reshape(-1, depth), w_down, ROWS_ROWS, preferred_element_type=F32
    )
    return out.reshape(len(blocks), rows, -1)


def join_kernel(n, s_ref, *refs):
    blocks, out_ref = refs[:n], refs[-1]
    rows = blocks[0].shape[0]
    for e, block in enumerate(blocks):
        start = pl.multiple_of(lax.rem(s_ref[0] + n - e, n) * rows, rows)
        out_ref[pl.ds(start, rows), :] = block[...]


def join(blocks, here, after):
    n = len(blocks)
    rows, depth = blocks[0].shape
    whole = pl.BlockSpec((rows, depth), lambda i, s: (0, 0))

    def kernel(*refs):
        join_kernel(n, *refs)

    return pl.pallas_call(
        kernel,
        grid_spec=pltpu.PrefetchScalarGridSpec(
            num_scalar_prefetch=1,
            grid=(1,),
            in_specs=[whole] * n + [ANYWHERE] * len(after),
            out_specs=pl.BlockSpec((n * rows, depth), lambda i, s: (0, 0)),
        ),
        out_shape=jax.ShapeDtypeStruct((n * rows, depth), BF16),
        compiler_params=pltpu.CompilerParams(vmem_limit_bytes=12 << 20),
        cost_estimate=SHORT,
        name="join",
    )(here.reshape(1), *blocks, *after)


def copy_kernel(s_ref, block_ref, after_ref, out_ref):
    del s_ref, after_ref
    out_ref[...] = block_ref[...]


def block_copy(array, row, column, shape, after):
    grid_spec = pltpu.PrefetchScalarGridSpec(
        num_scalar_prefetch=1,
        grid=(1,),
        in_specs=[pl.BlockSpec(shape, lambda i, s: (s[0], s[1])), ANYWHERE],
        out_specs=pl.BlockSpec(shape, lambda i, s: (0, 0)),
    )
    return pl.pallas_call(
        copy_kernel,
        grid_spec=grid_spec,
        out_shape=jax.ShapeDtypeStruct(shape, array.dtype),
        compiler_params=pltpu.CompilerParams(vmem_limit_bytes=12 << 20),
        cost_estimate=cost(1),
        name="block_copy",
    )(jnp.stack([row, column]).astype(jnp.int32), array, after)


def payload_kernel(n_got, n_mine, s_ref, *refs):
    got, mine, out_ref = refs[:n_got], refs[n_got : n_got + n_mine], refs[-1]
    rows = got[0].shape[0]
    each = n_got // (out_ref.shape[0] // rows)
    for c in range(n_got // each):
        at = pl.ds(c * rows, rows)
        term = mine[0][0, at, :]
        if n_mine == 2:
            term = jnp.where(s_ref[4] > 0, mine[1][0, at, :], term)
        came = got[c * each][...]
        if each == 2:
            came = jnp.where(s_ref[4] > 0, got[c * each + 1][...], came)
        came = jnp.where(s_ref[2] > 0, came.astype(F32), 0.0)
        out_ref[at, :] = (came + jnp.where(s_ref[3] > 0, term, 0.0)).astype(BF16)


def payload(scalars, got, parts, hidden, rows_at, after):
    part, hid = got[0].shape
    rows = part * parts
    step = block_of(hid, 1792)
    grid_spec = pltpu.PrefetchScalarGridSpec(
        num_scalar_prefetch=1,
        grid=(hid // step,),
        in_specs=[pl.BlockSpec((part, step), lambda i, s: (0, i))] * len(got)
        + [
            pl.BlockSpec((1, rows, step), lambda i, s, j=j: (s[j], rows_at[j] // rows, i))
            for j in range(len(hidden))
        ]
        + [ANYWHERE],
        out_specs=pl.BlockSpec((rows, step), lambda i, s: (0, i)),
    )

    def kernel(*refs):
        payload_kernel(len(got), len(hidden), *refs)

    return pl.pallas_call(
        kernel,
        grid_spec=grid_spec,
        out_shape=jax.ShapeDtypeStruct((rows, hid), BF16),
        compiler_params=pltpu.CompilerParams(vmem_limit_bytes=PAYLOAD_LIMIT << 20),
        cost_estimate=SHORT,
        name="payload",
    )(scalars, *got, *hidden, after)


def first_kernel(n, cores, s_ref, own_gate, proj, *refs):
    group = n // cores
    held, out_ref = refs[-2 - group : -2], refs[-1]
    gates = [
        jnp.concatenate([ref[...] for ref in refs[i * CHUNKS : (i + 1) * CHUNKS]])
        for i in range(2 * n - 2)
    ]

    @pl.when(pl.program_id(0) == 0)
    def _():
        out_ref[...] = jnp.zeros_like(out_ref)

    for k in range(n):
        if k:
            up, down = gates[2 * k - 2 : 2 * k], gates[2 * (n - 1 - k) : 2 * (n - k)]
            below = up[0] if k == 1 else jnp.where(s_ref[n] > 0, up[0], up[1])
            above = down[1] if k == n - 1 else jnp.where(s_ref[n] > 0, down[1], down[0])
            gate = jnp.where(s_ref[n + k] > 0, below, above)
        else:
            gate = own_gate[...]
        hidden = held[k % group][0]
        for e in range(1, cores):
            hidden = jnp.where(s_ref[k] == e, held[k % group][e], hidden)
        high, low = split(hidden * gate.astype(F32))
        out_ref[k] += lax.dot_general(
            proj[...], high, ROWS_ROWS, preferred_element_type=F32
        ) + lax.dot_general(proj[...], low, ROWS_ROWS, preferred_element_type=F32)


def projected_first(n, cores, scalars, gate_act, proj_t, gates, hidden, after):
    part, hid = gates[0].shape
    half = part * CHUNKS
    step = block_of(hid, 512)
    flat = pl.BlockSpec((half, step), lambda i, s: (0, i))
    grid_spec = pltpu.PrefetchScalarGridSpec(
        num_scalar_prefetch=1,
        grid=(hid // step,),
        in_specs=[
            flat,
            pl.BlockSpec((R, step), lambda i, s: (0, i)),
        ]
        + [pl.BlockSpec((part, step), lambda i, s: (0, i))] * len(gates)
        + [pl.BlockSpec((cores, half, step), lambda i, s: (0, 0, i))] * len(hidden)
        + [ANYWHERE],
        out_specs=pl.BlockSpec((n, R, half), lambda i, s: (0, 0, 0)),
    )

    def kernel(*refs):
        first_kernel(n, cores, *refs)

    return pl.pallas_call(
        kernel,
        grid_spec=grid_spec,
        out_shape=jax.ShapeDtypeStruct((n, R, half), F32),
        compiler_params=pltpu.CompilerParams(vmem_limit_bytes=FIRST_LIMIT << 20),
        cost_estimate=cost(16),
        name="projected_first",
    )(scalars, gate_act, proj_t, *gates, *hidden, after)


def inputs_kernel(x_ref, proj_ref, after_ref, out_ref):
    del after_ref
    out_ref[...] = jnp.dot(x_ref[...], proj_ref[...], preferred_element_type=F32)


def projected_inputs(inputs, proj_in, after):
    whole = pl.BlockSpec(memory_space=pltpu.VMEM)
    return pl.pallas_call(
        inputs_kernel,
        in_specs=[whole, whole, ANYWHERE],
        out_specs=whole,
        out_shape=jax.ShapeDtypeStruct((inputs.shape[0], R), F32),
        compiler_params=pltpu.CompilerParams(vmem_limit_bytes=12 << 20),
        cost_estimate=cost(1),
        name="projected_inputs",
    )(inputs, proj_in, after)


def local(grad_out, inputs, gate_act, w_down, proj_in, proj_out, queries, example_of):
    n = lax.axis_size("blk")
    cores = lax.axis_size("sub")
    n_f = lax.axis_size("fsdp")
    z, x, core = lax.axis_index("blk"), lax.axis_index("fsdp"), lax.axis_index("sub")
    tok = grad_out.shape[0]
    hid, dblk = w_down.shape
    group = n // cores
    half = tok // 2

    def features(p):
        part = tok // n_f
        mine = lax.dynamic_slice(grad_out, (x * part, ((z + p) % group) * dblk), (part, dblk))
        route = []
        for zs in range(n):
            for cs in range(cores):
                zd = cs * group + (zs + p) % group
                route.append((zs * cores + cs, zd * cores + zs // group))
        return lax.ppermute(mine, ("blk", "sub"), route)

    def whole_of(got, after):
        parts = [got] + [shifted(got, "fsdp", e) for e in range(1, n_f)]
        return join(parts, x, after)

    def spread(whole):
        return [whole] + [shifted(whole, "sub", e) for e in range(1, cores)]

    def block_at(distance):
        return (core - ((z - distance) % n) // group) % cores

    def needed(step):
        return sorted({step % group, (n - step) % group})

    begin = needed(1)
    later = [p for p in range(group) if p not in begin]
    features_of = {p: features(p) for p in begin + later}
    part = half // CHUNKS
    even = x % 2 == 0
    came = []
    for c in range(CHUNKS):
        own = gate_act[c * part : (c + 1) * part]
        came.append([[line_right(own), line_left(own)]])
    waits = came[0][0] + [features_of[p] for p in later[:1]]
    whole = {p: whole_of(features_of[p], waits) for p in begin}
    spreads = {p: spread(whole[p]) for p in begin}
    last = example_of
    second, first = {}, {}
    for p in begin:
        last = hidden_grad(spreads[p], w_down, half, half, last)
        second[p] = (last, 0)
    for p in later:
        whole[p] = whole_of(features_of[p], [last])
    last, middle = whole[later[0]], None

    def counts(rightward):
        return jnp.where(rightward, z > 0, z < n - 1)

    for s in range(1, n):
        parts = [came] if s == n - 1 else [[stream] for stream in came]
        sent = []
        for c, streams in enumerate(parts):
            both = []
            for reverse in (False, True):
                rightward = even != reverse
                right, left = block_at(s), block_at(n - s)
                flags = [
                    counts(rightward),
                    jnp.where(rightward, z < s, z + s >= n),
                    jnp.logical_not(rightward),
                ]
                if s % group == (n - s) % group:
                    which, arrays = [jnp.where(rightward, right, left)] * 2, [second[s % group]]
                else:
                    which, arrays = [right, left], [second[s % group], second[(n - s) % group]]
                scalars = jnp.stack(which + [f.astype(jnp.int32) for f in flags])
                if s == 1:
                    got = [block for stream in streams for block in stream[-1]]
                else:
                    got = [stream[-1][int(reverse)] for stream in streams]
                rows_at = [start + c * part * len(streams) for _, start in arrays]
                arrays = [array for array, _ in arrays]
                last = payload(scalars, got, len(streams), arrays, rows_at, last)
                both.append(onward(last, reverse))
            sent.append(both)
        if s < n - 1:
            for stream, both in zip(came, sent, strict=True):
                stream.append(both)
        if s == n - 2:
            middle = last
        for p in needed(s + 1):
            if p not in second:
                spreads[p] = spread(whole[p])
                first[p] = last = hidden_grad(spreads[p], w_down, 0, tok, last)
                second[p] = (last, half)
        if s == n - 2:
            for p in begin:
                first[p] = last = hidden_grad(spreads[p], w_down, 0, half, last)

    width = R * R // cores
    own_q = block_copy(queries[0], 0 * z, 0 * z, queries.shape[1:], middle)
    own_q = own_q.reshape(cores, -1, width)
    got_q = [lax.dynamic_index_in_dim(own_q, core, 0, keepdims=False)]
    for e in range(1, cores):
        got_q.append(
            shifted(lax.dynamic_index_in_dim(own_q, (core + e) % cores, 0, keepdims=False), "sub", e)
        )
    own_q = jnp.concatenate([lax.select_n((core - i) % cores, *got_q) for i in range(cores)], axis=1)
    n_q = own_q.shape[0]
    flat_q = own_q.astype(F32).reshape(-1, half)

    gates = [came[c][s][d] for s in range(n - 1) for d in (0, 1) for c in range(CHUNKS)]
    scalars = [block_at(k) for k in range(n)] + [even] + [z >= k for k in range(1, n)]
    scalars = jnp.stack([f.astype(jnp.int32) for f in scalars])
    ups = projected_first(
        n,
        cores,
        scalars,
        gate_act,
        proj_out.T,
        gates,
        [first[p] for p in range(group)],
        last,
    )
    up_first = ups[0]
    got_q = [flat_q]
    for k in range(1, n):
        got = shifted(jnp.concatenate([ups[k], flat_q]), "blk", -k)
        up_first = up_first + got[:R]
        got_q.append(got[R:])
    all_q = jnp.stack([lax.select_n((i - z) % n, *got_q) for i in range(n)])
    all_q = all_q.reshape(n, n_q, R * R).astype(BF16)

    own_second = lax.dynamic_index_in_dim(second[0][0], block_at(0), 0, keepdims=False)[second[0][1] :]
    total = own_second + sum(
        jnp.where(counts(even != bool(d)), sent[0][d].astype(F32), 0.0) for d in (0, 1)
    )
    up_second = lax.dot_general(
        proj_out.astype(F32),
        total * gate_act[half:].astype(F32),
        (((0,), (1,)), ((), ())),
        precision=lax.Precision.HIGH,
        preferred_element_type=F32,
    )
    up_proj = summed(jnp.concatenate([up_first, up_second], axis=1), ("sub", "fsdp"))

    left_proj = summed(projected_inputs(inputs, proj_in, middle), ("sub", "fsdp"))
    onehot = (example_of[:, None] == jnp.arange(EX_DEV, dtype=jnp.int32)[None, :]).astype(F32)
    weighted = (onehot[:, :, None] * left_proj[:, None, :]).reshape(tok, EX_DEV * R)
    full_sketch = lax.dot_general(
        weighted, up_proj, (((0,), (1,)), ((), ())), precision=lax.Precision.HIGHEST
    )
    sketch = full_sketch.reshape(EX_DEV, R * R).astype(BF16)
    sketch_part = lax.dynamic_slice(sketch, (0, core * width), (EX_DEV, width))
    scores = lax.dot_general(
        sketch, all_q, (((1,), (2,)), ((), ())), preferred_element_type=F32
    )
    return sketch_part, scores


def solution(mesh):
    in_specs = (
        P(("groups", "blk"), "sub"),
        P(("groups", "blk"), ("fsdp", "sub")),
        P(("groups", "blk"), ("fsdp", "sub")),
        P(("fsdp", "sub"), "blk"),
        P(("fsdp", "sub"), None),
        P(("fsdp", "sub"), None),
        P(("groups", "blk"), "fsdp", "sub"),
        P(("groups", "blk")),
    )
    out_specs = (P(("groups", "blk"), "sub"), P(("groups", "blk"), None, ("fsdp", "sub")))
    return jax.shard_map(local, mesh=mesh, in_specs=in_specs, out_specs=out_specs, check_vma=False)
```

time: 182 us -> 166 us (0.912)
  starting transfers between devices: 95.1 us -> 32.8 us
  Pallas kernels: 0 us -> 28.6 us
  waiting for transfers between devices: 40.6 us -> 53.6 us
  local copies, waits for them, and re-layouts: 4.76 us -> 14.4 us
  other arithmetic: 9.52 us -> 3.93 us
    ppermute x11 -> x8, starting transfers between devices: 42.3 us -> 6.44 us  [shifted(): lax.ppermute(block, axis, [(i, (i + distance) % n) for i in range(n)])]
    pallas_call x0 -> x18, Pallas kernels: none -> 28.6 us  [the longest x10 15.9 us: payload(): pl.pallas_call(kernel, grid_spec=grid_spec, out_shape=jax.ShapeDtypeStruc...]
    ppermute x8 -> x2, starting transfers between devices: 32 us -> 6.16 us  [line_right(): return lax.ppermute(block, 'blk', [(i, i + 1) for i in range(n - 1)])]
    ppermute x11 -> x8, waiting for transfers between devices: 6.43 us -> 18.9 us  [shifted(): lax.ppermute(block, axis, [(i, (i + distance) % n) for i in range(n)])]
    ppermute x2 -> x12, starting transfers between devices: 4.84 us -> 15 us  [the longest x10 11.3 us: onward(): return lax.ppermute(block, ('blk', 'fsdp'), route)]
    unnamed x52 -> x53, local copies, waits for them, and re-layouts: 0.13 us -> 8.36 us
    ppermute x8 -> x2, starting transfers between devices: 10.5 us -> 2.58 us  [line_left(): return lax.ppermute(block, 'blk', [(i + 1, i) for i in range(n - 1)])]
    ppermute x8 -> x2, waiting for transfers between devices: 15.8 us -> 10.2 us  [line_left(): return lax.ppermute(block, 'blk', [(i + 1, i) for i in range(n - 1)])]
  transfers between devices with their start and end apart: 37 -> 28, of which waited for: 13 -> 11; matrix products, arithmetic and copies ran while one was open for 21% -> 22% of each run, Pallas kernels for 0% -> 17%
where the time goes in v2:
time: 166 us; the launch traced here: 165 us
  waiting for transfers between devices  53.6 us (32%)
  starting transfers between devices  32.8 us (20%)
  matrix products  30.5 us (18%)
  Pallas kernels  28.6 us (17%)
  local copies, waits for them, and re-layouts  14.4 us (9%)
  other arithmetic  3.93 us (2%)
    dot_general x3, matrix products, hidden_grad(): lax.dot_general(stacked.reshape(-1, depth), w_down, ROWS_ROWS, preferred_...  26.3 us
    ppermute x8, waiting for transfers between devices, shifted(): lax.ppermute(block, axis, [(i, (i + distance) % n) for i in range(n)])  18.9 us
    pallas_call x10, Pallas kernels, payload(): pl.pallas_call(kernel, grid_spec=grid_spec, out_shape=jax.ShapeDtypeStruc...  15.9 us
    ppermute x10, starting transfers between devices, onward(): return lax.ppermute(block, ('blk', 'fsdp'), route)  11.3 us
    ppermute x2, waiting for transfers between devices, line_left(): return lax.ppermute(block, 'blk', [(i + 1, i) for i in range(n - 1)])  10.2 us
    ppermute x2, waiting for transfers between devices, features(): return lax.ppermute(mine, ('blk', 'sub'), route)  10.1 us
    pallas_call x1, Pallas kernels, projected_first(): pl.pallas_call(kernel, grid_spec=grid_spec, out_shape=jax.ShapeDtypeStruc...  10 us
    ppermute x2, waiting for transfers between devices, line_right(): return lax.ppermute(block, 'blk', [(i, i + 1) for i in range(n - 1)])  8.85 us
  transfers between devices with their start and end apart: 28, of which 11 were waited for; matrix products, arithmetic and copies ran while one was open for 22% of the time, Pallas kernels for 17%

profile of v2, /device:TPU:0, one launch (start us, length us, event | category | flops | bytes accessed | tf_op | source)
XLA Modules:
  0.0 165.4 jit_solution(6635891124435583594)
XLA Ops:
  0.7 1.4 fusion.30
  2.1 3.1 %collective-permute-start.2 = (bf16[128,2048]{1,0:T(8,128)(2,1)S(1)}, bf16[128,2048]{1,0:T(8,128)(2,1)S(1)}, u32[]{:S(2)}, u32[]{:S(2)}) collective-permute-start(bf16[128,2048]{1,0:T(8,128)(2,1)S(1)} %get-tuple-element.3), channel_id=1, source_target_pairs={{0,4},{1,12},{4,0},{5,8},{8,5},{9,13},{12,1},{13,9},{2,6},{3,14},{... | collective-permute-start | bytes 1572872 | tf_op jit(solution)/shard_map/ppermute | solution.py:301
  5.2 0.7 collective-permute-start.6
  5.9 10.1 %collective-permute-done.2.refs_1_ = bf16[128,2048]{1,0:T(8,128)(2,1)S(1)} collective-permute-done((bf16[128,2048]{1,0:T(8,128)(2,1)S(1)}, bf16[128,2048]{1,0:T(8,128)(2,1)S(1)}, u32[]{:S(2)}, u32[]{:S(2)}) %collective-permute-start.2) | collective-permute-done | bytes 524320 | tf_op jit(solution)/shard_map/ppermute | solution.py:301
  16.0 2.4 %collective-permute-start.3 = (bf16[128,2048]{1,0:T(8,128)(2,1)S(1)}, bf16[128,2048]{1,0:T(8,128)(2,1)S(1)}, u32[]{:S(2)}, u32[]{:S(2)}) collective-permute-start(bf16[128,2048]{1,0:T(8,128)(2,1)S(1)} %collective-permute-done.2.refs_1_), channel_id=1, source_target_pairs={{0,2},{2,0},{1,3},{3,1},{4,6},{6,4},{5,7},{7,5},{8,10},{10,8},{9,1... | collective-permute-start | bytes 1572872 | tf_op jit(solution)/shard_map/ppermute | solution.py:42
  18.3 0.8 fusion.31
  19.2 3.7 %collective-permute-start.4 = (bf16[64,3584]{1,0:T(8,128)(2,1)S(1)}, bf16[64,3584]{1,0:T(8,128)(2,1)S(1)}, u32[]{:S(2)}, u32[]{:S(2)}) collective-permute-start(bf16[64,3584]{1,0:T(8,128)(2,1)S(1)} %get-tuple-element.4), channel_id=1, source_target_pairs={{0,4},{4,8},{8,12},{1,5},{5,9},{9,13},{2,6},{6,10},{10,14},{3,7},{... | collective-permute-start | bytes 1376264 | tf_op jit(solution)/shard_map/ppermute | solution.py:22
  22.8 1.3 collective-permute-start.5
  24.1 8.8 %collective-permute-done.4.refs_3_.refs_1_ = bf16[64,3584]{1,0:T(8,128)(2,1)S(1)} collective-permute-done((bf16[64,3584]{1,0:T(8,128)(2,1)S(1)}, bf16[64,3584]{1,0:T(8,128)(2,1)S(1)}, u32[]{:S(2)}, u32[]{:S(2)}) %collective-permute-start.4) | collective-permute-done | bytes 458784 | tf_op jit(solution)/shard_map/ppermute | solution.py:22
  33.0 7.0 %collective-permute-done.5.refs_4_.refs_2_.refs_5_ = bf16[64,3584]{1,0:T(8,128)(2,1)S(1)} collective-permute-done((bf16[64,3584]{1,0:T(8,128)(2,1)S(1)}, bf16[64,3584]{1,0:T(8,128)(2,1)S(1)}, u32[]{:S(2)}, u32[]{:S(2)}) %collective-permute-start.5) | collective-permute-done | bytes 458784 | tf_op jit(solution)/shard_map/ppermute | solution.py:27
  40.2 1.6 collective-permute-start.8
  41.8 1.1 collective-permute-done.7.refs_1_
  42.9 1.0 copy-done.8
  43.9 7.3 %fusion.4.refs_3_ = f32[2,128,3584]{2,1,0:T(8,128)S(1)} fusion(bf16[2,128,2048]{2,1,0:T(8,128)(2,1)S(1)} %stack.249, bf16[3584,2048]{1,0:T(8,128)(2,1)} %param.11), kind=kOutput, calls=%fused_computation.4 | convolution fusion | flops 3758096384 | bytes 19398656 | tf_op jit(solution)/shard_map/dot_general | solution.py:101
  51.2 3.3 %collective-permute-done.8.refs_2_ = bf16[128,2048]{1,0:T(8,128)(2,1)S(1)} collective-permute-done((bf16[128,2048]{1,0:T(8,128)(2,1)S(1)}, bf16[128,2048]{1,0:T(8,128)(2,1)S(1)}, u32[]{:S(2)}, u32[]{:S(2)}) %collective-permute-start.8) | collective-permute-done | bytes 524320 | tf_op jit(solution)/shard_map/ppermute | solution.py:42
  54.7 2.5 %collective-permute-start = (bf16[64,3584]{1,0:T(8,128)(2,1)}, bf16[64,3584]{1,0:T(8,128)(2,1)S(1)}, u32[]{:S(2)}, u32[]{:S(2)}) collective-permute-start(bf16[64,3584]{1,0:T(8,128)(2,1)} %get-tuple-element.5), channel_id=1, source_target_pairs={{0,4},{4,8},{8,12},{1,5},{5,9},{9,13},{2,6},{6,10},{10,14},{3,7},{... | collective-permute-start | bytes 1376264 | tf_op jit(solution)/shard_map/ppermute | solution.py:22
  57.2 1.3 collective-permute-start.1
  58.9 2.0 %copy.11.proj_ref = bf16[2048,64]{1,0:T(8,128)(2,1)} copy(bf16[2048,64]{0,1:T(8,128)(2,1)} %param.12) | data formatting | bytes 524288 | tf_op args[4]
  61.4 0.6 fusion.25
  62.0 0.6 stack.221.refs_0_
  62.6 2.0 %copy-done.2 = f32[2,128,3584]{2,1,0:T(8,128)S(1)} copy-done((f32[2,128,3584]{2,1,0:T(8,128)S(1)}, f32[2,128,3584]{2,1,0:T(8,128)}, u32[]{:S(2)}) %copy-start.2) | copy-done | bytes 3670040
  64.7 0.9 payload.10.refs_4_
  65.6 2.7 %collective-permute-start.13 = (bf16[64,3584]{1,0:T(8,128)(2,1)S(1)}, bf16[64,3584]{1,0:T(8,128)(2,1)S(1)}, u32[]{:S(2)}, u32[]{:S(2)}) collective-permute-start(bf16[64,3584]{1,0:T(8,128)(2,1)S(1)} %payload.10.refs_4_), channel_id=1, source_target_pairs={{0,4},{2,0},{4,8},{6,2},{8,12},{10,6},{12,14},{14,10},{1,5},{3,1},... | collective-permute-start | bytes 1376264 | tf_op jit(solution)/shard_map/ppermute | solution.py:37
  68.3 0.9 payload.11.refs_4_
  69.3 3.1 %collective-permute-done.1.refs_2_.refs_6_ = bf16[64,3584]{1,0:T(8,128)(2,1)} collective-permute-done((bf16[64,3584]{1,0:T(8,128)(2,1)}, bf16[64,3584]{1,0:T(8,128)(2,1)}, u32[]{:S(2)}, u32[]{:S(2)}) %collective-permute-start.1) | collective-permute-done | bytes 458784 | tf_op jit(solution)/shard_map/ppermute | solution.py:27
  72.4 1.7 %payload.12.refs_4_ = bf16[64,3584]{1,0:T(8,128)(2,1)S(1)} custom-call(s32[5]{0:T(128)S(1)} %stack.206.refs_0_, bf16[64,3584]{1,0:T(8,128)(2,1)S(1)} %collective-permute-done.refs_1_.refs_4_, bf16[64,3584]{1,0:T(8,128)(2,1)} %collective-permute-done.1.refs_2_.refs_6_, f32[2,128,3584]{2,1,0:T(8,128)S(1)} %copy-done.3, bf16[64,3584]{1,0:T(8,128)(2,1)S(1)} %payload.11.refs_4_), custom_call_target="tpu_custom_call" | custom-call | flops 1000 | bytes 1000 | tf_op jit(solution)/shard_map/payload/pallas_call | solution.py:195
  74.2 0.9 collective-permute-start.11
  75.0 1.7 %payload.13.refs_2_ = bf16[64,3584]{1,0:T(8,128)(2,1)S(1)} custom-call(s32[5]{0:T(128)S(1)} %stack.198.refs_0_, bf16[64,3584]{1,0:T(8,128)(2,1)S(1)} %collective-permute-done.refs_1_.refs_4_, bf16[64,3584]{1,0:T(8,128)(2,1)} %collective-permute-done.1.refs_2_.refs_6_, f32[2,128,3584]{2,1,0:T(8,128)S(1)} %copy-done.3, bf16[64,3584]{1,0:T(8,128)(2,1)S(1)} %payload.12.refs_4_), custom_call_target="tpu_custom_call" | custom-call | flops 1000 | bytes 1000 | tf_op jit(solution)/shard_map/payload/pallas_call | solution.py:195
  76.8 1.3 collective-permute-start.9
  78.1 1.4 stack.250
  79.4 11.3 %fusion.2.refs_2_.refs_3_.refs_15_ = f32[2,256,3584]{2,1,0:T(8,128)S(1)} fusion(bf16[2,256,2048]{2,1,0:T(8,128)(2,1)S(1)} %stack.250, bf16[3584,2048]{1,0:T(8,128)(2,1)} %param.11), kind=kOutput, calls=%fused_computation.2 | convolution fusion | flops 7516192768 | bytes 24117248 | tf_op jit(solution)/shard_map/dot_general | solution.py:101
  90.7 2.0 %payload.14.refs_3_ = bf16[64,3584]{1,0:T(8,128)(2,1)} custom-call(s32[5]{0:T(128)S(1)} %stack.209.refs_0_, bf16[64,3584]{1,0:T(8,128)(2,1)S(1)} %collective-permute-done.13.refs_1_.refs_7_, f32[2,256,3584]{2,1,0:T(8,128)S(1)} %fusion.2.refs_2_.refs_3_.refs_15_, f32[2,256,3584]{2,1,0:T(8,128)S(1)} %fusion.2.refs_2_.refs_3_.refs_15_), custom_call_target="tpu_custom_call" | custom-call | flops 1000 | bytes 1000 | tf_op jit(solution)/shard_map/payload/pallas_call | solution.py:195
  92.8 0.8 collective-permute-start.16
  93.6 1.5 payload.15.refs_3_
  95.1 1.2 collective-permute-start.18
  96.4 1.5 payload.16.refs_3_
  97.9 0.8 collective-permute-start.17
  98.8 0.9 payload.17.after_ref.refs_2_
  99.7 1.5 collective-permute-start.19
  101.7 0.6 dynamic-slice_bitcast_fusion.1
  102.4 1.0 copy-done.18
  103.4 7.7 %fusion.refs_4_.refs_16_ = f32[2,128,3584]{2,1,0:T(8,128)S(1)} fusion(bf16[2,128,2048]{2,1,0:T(8,128)(2,1)} %copy-done.18, bf16[3584,2048]{1,0:T(8,128)(2,1)} %param.11), kind=kOutput, calls=%fused_computation | convolution fusion | flops 3758096384 | bytes 19398656 | tf_op jit(solution)/shard_map/dot_general | solution.py:101
  111.2 1.0 copy-done.12
  112.2 1.2 copy-done.19
  114.4 0.8 bitcast_select_fusion.1
  115.4 0.7 add.190
  116.1 1.9 %collective-permute-start.15 = (f32[256,64]{1,0:T(8,128)}, f32[256,64]{1,0:T(8,128)}, u32[]{:S(2)}, u32[]{:S(2)}) collective-permute-start(f32[256,64]{1,0:T(8,128)} %add.190), channel_id=1, source_target_pairs={{0,2},{2,0},{1,3},{3,1},{4,6},{6,4},{5,7},{7,5},{8,10},{10,8},{9,1... | collective-permute-start | bytes 196616 | tf_op jit(solution)/shard_map/ppermute | solution.py:59
  117.9 2.8 %payload.18.refs_4_ = bf16[128,3584]{1,0:T(8,128)(2,1)} custom-call(s32[5]{0:T(128)S(1)} %stack.229.refs_0_, bf16[64,3584]{1,0:T(8,128)(2,1)} %collective-permute-done.16.refs_1_.refs_11_, bf16[64,3584]{1,0:T(8,128)(2,1)} %collective-permute-done.17.refs_2_.refs_12_, f32[2,128,3584]{2,1,0:T(8,128)S(1)} %copy-done.4, f32[2,128,3584]{2,1,0:T(8,128)S(1)} %fusion.refs_4_.refs_16_), custom_call_target="tpu_custom_call" | custom-call | flops 1000 | bytes 1000 | tf_op jit(solution)/shard_map/payload/pallas_call | solution.py:195
  120.7 0.8 collective-permute-start.24
  121.5 1.8 %payload.19.refs_17_ = bf16[128,3584]{1,0:T(8,128)(2,1)S(1)} custom-call(s32[5]{0:T(128)S(1)} %stack.225.refs_0_, bf16[64,3584]{1,0:T(8,128)(2,1)S(1)} %collective-permute-done.18.refs_1_.refs_13_, bf16[64,3584]{1,0:T(8,128)(2,1)} %collective-permute-done.19.refs_2_.refs_14_, f32[2,128,3584]{2,1,0:T(8,128)S(1)} %copy-done.4, bf16[128,3584]{1,0:T(8,128)(2,1)} %payload.18.refs_4_), custom_call_target="tpu_custom_call" | custom-call | flops 1000 | bytes 1000 | tf_op jit(solution)/shard_map/payload/pallas_call | solution.py:195
  123.4 1.3 collective-permute-start.25
  124.7 1.0 add.191
  125.9 10.0 %projected_first.1 = f32[4,64,128]{2,1,0:T(8,128)} custom-call(s32[8]{0:T(128)} %stack.221.refs_0_, bf16[256,3584]{1,0:T(8,128)(2,1)} %refs_1_.1, bf16[64,3584]{1,0:T(8,128)(2,1)} %bitcast.67, bf16[64,3584]{1,0:T(8,128)(2,1)} %copy-done.6, bf16[64,3584]{1,0:T(8,128)(2,1)} %copy-done.10, bf16[64,3584]{1,0:T(8,128)(2,1)} %copy-done.7, ...), custom_call_target="tpu_custom_call" | custom-call | flops 1000 | bytes 59040000 | tf_op jit(solution)/shard_map/projected_first/pallas_call | solution.py:255
  135.9 0.8 slice_bitcast_fusion.2
  136.8 2.3 %collective-permute-start.22 = (f32[192,128]{1,0:T(8,128)S(1)}, f32[192,128]{1,0:T(8,128)S(1)}, u32[]{:S(2)}, u32[]{:S(2)}) collective-permute-start(f32[192,128]{1,0:T(8,128)S(1)} %get-tuple-element.13), channel_id=1, source_target_pairs={{0,8},{4,12},{8,0},{12,4},{1,9},{5,13},{9,1},{13,5},{2,10},{6,14},... | collective-permute-start | bytes 294920 | tf_op jit(solution)/shard_map/ppermute | solution.py:42
  139.2 8.7 %collective-permute-done.21 = f32[192,128]{1,0:T(8,128)S(1)} collective-permute-done((f32[192,128]{1,0:T(8,128)S(1)}, f32[192,128]{1,0:T(8,128)S(1)}, u32[]{:S(2)}, u32[]{:S(2)}) %collective-permute-start.21) | collective-permute-done | bytes 98336 | tf_op jit(solution)/shard_map/ppermute | solution.py:42
  147.8 5.8 %collective-permute-done.22 = f32[192,128]{1,0:T(8,128)S(1)} collective-permute-done((f32[192,128]{1,0:T(8,128)S(1)}, f32[192,128]{1,0:T(8,128)S(1)}, u32[]{:S(2)}, u32[]{:S(2)}) %collective-permute-start.22) | collective-permute-done | bytes 98336 | tf_op jit(solution)/shard_map/ppermute | solution.py:42
  153.7 0.8 slice_add_fusion
  154.5 2.7 %fusion.16 = f32[64,128]{1,0:T(8,128)S(1)} fusion(bf16[3584,64]{0,1:T(8,128)(2,1)S(1)} %copy-done.24, f32[2,256,3584]{2,1,0:T(8,128)} %copy-done, s32[]{:T(128)S(6)} %select_n.455, s32[]{:T(128)S(6)} %add.214, bf16[128,3584]{1,0:T(8,128)(2,1)S(1)} %collective-permute-done.25, bf16[128,3584]{1,0:T(8,128)(2,1)} %collective-permute-done.24, ...), kind=kOutput, calls=%fused_computation.17 | convolution fusion | flops 179830784 | bytes 5079050 | tf_op jit(solution)/shard_map/dot_general | solution.py:419
  157.3 1.2 collective-permute-done.26
  158.7 4.1 %collective-permute-done.27 = f32[64,256]{1,0:T(8,128)S(1)} collective-permute-done((f32[64,256]{1,0:T(8,128)S(1)}, f32[64,256]{1,0:T(8,128)S(1)}, u32[]{:S(2)}, u32[]{:S(2)}) %collective-permute-start.27) | collective-permute-done | bytes 65568 | tf_op jit(solution)/shard_map/ppermute | solution.py:59
  162.8 0.6 convolution_convert_fusion
  164.0 0.6 constant_dynamic-slice_fusion
  164.6 0.8 fusion.23
  (104 shorter events, 4.0 us)
Async XLA Ops:
  0.6 17.7 %copy-start.22 = (bf16[256,3584]{1,0:T(8,128)(2,1)S(1)}, bf16[256,3584]{1,0:T(8,128)(2,1)}, u32[]{:S(2)}) copy-start(bf16[256,3584]{1,0:T(8,128)(2,1)} %refs_1_.1) | copy-start | bytes 5505028
  2.1 13.9 %collective-permute-start.2 = (bf16[128,2048]{1,0:T(8,128)(2,1)S(1)}, bf16[128,2048]{1,0:T(8,128)(2,1)S(1)}, u32[]{:S(2)}, u32[]{:S(2)}) collective-permute-start(bf16[128,2048]{1,0:T(8,128)(2,1)S(1)} %get-tuple-element.3), channel_id=1, source_target_pairs={{0,4},{1,12},{4,0},{5,8},{8,5},{9,13},{12,1},{13,9},{2,6},{3,14},{... | collective-permute-start | bytes 1572872 | tf_op jit(solution)/shard_map/ppermute | solution.py:301
  5.2 34.9 %collective-permute-start.6 = (bf16[128,2048]{1,0:T(8,128)(2,1)S(1)}, bf16[128,2048]{1,0:T(8,128)(2,1)S(1)}, u32[]{:S(2)}, u32[]{:S(2)}) collective-permute-start(bf16[128,2048]{1,0:T(8,128)(2,1)S(1)} %get-tuple-element.2), channel_id=1, source_target_pairs={{0,0},{1,8},{4,4},{5,12},{8,1},{9,9},{12,5},{13,13},{2,2},{3,10},{... | collective-permute-start | bytes 1572872 | tf_op jit(solution)/shard_map/ppermute | solution.py:301
  16.0 24.1 %collective-permute-start.3 = (bf16[128,2048]{1,0:T(8,128)(2,1)S(1)}, bf16[128,2048]{1,0:T(8,128)(2,1)S(1)}, u32[]{:S(2)}, u32[]{:S(2)}) collective-permute-start(bf16[128,2048]{1,0:T(8,128)(2,1)S(1)} %collective-permute-done.2.refs_1_), channel_id=1, source_target_pairs={{0,2},{2,0},{1,3},{3,1},{4,6},{6,4},{5,7},{7,5},{8,10},{10,8},{9,1... | collective-permute-start | bytes 1572872 | tf_op jit(solution)/shard_map/ppermute | solution.py:42
  19.2 23.7 %copy-start.21 = (s32[256]{0:T(256)S(1)}, s32[256]{0:T(256)}, u32[]{:S(2)}) copy-start(s32[256]{0:T(256)} %refs_2_.1) | copy-start | bytes 3076
  19.2 13.8 %collective-permute-start.4 = (bf16[64,3584]{1,0:T(8,128)(2,1)S(1)}, bf16[64,3584]{1,0:T(8,128)(2,1)S(1)}, u32[]{:S(2)}, u32[]{:S(2)}) collective-permute-start(bf16[64,3584]{1,0:T(8,128)(2,1)S(1)} %get-tuple-element.4), channel_id=1, source_target_pairs={{0,4},{4,8},{8,12},{1,5},{5,9},{9,13},{2,6},{6,10},{10,14},{3,7},{... | collective-permute-start | bytes 1376264 | tf_op jit(solution)/shard_map/ppermute | solution.py:22
  22.8 17.2 %collective-permute-start.5 = (bf16[64,3584]{1,0:T(8,128)(2,1)S(1)}, bf16[64,3584]{1,0:T(8,128)(2,1)S(1)}, u32[]{:S(2)}, u32[]{:S(2)}) collective-permute-start(bf16[64,3584]{1,0:T(8,128)(2,1)S(1)} %get-tuple-element.4), channel_id=1, source_target_pairs={{4,0},{8,4},{12,8},{5,1},{9,5},{13,9},{6,2},{10,6},{14,10},{7,3},{... | collective-permute-start | bytes 1376264 | tf_op jit(solution)/shard_map/ppermute | solution.py:27
  33.0 35.3 %copy-start.6 = (bf16[64,3584]{1,0:T(8,128)(2,1)}, bf16[64,3584]{1,0:T(8,128)(2,1)S(1)}, u32[]{:S(2)}) copy-start(bf16[64,3584]{1,0:T(8,128)(2,1)S(1)} %collective-permute-done.4.refs_3_.refs_1_) | copy-start | bytes 1376260
  40.0 28.3 %copy-start.7 = (bf16[64,3584]{1,0:T(8,128)(2,1)}, bf16[64,3584]{1,0:T(8,128)(2,1)S(1)}, u32[]{:S(2)}) copy-start(bf16[64,3584]{1,0:T(8,128)(2,1)S(1)} %collective-permute-done.5.refs_4_.refs_2_.refs_5_) | copy-start | bytes 1376260
  40.1 2.7 %collective-permute-start.7 = (bf16[256,2048]{1,0:T(8,128)(2,1)S(1)}, bf16[256,2048]{1,0:T(8,128)(2,1)S(1)}, u32[]{:S(2)}, u32[]{:S(2)}) collective-permute-start(bf16[256,2048]{1,0:T(8,128)(2,1)S(1)} %join.2.refs_0_), channel_id=1, source_target_pairs={{0,1},{1,0},{2,3},{3,2},{4,5},{5,4},{6,7},{7,6},{8,9},{9,8},{10,11... | collective-permute-start | bytes 3145736 | tf_op jit(solution)/shard_map/ppermute | solution.py:42
  40.2 14.3 %collective-permute-start.8 = (bf16[128,2048]{1,0:T(8,128)(2,1)S(1)}, bf16[128,2048]{1,0:T(8,128)(2,1)S(1)}, u32[]{:S(2)}, u32[]{:S(2)}) collective-permute-start(bf16[128,2048]{1,0:T(8,128)(2,1)S(1)} %collective-permute-done.6.refs_5_.refs_1_), channel_id=1, source_target_pairs={{0,2},{2,0},{1,3},{3,1},{4,6},{6,4},{5,7},{7,5},{8,10},{10,8},{9,1... | collective-permute-start | bytes 1572872 | tf_op jit(solution)/shard_map/ppermute | solution.py:42
  42.9 1.0 copy-start.8
  51.2 3.4 %copy-start.1 = (f32[2,128,3584]{2,1,0:T(8,128)}, f32[2,128,3584]{2,1,0:T(8,128)S(1)}, u32[]{:S(2)}) copy-start(f32[2,128,3584]{2,1,0:T(8,128)S(1)} %fusion.4.refs_3_) | copy-start | bytes 11010052
  54.6 23.4 %collective-permute-start.10 = (bf16[256,2048]{1,0:T(8,128)(2,1)S(1)}, bf16[256,2048]{1,0:T(8,128)(2,1)}, u32[]{:S(2)}, u32[]{:S(2)}) collective-permute-start(bf16[256,2048]{1,0:T(8,128)(2,1)S(1)} %join.3.refs_4_.refs_0_), channel_id=1, source_target_pairs={{0,1},{1,0},{2,3},{3,2},{4,5},{5,4},{6,7},{7,6},{8,9},{9,8},{10,11... | collective-permute-start | bytes 3145736 | tf_op jit(solution)/shard_map/ppermute | solution.py:42
  54.7 14.6 %collective-permute-start = (bf16[64,3584]{1,0:T(8,128)(2,1)}, bf16[64,3584]{1,0:T(8,128)(2,1)S(1)}, u32[]{:S(2)}, u32[]{:S(2)}) collective-permute-start(bf16[64,3584]{1,0:T(8,128)(2,1)} %get-tuple-element.5), channel_id=1, source_target_pairs={{0,4},{4,8},{8,12},{1,5},{5,9},{9,13},{2,6},{6,10},{10,14},{3,7},{... | collective-permute-start | bytes 1376264 | tf_op jit(solution)/shard_map/ppermute | solution.py:22
  57.2 15.2 %collective-permute-start.1 = (bf16[64,3584]{1,0:T(8,128)(2,1)}, bf16[64,3584]{1,0:T(8,128)(2,1)}, u32[]{:S(2)}, u32[]{:S(2)}) collective-permute-start(bf16[64,3584]{1,0:T(8,128)(2,1)} %get-tuple-element.5), channel_id=1, source_target_pairs={{4,0},{8,4},{12,8},{5,1},{9,5},{13,9},{6,2},{10,6},{14,10},{7,3},{... | collective-permute-start | bytes 1376264 | tf_op jit(solution)/shard_map/ppermute | solution.py:27
  62.6 2.0 %copy-start.2 = (f32[2,128,3584]{2,1,0:T(8,128)S(1)}, f32[2,128,3584]{2,1,0:T(8,128)}, u32[]{:S(2)}) copy-start(f32[2,128,3584]{2,1,0:T(8,128)} %copy-done.1) | copy-start | bytes 11010052
  65.6 6.8 %copy-start.3 = (f32[2,128,3584]{2,1,0:T(8,128)S(1)}, f32[2,128,3584]{2,1,0:T(8,128)}, u32[]{:S(2)}) copy-start(f32[2,128,3584]{2,1,0:T(8,128)} %copy-done.1) | copy-start | bytes 11010052
  65.6 25.1 %collective-permute-start.13 = (bf16[64,3584]{1,0:T(8,128)(2,1)S(1)}, bf16[64,3584]{1,0:T(8,128)(2,1)S(1)}, u32[]{:S(2)}, u32[]{:S(2)}) collective-permute-start(bf16[64,3584]{1,0:T(8,128)(2,1)S(1)} %payload.10.refs_4_), channel_id=1, source_target_pairs={{0,4},{2,0},{4,8},{6,2},{8,12},{10,6},{12,14},{14,10},{1,5},{3,1},... | collective-permute-start | bytes 1376264 | tf_op jit(solution)/shard_map/ppermute | solution.py:37
  69.2 24.4 %collective-permute-start.12 = (bf16[64,3584]{1,0:T(8,128)(2,1)S(1)}, bf16[64,3584]{1,0:T(8,128)(2,1)S(1)}, u32[]{:S(2)}, u32[]{:S(2)}) collective-permute-start(bf16[64,3584]{1,0:T(8,128)(2,1)S(1)} %payload.11.refs_4_), channel_id=1, source_target_pairs={{0,2},{2,6},{4,0},{6,10},{8,4},{10,14},{12,8},{14,12},{1,3},{3,7},... | collective-permute-start | bytes 1376264 | tf_op jit(solution)/shard_map/ppermute | solution.py:37
  69.3 5.8 %copy-start.10 = (bf16[64,3584]{1,0:T(8,128)(2,1)}, bf16[64,3584]{1,0:T(8,128)(2,1)S(1)}, u32[]{:S(2)}) copy-start(bf16[64,3584]{1,0:T(8,128)(2,1)S(1)} %collective-permute-done.refs_1_.refs_4_) | copy-start | bytes 1376260
  74.2 22.2 %collective-permute-start.11 = (bf16[64,3584]{1,0:T(8,128)(2,1)S(1)}, bf16[64,3584]{1,0:T(8,128)(2,1)S(1)}, u32[]{:S(2)}, u32[]{:S(2)}) collective-permute-start(bf16[64,3584]{1,0:T(8,128)(2,1)S(1)} %payload.12.refs_4_), channel_id=1, source_target_pairs={{0,4},{2,0},{4,8},{6,2},{8,12},{10,6},{12,14},{14,10},{1,5},{3,1},... | collective-permute-start | bytes 1376264 | tf_op jit(solution)/shard_map/ppermute | solution.py:37
  76.8 22.0 %collective-permute-start.9 = (bf16[64,3584]{1,0:T(8,128)(2,1)S(1)}, bf16[64,3584]{1,0:T(8,128)(2,1)S(1)}, u32[]{:S(2)}, u32[]{:S(2)}) collective-permute-start(bf16[64,3584]{1,0:T(8,128)(2,1)S(1)} %payload.13.refs_2_), channel_id=1, source_target_pairs={{0,2},{2,6},{4,0},{6,10},{8,4},{10,14},{12,8},{14,12},{1,3},{3,7},... | collective-permute-start | bytes 1376264 | tf_op jit(solution)/shard_map/ppermute | solution.py:37
  90.7 8.0 %copy-start = (f32[2,256,3584]{2,1,0:T(8,128)}, f32[2,256,3584]{2,1,0:T(8,128)S(1)}, u32[]{:S(2)}) copy-start(f32[2,256,3584]{2,1,0:T(8,128)S(1)} %fusion.2.refs_2_.refs_3_.refs_15_) | copy-start | bytes 22020100
  90.7 2.1 %copy-start.14 = (bf16[64,3584]{1,0:T(8,128)(2,1)}, bf16[64,3584]{1,0:T(8,128)(2,1)S(1)}, u32[]{:S(2)}) copy-start(bf16[64,3584]{1,0:T(8,128)(2,1)S(1)} %collective-permute-done.13.refs_1_.refs_7_) | copy-start | bytes 1376260
  92.8 25.1 %collective-permute-start.16 = (bf16[64,3584]{1,0:T(8,128)(2,1)}, bf16[64,3584]{1,0:T(8,128)(2,1)}, u32[]{:S(2)}, u32[]{:S(2)}) collective-permute-start(bf16[64,3584]{1,0:T(8,128)(2,1)} %payload.14.refs_3_), channel_id=1, source_target_pairs={{0,4},{2,0},{4,8},{6,2},{8,12},{10,6},{12,14},{14,10},{1,5},{3,1},... | collective-permute-start | bytes 1376264 | tf_op jit(solution)/shard_map/ppermute | solution.py:37
  93.6 1.5 copy-start.15
  95.1 26.4 %collective-permute-start.18 = (bf16[64,3584]{1,0:T(8,128)(2,1)}, bf16[64,3584]{1,0:T(8,128)(2,1)S(1)}, u32[]{:S(2)}, u32[]{:S(2)}) collective-permute-start(bf16[64,3584]{1,0:T(8,128)(2,1)} %payload.15.refs_3_), channel_id=1, source_target_pairs={{0,2},{2,6},{4,0},{6,10},{8,4},{10,14},{12,8},{14,12},{1,3},{3,7},... | collective-permute-start | bytes 1376264 | tf_op jit(solution)/shard_map/ppermute | solution.py:37
  96.4 1.5 copy-start.16
  97.9 3.2 %copy-start.20 = (bf16[1,8,2048]{2,1,0:T(8,128)(2,1)S(1)}, bf16[1,8,2048]{2,1,0:T(8,128)(2,1)}, u32[]{:S(2)}) copy-start(bf16[1,8,2048]{2,1,0:T(8,128)(2,1)} %param.14) | copy-start | bytes 98308
  97.9 4.4 %copy-start.9 = (bf16[256,2048]{1,0:T(8,128)(2,1)S(1)}, bf16[256,2048]{1,0:T(8,128)(2,1)}, u32[]{:S(2)}) copy-start(bf16[256,2048]{1,0:T(8,128)(2,1)} %copy-done.8) | copy-start | bytes 3145732
  97.9 20.0 %collective-permute-start.17 = (bf16[64,3584]{1,0:T(8,128)(2,1)}, bf16[64,3584]{1,0:T(8,128)(2,1)}, u32[]{:S(2)}, u32[]{:S(2)}) collective-permute-start(bf16[64,3584]{1,0:T(8,128)(2,1)} %payload.16.refs_3_), channel_id=1, source_target_pairs={{0,4},{2,0},{4,8},{6,2},{8,12},{10,6},{12,14},{14,10},{1,5},{3,1},... | collective-permute-start | bytes 1376264 | tf_op jit(solution)/shard_map/ppermute | solution.py:37
  98.8 0.9 copy-start.17
  99.7 21.9 %collective-permute-start.19 = (bf16[64,3584]{1,0:T(8,128)(2,1)S(1)}, bf16[64,3584]{1,0:T(8,128)(2,1)}, u32[]{:S(2)}, u32[]{:S(2)}) collective-permute-start(bf16[64,3584]{1,0:T(8,128)(2,1)S(1)} %payload.17.after_ref.refs_2_), channel_id=1, source_target_pairs={{0,2},{2,6},{4,0},{6,10},{8,4},{10,14},{12,8},{14,12},{1,3},{3,7},... | collective-permute-start | bytes 1376264 | tf_op jit(solution)/shard_map/ppermute | solution.py:37
  102.3 11.5 %collective-permute-start.20 = (bf16[4,2048]{1,0:T(4,128)(2,1)}, bf16[4,2048]{1,0:T(4,128)(2,1)}, u32[]{:S(2)}, u32[]{:S(2)}) collective-permute-start(bf16[4,2048]{1,0:T(4,128)(2,1)} %dynamic-slice_bitcast_fusion.1), channel_id=1, source_target_pairs={{0,1},{1,0},{2,3},{3,2},{4,5},{5,4},{6,7},{7,6},{8,9},{9,8},{10,11... | collective-permute-start | bytes 49160 | tf_op jit(solution)/shard_map/ppermute | solution.py:42
  102.4 1.0 copy-start.18
  103.4 14.5 %copy-start.4 = (f32[2,128,3584]{2,1,0:T(8,128)S(1)}, f32[2,128,3584]{2,1,0:T(8,128)}, u32[]{:S(2)}) copy-start(f32[2,128,3584]{2,1,0:T(8,128)} %copy-done.1) | copy-start | bytes 11010052
  111.1 1.0 copy-start.12
  112.2 1.2 copy-start.19
  113.4 7.3 %copy-start.5 = (f32[2,128,3584]{2,1,0:T(8,128)}, f32[2,128,3584]{2,1,0:T(8,128)S(1)}, u32[]{:S(2)}) copy-start(f32[2,128,3584]{2,1,0:T(8,128)S(1)} %fusion.refs_4_.refs_16_) | copy-start | bytes 11010052
  113.8 1.6 collective-permute-start.14
  116.1 8.7 %collective-permute-start.15 = (f32[256,64]{1,0:T(8,128)}, f32[256,64]{1,0:T(8,128)}, u32[]{:S(2)}, u32[]{:S(2)}) collective-permute-start(f32[256,64]{1,0:T(8,128)} %add.190), channel_id=1, source_target_pairs={{0,2},{2,0},{1,3},{3,1},{4,6},{6,4},{5,7},{7,5},{8,10},{10,8},{9,1... | collective-permute-start | bytes 196616 | tf_op jit(solution)/shard_map/ppermute | solution.py:59
  120.7 33.7 %collective-permute-start.24 = (bf16[128,3584]{1,0:T(8,128)(2,1)}, bf16[128,3584]{1,0:T(8,128)(2,1)}, u32[]{:S(2)}, u32[]{:S(2)}) collective-permute-start(bf16[128,3584]{1,0:T(8,128)(2,1)} %payload.18.refs_4_), channel_id=1, source_target_pairs={{0,4},{2,0},{4,8},{6,2},{8,12},{10,6},{12,14},{14,10},{1,5},{3,1},... | collective-permute-start | bytes 2752520 | tf_op jit(solution)/shard_map/ppermute | solution.py:37
  121.5 1.8 %copy-start.13 = (bf16[64,3584]{1,0:T(8,128)(2,1)}, bf16[64,3584]{1,0:T(8,128)(2,1)S(1)}, u32[]{:S(2)}) copy-start(bf16[64,3584]{1,0:T(8,128)(2,1)S(1)} %collective-permute-done.18.refs_1_.refs_13_) | copy-start | bytes 1376260
  123.4 2.4 %copy-start.11 = (bf16[128,3584]{1,0:T(8,128)(2,1)}, bf16[128,3584]{1,0:T(8,128)(2,1)S(1)}, u32[]{:S(2)}) copy-start(bf16[128,3584]{1,0:T(8,128)(2,1)S(1)} %payload.19.refs_17_) | copy-start | bytes 2752516
  123.4 31.0 %collective-permute-start.25 = (bf16[128,3584]{1,0:T(8,128)(2,1)S(1)}, bf16[128,3584]{1,0:T(8,128)(2,1)S(1)}, u32[]{:S(2)}, u32[]{:S(2)}) collective-permute-start(bf16[128,3584]{1,0:T(8,128)(2,1)S(1)} %payload.19.refs_17_), channel_id=1, source_target_pairs={{0,2},{2,6},{4,0},{6,10},{8,4},{10,14},{12,8},{14,12},{1,3},{3,7},... | collective-permute-start | bytes 2752520 | tf_op jit(solution)/shard_map/ppermute | solution.py:37
  125.8 13.3 %copy-start.25 = (f32[256,8]{0,1:T(8,128)S(1)}, f32[256,8]{0,1:T(8,128)}, u32[]{:S(2)}) copy-start(f32[256,8]{0,1:T(8,128)} %fusion.25) | copy-start | bytes 24580
  125.8 28.6 %copy-start.23 = (bf16[256,3584]{1,0:T(8,128)(2,1)S(1)}, bf16[256,3584]{1,0:T(8,128)(2,1)}, u32[]{:S(2)}) copy-start(bf16[256,3584]{1,0:T(8,128)(2,1)} %refs_1_.1) | copy-start | bytes 5505028
  125.8 28.6 %copy-start.24 = (bf16[3584,64]{0,1:T(8,128)(2,1)S(1)}, bf16[3584,64]{0,1:T(8,128)(2,1)}, u32[]{:S(2)}) copy-start(bf16[3584,64]{0,1:T(8,128)(2,1)} %param.13) | copy-start | bytes 1376260
  136.7 11.1 %collective-permute-start.21 = (f32[192,128]{1,0:T(8,128)S(1)}, f32[192,128]{1,0:T(8,128)S(1)}, u32[]{:S(2)}, u32[]{:S(2)}) collective-permute-start(f32[192,128]{1,0:T(8,128)S(1)} %get-tuple-element.12), channel_id=1, source_target_pairs={{0,12},{4,0},{8,4},{12,8},{1,13},{5,1},{9,5},{13,9},{2,14},{6,2},{... | collective-permute-start | bytes 294920 | tf_op jit(solution)/shard_map/ppermute | solution.py:42
  136.8 16.9 %collective-permute-start.22 = (f32[192,128]{1,0:T(8,128)S(1)}, f32[192,128]{1,0:T(8,128)S(1)}, u32[]{:S(2)}, u32[]{:S(2)}) collective-permute-start(f32[192,128]{1,0:T(8,128)S(1)} %get-tuple-element.13), channel_id=1, source_target_pairs={{0,8},{4,12},{8,0},{12,4},{1,9},{5,13},{9,1},{13,5},{2,10},{6,14},... | collective-permute-start | bytes 294920 | tf_op jit(solution)/shard_map/ppermute | solution.py:42
  139.1 14.6 %collective-permute-start.23 = (f32[192,128]{1,0:T(8,128)S(1)}, f32[192,128]{1,0:T(8,128)S(1)}, u32[]{:S(2)}, u32[]{:S(2)}) collective-permute-start(f32[192,128]{1,0:T(8,128)S(1)} %get-tuple-element.14), channel_id=1, source_target_pairs={{0,4},{4,8},{8,12},{12,0},{1,5},{5,9},{9,13},{13,1},{2,6},{6,10},{... | collective-permute-start | bytes 294920 | tf_op jit(solution)/shard_map/ppermute | solution.py:42
  157.2 1.3 collective-permute-start.26
  158.5 4.3 %collective-permute-start.27 = (f32[64,256]{1,0:T(8,128)S(1)}, f32[64,256]{1,0:T(8,128)S(1)}, u32[]{:S(2)}, u32[]{:S(2)}) collective-permute-start(f32[64,256]{1,0:T(8,128)S(1)} %fusion.29), channel_id=1, source_target_pairs={{0,2},{2,0},{1,3},{3,1},{4,6},{6,4},{5,7},{7,5},{8,10},{10,8},{9,1... | collective-permute-start | bytes 196616 | tf_op jit(solution)/shard_map/ppermute | solution.py:59

commit v3 on v2

--- a/solution.py
+++ b/solution.py
@@ -173,7 +173,7 @@
         out_ref[at, :] = (came + jnp.where(s_ref[3] > 0, term, 0.0)).astype(BF16)
 
 
-def payload(scalars, got, parts, hidden, rows_at, after):
+def payload(scalars, got, parts, hidden, rows_at, *after):
     part, hid = got[0].shape
     rows = part * parts
     step = block_of(hid, 1792)
@@ -185,7 +185,7 @@
             pl.BlockSpec((1, rows, step), lambda i, s, j=j: (s[j], rows_at[j] // rows, i))
             for j in range(len(hidden))
         ]
-        + [ANYWHERE],
+        + [ANYWHERE] * len(after),
         out_specs=pl.BlockSpec((rows, step), lambda i, s: (0, i)),
     )
 
@@ -199,7 +199,7 @@
         compiler_params=pltpu.CompilerParams(vmem_limit_bytes=PAYLOAD_LIMIT << 20),
         cost_estimate=SHORT,
         name="payload",
-    )(scalars, *got, *hidden, after)
+    )(scalars, *got, *hidden, *after)
 
 
 def first_kernel(n, cores, s_ref, own_gate, proj, *refs):
@@ -264,10 +264,12 @@
 
 def inputs_kernel(x_ref, proj_ref, after_ref, out_ref):
     del after_ref
-    out_ref[...] = jnp.dot(x_ref[...], proj_ref[...], preferred_element_type=F32)
-
-
-def projected_inputs(inputs, proj_in, after):
+    out_ref[...] = lax.dot_general(
+        x_ref[...], proj_ref[...], ROWS_ROWS, preferred_element_type=F32
+    )
+
+
+def projected_inputs(inputs, proj_t, after):
     whole = pl.BlockSpec(memory_space=pltpu.VMEM)
     return pl.pallas_call(
         inputs_kernel,
@@ -277,7 +279,7 @@
         compiler_params=pltpu.CompilerParams(vmem_limit_bytes=12 << 20),
         cost_estimate=cost(1),
         name="projected_inputs",
-    )(inputs, proj_in, after)
+    )(inputs, proj_t, after)
 
 
 def local(grad_out, inputs, gate_act, w_down, proj_in, proj_out, queries, example_of):
@@ -331,8 +333,21 @@
         last = hidden_grad(spreads[p], w_down, half, half, last)
         second[p] = (last, 0)
     for p in later:
-        whole[p] = whole_of(features_of[p], [last])
-    last, middle = whole[later[0]], None
+        whole[p] = whole_of(features_of[p], [last] + came[-1][0])
+    last, all_q = [whole[later[0]]], None
+
+    width = R * R // cores
+
+    def all_queries(after):
+        own_q = block_copy(queries[0], 0 * z, 0 * z, queries.shape[1:], after)
+        own_q = own_q.reshape(cores, -1, width)
+        got_q = [lax.dynamic_index_in_dim(own_q, core, 0, keepdims=False)]
+        for e in range(1, cores):
+            got_q.append(
+                shifted(lax.dynamic_index_in_dim(own_q, (core + e) % cores, 0, keepdims=False), "sub", e)
+            )
+        own_q = jnp.concatenate([lax.select_n((core - i) % cores, *got_q) for i in range(cores)], axis=1)
+        return gathered(own_q, "blk")
 
     def counts(rightward):
         return jnp.where(rightward, z > 0, z < n - 1)
@@ -361,34 +376,24 @@
                     got = [stream[-1][int(reverse)] for stream in streams]
                 rows_at = [start + c * part * len(streams) for _, start in arrays]
                 arrays = [array for array, _ in arrays]
-                last = payload(scalars, got, len(streams), arrays, rows_at, last)
-                both.append(onward(last, reverse))
+                last = payload(scalars, got, len(streams), arrays, rows_at, *last)
+                last = [last]
+                both.append(onward(last[0], reverse))
             sent.append(both)
         if s < n - 1:
             for stream, both in zip(came, sent, strict=True):
                 stream.append(both)
         if s == n - 2:
-            middle = last
+            all_q = all_queries(last[0])
         for p in needed(s + 1):
             if p not in second:
                 spreads[p] = spread(whole[p])
-                first[p] = last = hidden_grad(spreads[p], w_down, 0, tok, last)
-                second[p] = (last, half)
+                first[p] = hidden_grad(spreads[p], w_down, 0, tok, last[0])
+                last, second[p] = [first[p]], (first[p], half)
         if s == n - 2:
             for p in begin:
-                first[p] = last = hidden_grad(spreads[p], w_down, 0, half, last)
-
-    width = R * R // cores
-    own_q = block_copy(queries[0], 0 * z, 0 * z, queries.shape[1:], middle)
-    own_q = own_q.reshape(cores, -1, width)
-    got_q = [lax.dynamic_index_in_dim(own_q, core, 0, keepdims=False)]
-    for e in range(1, cores):
-        got_q.append(
-            shifted(lax.dynamic_index_in_dim(own_q, (core + e) % cores, 0, keepdims=False), "sub", e)
-        )
-    own_q = jnp.concatenate([lax.select_n((core - i) % cores, *got_q) for i in range(cores)], axis=1)
-    n_q = own_q.shape[0]
-    flat_q = own_q.astype(F32).reshape(-1, half)
+                first[p] = hidden_grad(spreads[p], w_down, 0, half, last[0])
+                last = [first[p]]
 
     gates = [came[c][s][d] for s in range(n - 1) for d in (0, 1) for c in range(CHUNKS)]
     scalars = [block_at(k) for k in range(n)] + [even] + [z >= k for k in range(1, n)]
@@ -401,16 +406,11 @@
         proj_out.T,
         gates,
         [first[p] for p in range(group)],
-        last,
+        last[0],
     )
     up_first = ups[0]
-    got_q = [flat_q]
     for k in range(1, n):
-        got = shifted(jnp.concatenate([ups[k], flat_q]), "blk", -k)
-        up_first = up_first + got[:R]
-        got_q.append(got[R:])
-    all_q = jnp.stack([lax.select_n((i - z) % n, *got_q) for i in range(n)])
-    all_q = all_q.reshape(n, n_q, R * R).astype(BF16)
+        up_first = up_first + shifted(ups[k], "blk", -k)
 
     own_second = lax.dynamic_index_in_dim(second[0][0], block_at(0), 0, keepdims=False)[second[0][1] :]
     total = own_second + sum(
@@ -425,7 +425,7 @@
     )
     up_proj = summed(jnp.concatenate([up_first, up_second], axis=1), ("sub", "fsdp"))
 
-    left_proj = summed(projected_inputs(inputs, proj_in, middle), ("sub", "fsdp"))
+    left_proj = summed(projected_inputs(inputs, proj_in.T, ups), ("sub", "fsdp"))
     onehot = (example_of[:, None] == jnp.arange(EX_DEV, dtype=jnp.int32)[None, :]).astype(F32)
     weighted = (onehot[:, :, None] * left_proj[:, None, :]).reshape(tok, EX_DEV * R)
     full_sketch = lax.dot_general(

time: 166 us -> 154 us (0.928)
  waiting for transfers between devices: 53.6 us -> 40.7 us
  starting transfers between devices: 32.8 us -> 37.4 us
  local copies, waits for them, and re-layouts: 14.4 us -> 12.6 us
    ppermute x8 -> x11, waiting for transfers between devices: 18.9 us -> 6.84 us  [shifted(): lax.ppermute(block, axis, [(i, (i + distance) % n) for i in range(n)])]
    ppermute x8 -> x11, starting transfers between devices: 6.44 us -> 12.4 us  [shifted(): lax.ppermute(block, axis, [(i, (i + distance) % n) for i in range(n)])]
    pallas_call x10, Pallas kernels: 15.9 us -> 14.2 us  [payload(): pl.pallas_call(kernel, grid_spec=grid_spec, out_shape=jax.ShapeDtypeStruc...]
    unnamed x53 -> x58, local copies, waits for them, and re-layouts: 8.36 us -> 7.16 us
  transfers between devices with their start and end apart: 28 -> 31, of which waited for: 11 -> 10; matrix products, arithmetic and copies ran while one was open for 22% -> 23% of each run, Pallas kernels for 17% -> 18%
where the time goes in v3:
time: 154 us; the launch traced here: 153 us
  waiting for transfers between devices  40.7 us (26%)
  starting transfers between devices  37.4 us (24%)
  matrix products  30.3 us (20%)
  Pallas kernels  27.1 us (18%)
  local copies, waits for them, and re-layouts  12.6 us (8%)
  other arithmetic  3.6 us (2%)
  between operations  1.56 us (1%)
    dot_general x3, matrix products, hidden_grad(): lax.dot_general(stacked.reshape(-1, depth), w_down, ROWS_ROWS, preferred_...  26.3 us
    pallas_call x10, Pallas kernels, payload(): pl.pallas_call(kernel, grid_spec=grid_spec, out_shape=jax.ShapeDtypeStruc...  14.2 us
    ppermute x11, starting transfers between devices, shifted(): lax.ppermute(block, axis, [(i, (i + distance) % n) for i in range(n)])  12.4 us
    ppermute x10, starting transfers between devices, onward(): return lax.ppermute(block, ('blk', 'fsdp'), route)  10.9 us
    pallas_call x1, Pallas kernels, projected_first(): pl.pallas_call(kernel, grid_spec=grid_spec, out_shape=jax.ShapeDtypeStruc...  10.3 us
    ppermute x2, waiting for transfers between devices, features(): return lax.ppermute(mine, ('blk', 'sub'), route)  10.1 us
    ppermute x2, waiting for transfers between devices, line_left(): return lax.ppermute(block, 'blk', [(i + 1, i) for i in range(n - 1)])  9.88 us
    ppermute x2, waiting for transfers between devices, line_right(): return lax.ppermute(block, 'blk', [(i, i + 1) for i in range(n - 1)])  8.8 us
  transfers between devices with their start and end apart: 31, of which 10 were waited for; matrix products, arithmetic and copies ran while one was open for 23% of the time, Pallas kernels for 18%

profile of v3, /device:TPU:0, one launch (start us, length us, event | category | flops | bytes accessed | tf_op | source)
XLA Modules:
  0.0 153.2 jit_solution(8223890588148312260)
XLA Ops:
  0.7 1.4 fusion.33
  2.1 3.1 %collective-permute-start.4 = (bf16[128,2048]{1,0:T(8,128)(2,1)S(1)}, bf16[128,2048]{1,0:T(8,128)(2,1)S(1)}, u32[]{:S(2)}, u32[]{:S(2)}) collective-permute-start(bf16[128,2048]{1,0:T(8,128)(2,1)S(1)} %get-tuple-element.3), channel_id=1, source_target_pairs={{0,4},{1,12},{4,0},{5,8},{8,5},{9,13},{12,1},{13,9},{2,6},{3,14},{... | collective-permute-start | bytes 1572872 | tf_op jit(solution)/shard_map/ppermute | solution.py:303
  5.2 0.7 collective-permute-start.6
  5.9 10.1 %collective-permute-done.4.refs_1_ = bf16[128,2048]{1,0:T(8,128)(2,1)S(1)} collective-permute-done((bf16[128,2048]{1,0:T(8,128)(2,1)S(1)}, bf16[128,2048]{1,0:T(8,128)(2,1)S(1)}, u32[]{:S(2)}, u32[]{:S(2)}) %collective-permute-start.4) | collective-permute-done | bytes 524320 | tf_op jit(solution)/shard_map/ppermute | solution.py:303
  16.0 2.4 %collective-permute-start.5 = (bf16[128,2048]{1,0:T(8,128)(2,1)S(1)}, bf16[128,2048]{1,0:T(8,128)(2,1)S(1)}, u32[]{:S(2)}, u32[]{:S(2)}) collective-permute-start(bf16[128,2048]{1,0:T(8,128)(2,1)S(1)} %collective-permute-done.4.refs_1_), channel_id=1, source_target_pairs={{0,2},{2,0},{1,3},{3,1},{4,6},{6,4},{5,7},{7,5},{8,10},{10,8},{9,1... | collective-permute-start | bytes 1572872 | tf_op jit(solution)/shard_map/ppermute | solution.py:42
  18.3 0.9 fusion.34
  19.2 3.7 %collective-permute-start = (bf16[64,3584]{1,0:T(8,128)(2,1)S(1)}, bf16[64,3584]{1,0:T(8,128)(2,1)S(1)}, u32[]{:S(2)}, u32[]{:S(2)}) collective-permute-start(bf16[64,3584]{1,0:T(8,128)(2,1)S(1)} %get-tuple-element.5), channel_id=1, source_target_pairs={{0,4},{4,8},{8,12},{1,5},{5,9},{9,13},{2,6},{6,10},{10,14},{3,7},{... | collective-permute-start | bytes 1376264 | tf_op jit(solution)/shard_map/ppermute | solution.py:22
  22.9 1.3 collective-permute-start.2
  24.2 8.8 %collective-permute-done.refs_3_.refs_1_ = bf16[64,3584]{1,0:T(8,128)(2,1)S(1)} collective-permute-done((bf16[64,3584]{1,0:T(8,128)(2,1)S(1)}, bf16[64,3584]{1,0:T(8,128)(2,1)S(1)}, u32[]{:S(2)}, u32[]{:S(2)}) %collective-permute-start) | collective-permute-done | bytes 458784 | tf_op jit(solution)/shard_map/ppermute | solution.py:22
  33.0 7.0 %collective-permute-done.2.refs_4_.refs_2_.refs_5_ = bf16[64,3584]{1,0:T(8,128)(2,1)S(1)} collective-permute-done((bf16[64,3584]{1,0:T(8,128)(2,1)S(1)}, bf16[64,3584]{1,0:T(8,128)(2,1)S(1)}, u32[]{:S(2)}, u32[]{:S(2)}) %collective-permute-start.2) | collective-permute-done | bytes 458784 | tf_op jit(solution)/shard_map/ppermute | solution.py:27
  40.2 0.6 copy-done.9
  40.8 2.5 %collective-permute-start.1 = (bf16[64,3584]{1,0:T(8,128)(2,1)}, bf16[64,3584]{1,0:T(8,128)(2,1)S(1)}, u32[]{:S(2)}, u32[]{:S(2)}) collective-permute-start(bf16[64,3584]{1,0:T(8,128)(2,1)} %get-tuple-element.4), channel_id=1, source_target_pairs={{0,4},{4,8},{8,12},{1,5},{5,9},{9,13},{2,6},{6,10},{10,14},{3,7},{... | collective-permute-start | bytes 1376264 | tf_op jit(solution)/shard_map/ppermute | solution.py:22
  43.3 1.3 collective-permute-start.3
  44.6 1.6 %collective-permute-start.8 = (bf16[128,2048]{1,0:T(8,128)(2,1)S(1)}, bf16[128,2048]{1,0:T(8,128)(2,1)S(1)}, u32[]{:S(2)}, u32[]{:S(2)}) collective-permute-start(bf16[128,2048]{1,0:T(8,128)(2,1)S(1)} %collective-permute-done.6.refs_5_.refs_1_), channel_id=1, source_target_pairs={{0,2},{2,0},{1,3},{3,1},{4,6},{6,4},{5,7},{7,5},{8,10},{10,8},{9,1... | collective-permute-start | bytes 1572872 | tf_op jit(solution)/shard_map/ppermute | solution.py:42
  46.2 1.0 copy-done.11
  47.2 7.3 %fusion.4.refs_3_ = f32[2,128,3584]{2,1,0:T(8,128)S(1)} fusion(bf16[2,128,2048]{2,1,0:T(8,128)(2,1)S(1)} %stack.249, bf16[3584,2048]{1,0:T(8,128)(2,1)} %param.11), kind=kOutput, calls=%fused_computation.4 | convolution fusion | flops 3758096384 | bytes 19398656 | tf_op jit(solution)/shard_map/dot_general | solution.py:101
  54.6 2.8 %collective-permute-done.3.refs_5_.refs_2_.refs_6_ = bf16[64,3584]{1,0:T(8,128)(2,1)S(1)} collective-permute-done((bf16[64,3584]{1,0:T(8,128)(2,1)}, bf16[64,3584]{1,0:T(8,128)(2,1)S(1)}, u32[]{:S(2)}, u32[]{:S(2)}) %collective-permute-start.3) | collective-permute-done | bytes 458784 | tf_op jit(solution)/shard_map/ppermute | solution.py:27
  57.4 0.7 collective-permute-done.8.refs_2_
  59.2 0.6 stack.199.refs_0_
  59.8 2.0 %copy-done.2 = f32[2,128,3584]{2,1,0:T(8,128)S(1)} copy-done((f32[2,128,3584]{2,1,0:T(8,128)S(1)}, f32[2,128,3584]{2,1,0:T(8,128)}, u32[]{:S(2)}) %copy-start.2) | copy-done | bytes 3670040
  61.8 1.0 copy-done.10
  62.8 0.9 payload.10.refs_4_
  63.7 2.4 %collective-permute-start.9 = (bf16[64,3584]{1,0:T(8,128)(2,1)S(1)}, bf16[64,3584]{1,0:T(8,128)(2,1)S(1)}, u32[]{:S(2)}, u32[]{:S(2)}) collective-permute-start(bf16[64,3584]{1,0:T(8,128)(2,1)S(1)} %payload.10.refs_4_), channel_id=1, source_target_pairs={{0,4},{2,0},{4,8},{6,2},{8,12},{10,6},{12,14},{14,10},{1,5},{3,1},... | collective-permute-start | bytes 1376264 | tf_op jit(solution)/shard_map/ppermute | solution.py:37
  66.2 0.9 payload.11.refs_4_
  67.1 0.9 payload.12.refs_4_
  68.1 2.1 %collective-permute-start.10 = (bf16[64,3584]{1,0:T(8,128)(2,1)S(1)}, bf16[64,3584]{1,0:T(8,128)(2,1)S(1)}, u32[]{:S(2)}, u32[]{:S(2)}) collective-permute-start(bf16[64,3584]{1,0:T(8,128)(2,1)S(1)} %payload.12.refs_4_), channel_id=1, source_target_pairs={{0,4},{2,0},{4,8},{6,2},{8,12},{10,6},{12,14},{14,10},{1,5},{3,1},... | collective-permute-start | bytes 1376264 | tf_op jit(solution)/shard_map/ppermute | solution.py:37
  70.1 0.9 payload.13.refs_2_
  71.1 1.4 stack.250
  72.5 11.3 %fusion.2.refs_2_.refs_3_.refs_15_ = f32[2,256,3584]{2,1,0:T(8,128)S(1)} fusion(bf16[2,256,2048]{2,1,0:T(8,128)(2,1)S(1)} %stack.250, bf16[3584,2048]{1,0:T(8,128)(2,1)} %param.11), kind=kOutput, calls=%fused_computation.2 | convolution fusion | flops 7516192768 | bytes 24117248 | tf_op jit(solution)/shard_map/dot_general | solution.py:101
  83.8 2.0 %payload.14.refs_3_ = bf16[64,3584]{1,0:T(8,128)(2,1)} custom-call(s32[5]{0:T(128)S(1)} %stack.218.refs_0_, bf16[64,3584]{1,0:T(8,128)(2,1)S(1)} %collective-permute-done.9.refs_1_.refs_7_, f32[2,256,3584]{2,1,0:T(8,128)S(1)} %fusion.2.refs_2_.refs_3_.refs_15_, f32[2,256,3584]{2,1,0:T(8,128)S(1)} %fusion.2.refs_2_.refs_3_.refs_15_), custom_call_target="tpu_custom_call" | custom-call | flops 1000 | bytes 1000 | tf_op jit(solution)/shard_map/payload/pallas_call | solution.py:195
  85.8 2.0 %collective-permute-start.14 = (bf16[64,3584]{1,0:T(8,128)(2,1)}, bf16[64,3584]{1,0:T(8,128)(2,1)}, u32[]{:S(2)}, u32[]{:S(2)}) collective-permute-start(bf16[64,3584]{1,0:T(8,128)(2,1)} %payload.14.refs_3_), channel_id=1, source_target_pairs={{0,4},{2,0},{4,8},{6,2},{8,12},{10,6},{12,14},{14,10},{1,5},{3,1},... | collective-permute-start | bytes 1376264 | tf_op jit(solution)/shard_map/ppermute | solution.py:37
  87.9 1.5 %payload.15.refs_3_ = bf16[64,3584]{1,0:T(8,128)(2,1)} custom-call(s32[5]{0:T(128)S(1)} %stack.221.refs_0_, bf16[64,3584]{1,0:T(8,128)(2,1)S(1)} %collective-permute-done.11.refs_1_.refs_9_, f32[2,256,3584]{2,1,0:T(8,128)S(1)} %fusion.2.refs_2_.refs_3_.refs_15_, bf16[64,3584]{1,0:T(8,128)(2,1)} %payload.14.refs_3_), custom_call_target="tpu_custom_call" | custom-call | flops 1000 | bytes 1000 | tf_op jit(solution)/shard_map/payload/pallas_call | solution.py:195
  89.4 1.5 payload.16.refs_3_
  91.0 2.0 %collective-permute-start.15 = (bf16[64,3584]{1,0:T(8,128)(2,1)}, bf16[64,3584]{1,0:T(8,128)(2,1)}, u32[]{:S(2)}, u32[]{:S(2)}) collective-permute-start(bf16[64,3584]{1,0:T(8,128)(2,1)} %payload.16.refs_3_), channel_id=1, source_target_pairs={{0,4},{2,0},{4,8},{6,2},{8,12},{10,6},{12,14},{14,10},{1,5},{3,1},... | collective-permute-start | bytes 1376264 | tf_op jit(solution)/shard_map/ppermute | solution.py:37
  93.0 0.9 payload.17.refs_2_.after_ref
  94.0 0.6 block_copy.1
  95.3 1.0 copy-done.20
  96.3 7.7 %fusion.refs_4_.refs_16_ = f32[2,128,3584]{2,1,0:T(8,128)S(1)} fusion(bf16[2,128,2048]{2,1,0:T(8,128)(2,1)} %copy-done.20, bf16[3584,2048]{1,0:T(8,128)(2,1)} %param.11), kind=kOutput, calls=%fused_computation | convolution fusion | flops 3758096384 | bytes 19398656 | tf_op jit(solution)/shard_map/dot_general | solution.py:101
  104.0 0.8 bitcast_select_fusion.1
  104.9 1.0 pad_maximum_fusion.3
  105.8 2.0 %collective-permute-start.28 = (bf16[4,4096]{1,0:T(4,128)(2,1)}, bf16[4,4096]{1,0:T(4,128)(2,1)}, u32[]{:S(2)}, u32[]{:S(2)}) collective-permute-start(bf16[4,4096]{1,0:T(4,128)(2,1)} %pad_maximum_fusion.3), channel_id=1, source_target_pairs={{0,4},{4,8},{8,12},{12,0},{1,5},{5,9},{9,13},{13,1},{2,6},{6,10},{... | collective-permute-start | bytes 98312 | tf_op jit(solution)/shard_map/ppermute | solution.py:42
  107.8 2.4 %collective-permute-start.29 = (bf16[4,4096]{1,0:T(4,128)(2,1)}, bf16[4,4096]{1,0:T(4,128)(2,1)}, u32[]{:S(2)}, u32[]{:S(2)}) collective-permute-start(bf16[4,4096]{1,0:T(4,128)(2,1)} %pad_maximum_fusion.3), channel_id=1, source_target_pairs={{0,8},{4,12},{8,0},{12,4},{1,9},{5,13},{9,1},{13,5},{2,10},{6,14},... | collective-permute-start | bytes 98312 | tf_op jit(solution)/shard_map/ppermute | solution.py:42
  110.2 1.5 %collective-permute-start.30 = (bf16[4,4096]{1,0:T(4,128)(2,1)}, bf16[4,4096]{1,0:T(4,128)(2,1)}, u32[]{:S(2)}, u32[]{:S(2)}) collective-permute-start(bf16[4,4096]{1,0:T(4,128)(2,1)} %pad_maximum_fusion.3), channel_id=1, source_target_pairs={{0,12},{4,0},{8,4},{12,8},{1,13},{5,1},{9,5},{13,9},{2,14},{6,2},{... | collective-permute-start | bytes 98312 | tf_op jit(solution)/shard_map/ppermute | solution.py:42
  111.8 2.8 %payload.18.refs_4_ = bf16[128,3584]{1,0:T(8,128)(2,1)} custom-call(s32[5]{0:T(128)S(1)} %stack.229.refs_0_, bf16[64,3584]{1,0:T(8,128)(2,1)} %collective-permute-done.14.refs_1_.refs_11_, bf16[64,3584]{1,0:T(8,128)(2,1)} %collective-permute-done.15.refs_2_.refs_12_, f32[2,128,3584]{2,1,0:T(8,128)S(1)} %copy-done.4, f32[2,128,3584]{2,1,0:T(8,128)S(1)} %fusion.refs_4_.refs_16_), custom_call_target="tpu_custom_call" | custom-call | flops 1000 | bytes 1000 | tf_op jit(solution)/shard_map/payload/pallas_call | solution.py:195
  114.6 0.5 collective-permute-start.23
  115.1 1.8 %payload.19.refs_17_ = bf16[128,3584]{1,0:T(8,128)(2,1)S(1)} custom-call(s32[5]{0:T(128)S(1)} %stack.225.refs_0_, bf16[64,3584]{1,0:T(8,128)(2,1)S(1)} %collective-permute-done.16.refs_1_.refs_13_, bf16[64,3584]{1,0:T(8,128)(2,1)} %collective-permute-done.17.refs_2_.refs_14_, f32[2,128,3584]{2,1,0:T(8,128)S(1)} %copy-done.4, bf16[128,3584]{1,0:T(8,128)(2,1)} %payload.18.refs_4_), custom_call_target="tpu_custom_call" | custom-call | flops 1000 | bytes 1000 | tf_op jit(solution)/shard_map/payload/pallas_call | solution.py:195
  117.0 1.6 %collective-permute-start.24 = (bf16[128,3584]{1,0:T(8,128)(2,1)S(1)}, bf16[128,3584]{1,0:T(8,128)(2,1)S(1)}, u32[]{:S(2)}, u32[]{:S(2)}) collective-permute-start(bf16[128,3584]{1,0:T(8,128)(2,1)S(1)} %payload.19.refs_17_), channel_id=1, source_target_pairs={{0,2},{2,6},{4,0},{6,10},{8,4},{10,14},{12,8},{14,12},{1,3},{3,7},... | collective-permute-start | bytes 2752520 | tf_op jit(solution)/shard_map/ppermute | solution.py:37
  118.6 10.3 %projected_first.1.after_ref = f32[4,64,128]{2,1,0:T(8,128)} custom-call(s32[8]{0:T(128)} %stack.199.refs_0_, bf16[256,3584]{1,0:T(8,128)(2,1)} %refs_1_.1, bf16[64,3584]{1,0:T(8,128)(2,1)} %bitcast.81, bf16[64,3584]{1,0:T(8,128)(2,1)} %copy-done.8, bf16[64,3584]{1,0:T(8,128)(2,1)} %copy-done.6, bf16[64,3584]{1,0:T(8,128)(2,1)} %copy-done.9, ...), custom_call_target="tpu_custom_call" | custom-call | flops 1000 | bytes 59040000 | tf_op jit(solution)/shard_map/projected_first/pallas_call | solution.py:255
  128.9 0.8 slice_bitcast_fusion.2
  129.7 0.8 collective-permute-start.20
  130.5 1.2 collective-permute-start.21
  132.0 0.9 select_bitcast_fusion.3
  132.9 0.9 copy-done.19
  134.2 4.9 %collective-permute-done.20 = f32[64,128]{1,0:T(8,128)S(1)} collective-permute-done((f32[64,128]{1,0:T(8,128)S(1)}, f32[64,128]{1,0:T(8,128)S(1)}, u32[]{:S(2)}, u32[]{:S(2)}) %collective-permute-start.20) | collective-permute-done | bytes 32800 | tf_op jit(solution)/shard_map/ppermute | solution.py:42
  139.2 1.2 collective-permute-done.21
  140.5 0.8 collective-permute-start.19
  141.3 2.5 %fusion.16 = f32[64,128]{1,0:T(8,128)S(1)} fusion(bf16[3584,64]{0,1:T(8,128)(2,1)S(1)} %copy-done.27, f32[2,256,3584]{2,1,0:T(8,128)} %copy-done, s32[]{:T(128)S(6)} %select_n.436, s32[]{:T(128)S(6)} %add.202, bf16[128,3584]{1,0:T(8,128)(2,1)S(1)} %collective-permute-done.24, bf16[128,3584]{1,0:T(8,128)(2,1)S(1)} %collective-permute-done.23, ...), kind=kOutput, calls=%fused_computation.17 | convolution fusion | flops 179830784 | bytes 5079050 | tf_op jit(solution)/shard_map/dot_general | solution.py:419
  143.9 0.8 select_bitcast_fusion.2
  144.8 1.4 collective-permute-done.19
  146.3 0.8 collective-permute-start.26
  147.1 3.5 %collective-permute-done.26 = f32[64,256]{1,0:T(8,128)S(1)} collective-permute-done((f32[64,256]{1,0:T(8,128)S(1)}, f32[64,256]{1,0:T(8,128)S(1)}, u32[]{:S(2)}, u32[]{:S(2)}) %collective-permute-start.26) | collective-permute-done | bytes 65568 | tf_op jit(solution)/shard_map/ppermute | solution.py:59
  150.6 0.6 convolution_convert_fusion
  151.8 0.6 constant_dynamic-slice_fusion
  152.4 0.8 fusion.23
  (109 shorter events, 3.5 us)
Async XLA Ops:
  0.6 17.7 %copy-start.25 = (bf16[256,3584]{1,0:T(8,128)(2,1)S(1)}, bf16[256,3584]{1,0:T(8,128)(2,1)}, u32[]{:S(2)}) copy-start(bf16[256,3584]{1,0:T(8,128)(2,1)} %refs_1_.1) | copy-start | bytes 5505028
  2.1 13.9 %collective-permute-start.4 = (bf16[128,2048]{1,0:T(8,128)(2,1)S(1)}, bf16[128,2048]{1,0:T(8,128)(2,1)S(1)}, u32[]{:S(2)}, u32[]{:S(2)}) collective-permute-start(bf16[128,2048]{1,0:T(8,128)(2,1)S(1)} %get-tuple-element.3), channel_id=1, source_target_pairs={{0,4},{1,12},{4,0},{5,8},{8,5},{9,13},{12,1},{13,9},{2,6},{3,14},{... | collective-permute-start | bytes 1572872 | tf_op jit(solution)/shard_map/ppermute | solution.py:303
  5.2 34.9 %collective-permute-start.6 = (bf16[128,2048]{1,0:T(8,128)(2,1)S(1)}, bf16[128,2048]{1,0:T(8,128)(2,1)S(1)}, u32[]{:S(2)}, u32[]{:S(2)}) collective-permute-start(bf16[128,2048]{1,0:T(8,128)(2,1)S(1)} %get-tuple-element.2), channel_id=1, source_target_pairs={{0,0},{1,8},{4,4},{5,12},{8,1},{9,9},{12,5},{13,13},{2,2},{3,10},{... | collective-permute-start | bytes 1572872 | tf_op jit(solution)/shard_map/ppermute | solution.py:303
  16.0 24.1 %collective-permute-start.5 = (bf16[128,2048]{1,0:T(8,128)(2,1)S(1)}, bf16[128,2048]{1,0:T(8,128)(2,1)S(1)}, u32[]{:S(2)}, u32[]{:S(2)}) collective-permute-start(bf16[128,2048]{1,0:T(8,128)(2,1)S(1)} %collective-permute-done.4.refs_1_), channel_id=1, source_target_pairs={{0,2},{2,0},{1,3},{3,1},{4,6},{6,4},{5,7},{7,5},{8,10},{10,8},{9,1... | collective-permute-start | bytes 1572872 | tf_op jit(solution)/shard_map/ppermute | solution.py:42
  19.2 26.9 %copy-start.24 = (s32[256]{0:T(256)S(1)}, s32[256]{0:T(256)}, u32[]{:S(2)}) copy-start(s32[256]{0:T(256)} %refs_2_.1) | copy-start | bytes 3076
  19.2 13.8 %collective-permute-start = (bf16[64,3584]{1,0:T(8,128)(2,1)S(1)}, bf16[64,3584]{1,0:T(8,128)(2,1)S(1)}, u32[]{:S(2)}, u32[]{:S(2)}) collective-permute-start(bf16[64,3584]{1,0:T(8,128)(2,1)S(1)} %get-tuple-element.5), channel_id=1, source_target_pairs={{0,4},{4,8},{8,12},{1,5},{5,9},{9,13},{2,6},{6,10},{10,14},{3,7},{... | collective-permute-start | bytes 1376264 | tf_op jit(solution)/shard_map/ppermute | solution.py:22
  22.9 17.1 %collective-permute-start.2 = (bf16[64,3584]{1,0:T(8,128)(2,1)S(1)}, bf16[64,3584]{1,0:T(8,128)(2,1)S(1)}, u32[]{:S(2)}, u32[]{:S(2)}) collective-permute-start(bf16[64,3584]{1,0:T(8,128)(2,1)S(1)} %get-tuple-element.5), channel_id=1, source_target_pairs={{4,0},{8,4},{12,8},{5,1},{9,5},{13,9},{6,2},{10,6},{14,10},{7,3},{... | collective-permute-start | bytes 1376264 | tf_op jit(solution)/shard_map/ppermute | solution.py:27
  33.0 33.2 %copy-start.8 = (bf16[64,3584]{1,0:T(8,128)(2,1)}, bf16[64,3584]{1,0:T(8,128)(2,1)S(1)}, u32[]{:S(2)}) copy-start(bf16[64,3584]{1,0:T(8,128)(2,1)S(1)} %collective-permute-done.refs_3_.refs_1_) | copy-start | bytes 1376260
  40.0 0.8 copy-start.9
  40.1 6.0 %collective-permute-start.7 = (bf16[256,2048]{1,0:T(8,128)(2,1)S(1)}, bf16[256,2048]{1,0:T(8,128)(2,1)S(1)}, u32[]{:S(2)}, u32[]{:S(2)}) collective-permute-start(bf16[256,2048]{1,0:T(8,128)(2,1)S(1)} %join.2.refs_0_), channel_id=1, source_target_pairs={{0,1},{1,0},{2,3},{3,2},{4,5},{5,4},{6,7},{7,6},{8,9},{9,8},{10,11... | collective-permute-start | bytes 3145736 | tf_op jit(solution)/shard_map/ppermute | solution.py:42
  40.8 13.8 %collective-permute-start.1 = (bf16[64,3584]{1,0:T(8,128)(2,1)}, bf16[64,3584]{1,0:T(8,128)(2,1)S(1)}, u32[]{:S(2)}, u32[]{:S(2)}) collective-permute-start(bf16[64,3584]{1,0:T(8,128)(2,1)} %get-tuple-element.4), channel_id=1, source_target_pairs={{0,4},{4,8},{8,12},{1,5},{5,9},{9,13},{2,6},{6,10},{10,14},{3,7},{... | collective-permute-start | bytes 1376264 | tf_op jit(solution)/shard_map/ppermute | solution.py:22
  43.3 14.1 %collective-permute-start.3 = (bf16[64,3584]{1,0:T(8,128)(2,1)}, bf16[64,3584]{1,0:T(8,128)(2,1)S(1)}, u32[]{:S(2)}, u32[]{:S(2)}) collective-permute-start(bf16[64,3584]{1,0:T(8,128)(2,1)} %get-tuple-element.4), channel_id=1, source_target_pairs={{4,0},{8,4},{12,8},{5,1},{9,5},{13,9},{6,2},{10,6},{14,10},{7,3},{... | collective-permute-start | bytes 1376264 | tf_op jit(solution)/shard_map/ppermute | solution.py:27
  44.6 13.5 %collective-permute-start.8 = (bf16[128,2048]{1,0:T(8,128)(2,1)S(1)}, bf16[128,2048]{1,0:T(8,128)(2,1)S(1)}, u32[]{:S(2)}, u32[]{:S(2)}) collective-permute-start(bf16[128,2048]{1,0:T(8,128)(2,1)S(1)} %collective-permute-done.6.refs_5_.refs_1_), channel_id=1, source_target_pairs={{0,2},{2,0},{1,3},{3,1},{4,6},{6,4},{5,7},{7,5},{8,10},{10,8},{9,1... | collective-permute-start | bytes 1572872 | tf_op jit(solution)/shard_map/ppermute | solution.py:42
  46.2 1.0 copy-start.11
  54.6 3.6 %copy-start.1 = (f32[2,128,3584]{2,1,0:T(8,128)}, f32[2,128,3584]{2,1,0:T(8,128)S(1)}, u32[]{:S(2)}) copy-start(f32[2,128,3584]{2,1,0:T(8,128)S(1)} %fusion.4.refs_3_) | copy-start | bytes 11010052
  54.6 15.5 %copy-start.6 = (bf16[64,3584]{1,0:T(8,128)(2,1)}, bf16[64,3584]{1,0:T(8,128)(2,1)S(1)}, u32[]{:S(2)}) copy-start(bf16[64,3584]{1,0:T(8,128)(2,1)S(1)} %collective-permute-done.1.refs_4_.refs_1_) | copy-start | bytes 1376260
  57.4 12.7 %copy-start.7 = (bf16[64,3584]{1,0:T(8,128)(2,1)}, bf16[64,3584]{1,0:T(8,128)(2,1)S(1)}, u32[]{:S(2)}) copy-start(bf16[64,3584]{1,0:T(8,128)(2,1)S(1)} %collective-permute-done.3.refs_5_.refs_2_.refs_6_) | copy-start | bytes 1376260
  58.2 12.9 %collective-permute-start.13 = (bf16[256,2048]{1,0:T(8,128)(2,1)S(1)}, bf16[256,2048]{1,0:T(8,128)(2,1)}, u32[]{:S(2)}, u32[]{:S(2)}) collective-permute-start(bf16[256,2048]{1,0:T(8,128)(2,1)S(1)} %join.3.refs_4_.refs_0_), channel_id=1, source_target_pairs={{0,1},{1,0},{2,3},{3,2},{4,5},{5,4},{6,7},{7,6},{8,9},{9,8},{10,11... | collective-permute-start | bytes 3145736 | tf_op jit(solution)/shard_map/ppermute | solution.py:42
  59.8 2.0 %copy-start.2 = (f32[2,128,3584]{2,1,0:T(8,128)S(1)}, f32[2,128,3584]{2,1,0:T(8,128)}, u32[]{:S(2)}) copy-start(f32[2,128,3584]{2,1,0:T(8,128)} %copy-done.1) | copy-start | bytes 11010052
  61.8 1.0 copy-start.10
  63.7 3.4 %copy-start.3 = (f32[2,128,3584]{2,1,0:T(8,128)S(1)}, f32[2,128,3584]{2,1,0:T(8,128)}, u32[]{:S(2)}) copy-start(f32[2,128,3584]{2,1,0:T(8,128)} %copy-done.1) | copy-start | bytes 11010052
  63.7 20.0 %collective-permute-start.9 = (bf16[64,3584]{1,0:T(8,128)(2,1)S(1)}, bf16[64,3584]{1,0:T(8,128)(2,1)S(1)}, u32[]{:S(2)}, u32[]{:S(2)}) collective-permute-start(bf16[64,3584]{1,0:T(8,128)(2,1)S(1)} %payload.10.refs_4_), channel_id=1, source_target_pairs={{0,4},{2,0},{4,8},{6,2},{8,12},{10,6},{12,14},{14,10},{1,5},{3,1},... | collective-permute-start | bytes 1376264 | tf_op jit(solution)/shard_map/ppermute | solution.py:37
  67.1 20.8 %collective-permute-start.11 = (bf16[64,3584]{1,0:T(8,128)(2,1)S(1)}, bf16[64,3584]{1,0:T(8,128)(2,1)S(1)}, u32[]{:S(2)}, u32[]{:S(2)}) collective-permute-start(bf16[64,3584]{1,0:T(8,128)(2,1)S(1)} %payload.11.refs_4_), channel_id=1, source_target_pairs={{0,2},{2,6},{4,0},{6,10},{8,4},{10,14},{12,8},{14,12},{1,3},{3,7},... | collective-permute-start | bytes 1376264 | tf_op jit(solution)/shard_map/ppermute | solution.py:37
  68.1 21.4 %collective-permute-start.10 = (bf16[64,3584]{1,0:T(8,128)(2,1)S(1)}, bf16[64,3584]{1,0:T(8,128)(2,1)S(1)}, u32[]{:S(2)}, u32[]{:S(2)}) collective-permute-start(bf16[64,3584]{1,0:T(8,128)(2,1)S(1)} %payload.12.refs_4_), channel_id=1, source_target_pairs={{0,4},{2,0},{4,8},{6,2},{8,12},{10,6},{12,14},{14,10},{1,5},{3,1},... | collective-permute-start | bytes 1376264 | tf_op jit(solution)/shard_map/ppermute | solution.py:37
  71.0 22.0 %collective-permute-start.12 = (bf16[64,3584]{1,0:T(8,128)(2,1)S(1)}, bf16[64,3584]{1,0:T(8,128)(2,1)S(1)}, u32[]{:S(2)}, u32[]{:S(2)}) collective-permute-start(bf16[64,3584]{1,0:T(8,128)(2,1)S(1)} %payload.13.refs_2_), channel_id=1, source_target_pairs={{0,2},{2,6},{4,0},{6,10},{8,4},{10,14},{12,8},{14,12},{1,3},{3,7},... | collective-permute-start | bytes 1376264 | tf_op jit(solution)/shard_map/ppermute | solution.py:37
  83.8 9.2 %copy-start = (f32[2,256,3584]{2,1,0:T(8,128)}, f32[2,256,3584]{2,1,0:T(8,128)S(1)}, u32[]{:S(2)}) copy-start(f32[2,256,3584]{2,1,0:T(8,128)S(1)} %fusion.2.refs_2_.refs_3_.refs_15_) | copy-start | bytes 22020100
  83.8 2.1 %copy-start.15 = (bf16[64,3584]{1,0:T(8,128)(2,1)}, bf16[64,3584]{1,0:T(8,128)(2,1)S(1)}, u32[]{:S(2)}) copy-start(bf16[64,3584]{1,0:T(8,128)(2,1)S(1)} %collective-permute-done.9.refs_1_.refs_7_) | copy-start | bytes 1376260
  85.8 24.4 %collective-permute-start.14 = (bf16[64,3584]{1,0:T(8,128)(2,1)}, bf16[64,3584]{1,0:T(8,128)(2,1)}, u32[]{:S(2)}, u32[]{:S(2)}) collective-permute-start(bf16[64,3584]{1,0:T(8,128)(2,1)} %payload.14.refs_3_), channel_id=1, source_target_pairs={{0,4},{2,0},{4,8},{6,2},{8,12},{10,6},{12,14},{14,10},{1,5},{3,1},... | collective-permute-start | bytes 1376264 | tf_op jit(solution)/shard_map/ppermute | solution.py:37
  87.9 1.5 %copy-start.16 = (bf16[64,3584]{1,0:T(8,128)(2,1)}, bf16[64,3584]{1,0:T(8,128)(2,1)S(1)}, u32[]{:S(2)}) copy-start(bf16[64,3584]{1,0:T(8,128)(2,1)S(1)} %collective-permute-done.11.refs_1_.refs_9_) | copy-start | bytes 1376260
  89.4 25.7 %collective-permute-start.16 = (bf16[64,3584]{1,0:T(8,128)(2,1)}, bf16[64,3584]{1,0:T(8,128)(2,1)S(1)}, u32[]{:S(2)}, u32[]{:S(2)}) collective-permute-start(bf16[64,3584]{1,0:T(8,128)(2,1)} %payload.15.refs_3_), channel_id=1, source_target_pairs={{0,2},{2,6},{4,0},{6,10},{8,4},{10,14},{12,8},{14,12},{1,3},{3,7},... | collective-permute-start | bytes 1376264 | tf_op jit(solution)/shard_map/ppermute | solution.py:37
  89.4 1.5 %copy-start.17 = (bf16[64,3584]{1,0:T(8,128)(2,1)}, bf16[64,3584]{1,0:T(8,128)(2,1)S(1)}, u32[]{:S(2)}) copy-start(bf16[64,3584]{1,0:T(8,128)(2,1)S(1)} %collective-permute-done.10.refs_1_.refs_8_) | copy-start | bytes 1376260
  91.0 3.0 %copy-start.23 = (bf16[1,8,2048]{2,1,0:T(8,128)(2,1)S(1)}, bf16[1,8,2048]{2,1,0:T(8,128)(2,1)}, u32[]{:S(2)}) copy-start(bf16[1,8,2048]{2,1,0:T(8,128)(2,1)} %param.14) | copy-start | bytes 98308
  91.0 4.2 %copy-start.12 = (bf16[256,2048]{1,0:T(8,128)(2,1)S(1)}, bf16[256,2048]{1,0:T(8,128)(2,1)}, u32[]{:S(2)}) copy-start(bf16[256,2048]{1,0:T(8,128)(2,1)} %copy-done.11) | copy-start | bytes 3145732
  91.0 16.9 %collective-permute-start.15 = (bf16[64,3584]{1,0:T(8,128)(2,1)}, bf16[64,3584]{1,0:T(8,128)(2,1)}, u32[]{:S(2)}, u32[]{:S(2)}) collective-permute-start(bf16[64,3584]{1,0:T(8,128)(2,1)} %payload.16.refs_3_), channel_id=1, source_target_pairs={{0,4},{2,0},{4,8},{6,2},{8,12},{10,6},{12,14},{14,10},{1,5},{3,1},... | collective-permute-start | bytes 1376264 | tf_op jit(solution)/shard_map/ppermute | solution.py:37
  93.0 0.9 copy-start.18
  93.9 20.7 %collective-permute-start.17 = (bf16[64,3584]{1,0:T(8,128)(2,1)S(1)}, bf16[64,3584]{1,0:T(8,128)(2,1)}, u32[]{:S(2)}, u32[]{:S(2)}) collective-permute-start(bf16[64,3584]{1,0:T(8,128)(2,1)S(1)} %payload.17.refs_2_.after_ref), channel_id=1, source_target_pairs={{0,2},{2,6},{4,0},{6,10},{8,4},{10,14},{12,8},{14,12},{1,3},{3,7},... | collective-permute-start | bytes 1376264 | tf_op jit(solution)/shard_map/ppermute | solution.py:37
  94.6 0.6 copy-start.28
  94.6 9.4 %collective-permute-start.27 = (bf16[4,2048]{1,0:T(4,128)(2,1)S(1)}, bf16[4,2048]{1,0:T(4,128)(2,1)}, u32[]{:S(2)}, u32[]{:S(2)}) collective-permute-start(bf16[4,2048]{1,0:T(4,128)(2,1)S(1)} %dynamic-slice_bitcast_fusion.1), channel_id=1, source_target_pairs={{0,1},{1,0},{2,3},{3,2},{4,5},{5,4},{6,7},{7,6},{8,9},{9,8},{10,11... | collective-permute-start | bytes 49160 | tf_op jit(solution)/shard_map/ppermute | solution.py:42
  95.3 1.0 copy-start.20
  96.3 15.5 %copy-start.4 = (f32[2,128,3584]{2,1,0:T(8,128)S(1)}, f32[2,128,3584]{2,1,0:T(8,128)}, u32[]{:S(2)}) copy-start(f32[2,128,3584]{2,1,0:T(8,128)} %copy-done.1) | copy-start | bytes 11010052
  104.0 10.5 %copy-start.5 = (f32[2,128,3584]{2,1,0:T(8,128)}, f32[2,128,3584]{2,1,0:T(8,128)S(1)}, u32[]{:S(2)}) copy-start(f32[2,128,3584]{2,1,0:T(8,128)S(1)} %fusion.refs_4_.refs_16_) | copy-start | bytes 11010052
  105.8 23.8 %collective-permute-start.28 = (bf16[4,4096]{1,0:T(4,128)(2,1)}, bf16[4,4096]{1,0:T(4,128)(2,1)}, u32[]{:S(2)}, u32[]{:S(2)}) collective-permute-start(bf16[4,4096]{1,0:T(4,128)(2,1)} %pad_maximum_fusion.3), channel_id=1, source_target_pairs={{0,4},{4,8},{8,12},{12,0},{1,5},{5,9},{9,13},{13,1},{2,6},{6,10},{... | collective-permute-start | bytes 98312 | tf_op jit(solution)/shard_map/ppermute | solution.py:42
  107.8 22.7 %collective-permute-start.29 = (bf16[4,4096]{1,0:T(4,128)(2,1)}, bf16[4,4096]{1,0:T(4,128)(2,1)}, u32[]{:S(2)}, u32[]{:S(2)}) collective-permute-start(bf16[4,4096]{1,0:T(4,128)(2,1)} %pad_maximum_fusion.3), channel_id=1, source_target_pairs={{0,8},{4,12},{8,0},{12,4},{1,9},{5,13},{9,1},{13,5},{2,10},{6,14},... | collective-permute-start | bytes 98312 | tf_op jit(solution)/shard_map/ppermute | solution.py:42
  110.2 21.4 %collective-permute-start.30 = (bf16[4,4096]{1,0:T(4,128)(2,1)}, bf16[4,4096]{1,0:T(4,128)(2,1)}, u32[]{:S(2)}, u32[]{:S(2)}) collective-permute-start(bf16[4,4096]{1,0:T(4,128)(2,1)} %pad_maximum_fusion.3), channel_id=1, source_target_pairs={{0,12},{4,0},{8,4},{12,8},{1,13},{5,1},{9,5},{13,9},{2,14},{6,2},{... | collective-permute-start | bytes 98312 | tf_op jit(solution)/shard_map/ppermute | solution.py:42
  114.6 26.8 %collective-permute-start.23 = (bf16[128,3584]{1,0:T(8,128)(2,1)}, bf16[128,3584]{1,0:T(8,128)(2,1)S(1)}, u32[]{:S(2)}, u32[]{:S(2)}) collective-permute-start(bf16[128,3584]{1,0:T(8,128)(2,1)} %payload.18.refs_4_), channel_id=1, source_target_pairs={{0,4},{2,0},{4,8},{6,2},{8,12},{10,6},{12,14},{14,10},{1,5},{3,1},... | collective-permute-start | bytes 2752520 | tf_op jit(solution)/shard_map/ppermute | solution.py:37
  115.1 1.8 %copy-start.14 = (bf16[64,3584]{1,0:T(8,128)(2,1)}, bf16[64,3584]{1,0:T(8,128)(2,1)S(1)}, u32[]{:S(2)}) copy-start(bf16[64,3584]{1,0:T(8,128)(2,1)S(1)} %collective-permute-done.16.refs_1_.refs_13_) | copy-start | bytes 1376260
  116.9 1.6 %copy-start.13 = (bf16[128,3584]{1,0:T(8,128)(2,1)}, bf16[128,3584]{1,0:T(8,128)(2,1)S(1)}, u32[]{:S(2)}) copy-start(bf16[128,3584]{1,0:T(8,128)(2,1)S(1)} %payload.19.refs_17_) | copy-start | bytes 2752516
  117.0 24.4 %collective-permute-start.24 = (bf16[128,3584]{1,0:T(8,128)(2,1)S(1)}, bf16[128,3584]{1,0:T(8,128)(2,1)S(1)}, u32[]{:S(2)}, u32[]{:S(2)}) collective-permute-start(bf16[128,3584]{1,0:T(8,128)(2,1)S(1)} %payload.19.refs_17_), channel_id=1, source_target_pairs={{0,2},{2,6},{4,0},{6,10},{8,4},{10,14},{12,8},{14,12},{1,3},{3,7},... | collective-permute-start | bytes 2752520 | tf_op jit(solution)/shard_map/ppermute | solution.py:37
  118.6 14.3 %copy-start.21 = (bf16[256,2048]{1,0:T(8,128)(2,1)S(1)}, bf16[256,2048]{1,0:T(8,128)(2,1)}, u32[]{:S(2)}) copy-start(bf16[256,2048]{1,0:T(8,128)(2,1)} %x_ref.1) | copy-start | bytes 3145732
  118.6 14.3 %copy-start.22 = (bf16[2048,64]{0,1:T(8,128)(2,1)S(1)}, bf16[2048,64]{0,1:T(8,128)(2,1)}, u32[]{:S(2)}) copy-start(bf16[2048,64]{0,1:T(8,128)(2,1)} %param.12) | copy-start | bytes 786436
  118.6 22.8 %copy-start.26 = (bf16[256,3584]{1,0:T(8,128)(2,1)S(1)}, bf16[256,3584]{1,0:T(8,128)(2,1)}, u32[]{:S(2)}) copy-start(bf16[256,3584]{1,0:T(8,128)(2,1)} %refs_1_.1) | copy-start | bytes 5505028
  118.6 22.8 %copy-start.27 = (bf16[3584,64]{0,1:T(8,128)(2,1)S(1)}, bf16[3584,64]{0,1:T(8,128)(2,1)}, u32[]{:S(2)}) copy-start(bf16[3584,64]{0,1:T(8,128)(2,1)} %param.13) | copy-start | bytes 1376260
  129.7 9.5 %collective-permute-start.20 = (f32[64,128]{1,0:T(8,128)S(1)}, f32[64,128]{1,0:T(8,128)S(1)}, u32[]{:S(2)}, u32[]{:S(2)}) collective-permute-start(f32[64,128]{1,0:T(8,128)S(1)} %get-tuple-element.9), channel_id=1, source_target_pairs={{0,12},{4,0},{8,4},{12,8},{1,13},{5,1},{9,5},{13,9},{2,14},{6,2},{... | collective-permute-start | bytes 98312 | tf_op jit(solution)/shard_map/ppermute | solution.py:42
  130.5 9.9 %collective-permute-start.21 = (f32[64,128]{1,0:T(8,128)S(1)}, f32[64,128]{1,0:T(8,128)S(1)}, u32[]{:S(2)}, u32[]{:S(2)}) collective-permute-start(f32[64,128]{1,0:T(8,128)S(1)} %get-tuple-element.11), channel_id=1, source_target_pairs={{0,8},{4,12},{8,0},{12,4},{1,9},{5,13},{9,1},{13,5},{2,10},{6,14},... | collective-permute-start | bytes 98312 | tf_op jit(solution)/shard_map/ppermute | solution.py:42
  131.7 8.7 %collective-permute-start.22 = (f32[64,128]{1,0:T(8,128)S(1)}, f32[64,128]{1,0:T(8,128)S(1)}, u32[]{:S(2)}, u32[]{:S(2)}) collective-permute-start(f32[64,128]{1,0:T(8,128)S(1)} %get-tuple-element.10), channel_id=1, source_target_pairs={{0,4},{4,8},{8,12},{12,0},{1,5},{5,9},{9,13},{13,1},{2,6},{6,10},{... | collective-permute-start | bytes 98312 | tf_op jit(solution)/shard_map/ppermute | solution.py:42
  132.9 0.9 copy-start.19
  139.2 1.3 collective-permute-start.18
  140.5 5.6 %collective-permute-start.19 = (f32[256,64]{1,0:T(8,128)S(1)}, f32[256,64]{1,0:T(8,128)S(1)}, u32[]{:S(2)}, u32[]{:S(2)}) collective-permute-start(f32[256,64]{1,0:T(8,128)S(1)} %add.185), channel_id=1, source_target_pairs={{0,2},{2,0},{1,3},{3,1},{4,6},{6,4},{5,7},{7,5},{8,10},{10,8},{9,1... | collective-permute-start | bytes 196616 | tf_op jit(solution)/shard_map/ppermute | solution.py:59
  143.8 2.4 %collective-permute-start.25 = (f32[64,256]{1,0:T(8,128)S(1)}, f32[64,256]{1,0:T(8,128)S(1)}, u32[]{:S(2)}, u32[]{:S(2)}) collective-permute-start(f32[64,256]{1,0:T(8,128)S(1)} %pad_maximum_fusion.2), channel_id=1, source_target_pairs={{0,1},{1,0},{2,3},{3,2},{4,5},{5,4},{6,7},{7,6},{8,9},{9,8},{10,11... | collective-permute-start | bytes 196616 | tf_op jit(solution)/shard_map/ppermute | solution.py:59
  146.3 4.3 %collective-permute-start.26 = (f32[64,256]{1,0:T(8,128)S(1)}, f32[64,256]{1,0:T(8,128)S(1)}, u32[]{:S(2)}, u32[]{:S(2)}) collective-permute-start(f32[64,256]{1,0:T(8,128)S(1)} %fusion.32), channel_id=1, source_target_pairs={{0,2},{2,0},{1,3},{3,1},{4,6},{6,4},{5,7},{7,5},{8,10},{10,8},{9,1... | collective-permute-start | bytes 196616 | tf_op jit(solution)/shard_map/ppermute | solution.py:59

commit v4 on v3

--- a/solution.py
+++ b/solution.py
@@ -332,9 +332,7 @@
     for p in begin:
         last = hidden_grad(spreads[p], w_down, half, half, last)
         second[p] = (last, 0)
-    for p in later:
-        whole[p] = whole_of(features_of[p], [last] + came[-1][0])
-    last, all_q = [whole[later[0]]], None
+    last, all_q = list(came[-1][0]), None
 
     width = R * R // cores
 
@@ -376,6 +374,10 @@
                     got = [stream[-1][int(reverse)] for stream in streams]
                 rows_at = [start + c * part * len(streams) for _, start in arrays]
                 arrays = [array for array, _ in arrays]
+                if s == 1 and not reverse and c == len(parts) - 1:
+                    for p in later:
+                        whole[p] = whole_of(features_of[p], last)
+                    last = last + [whole[later[0]]]
                 last = payload(scalars, got, len(streams), arrays, rows_at, *last)
                 last = [last]
                 both.append(onward(last[0], reverse))

time: 154 us -> 154 us (level)
  Pallas kernels: 27.1 us -> 30.4 us
  local copies, waits for them, and re-layouts: 12.6 us -> 9.96 us
    unnamed x58 -> x54, local copies, waits for them, and re-layouts: 7.16 us -> 4.54 us
    pallas_call x3, Pallas kernels: 1.5 us -> 3.58 us  [hidden_grad(): pl.pallas_call(stack_kernel, grid=(1,), in_specs=[pl.BlockSpec((rows, dep...]
  transfers between devices with their start and end apart: 31 -> 31, of which waited for: 10 -> 8; matrix products, arithmetic and copies ran while one was open for 23% -> 23% of each run, Pallas kernels for 18% -> 19%
where the time goes in v4:
time: 154 us; the launch traced here: 153 us
  waiting for transfers between devices  39.8 us (26%)
  starting transfers between devices  37.2 us (24%)
  Pallas kernels  30.4 us (20%)
  matrix products  30.3 us (20%)
  local copies, waits for them, and re-layouts  9.96 us (6%)
  other arithmetic  3.6 us (2%)
  between operations  1.61 us (1%)
    dot_general x3, matrix products, hidden_grad(): lax.dot_general(stacked.reshape(-1, depth), w_down, ROWS_ROWS, preferred_...  26.3 us
    pallas_call x10, Pallas kernels, payload(): pl.pallas_call(kernel, grid_spec=grid_spec, out_shape=jax.ShapeDtypeStruc...  14.2 us
    ppermute x11, starting transfers between devices, shifted(): lax.ppermute(block, axis, [(i, (i + distance) % n) for i in range(n)])  12 us
    ppermute x10, starting transfers between devices, onward(): return lax.ppermute(block, ('blk', 'fsdp'), route)  10.9 us
    pallas_call x1, Pallas kernels, projected_first(): pl.pallas_call(kernel, grid_spec=grid_spec, out_shape=jax.ShapeDtypeStruc...  10.3 us
    ppermute x2, waiting for transfers between devices, line_left(): return lax.ppermute(block, 'blk', [(i + 1, i) for i in range(n - 1)])  10.2 us
    ppermute x2, waiting for transfers between devices, features(): return lax.ppermute(mine, ('blk', 'sub'), route)  9.36 us
    ppermute x2, waiting for transfers between devices, line_right(): return lax.ppermute(block, 'blk', [(i, i + 1) for i in range(n - 1)])  8.79 us
  transfers between devices with their start and end apart: 31, of which 8 were waited for; matrix products, arithmetic and copies ran while one was open for 23% of the time, Pallas kernels for 19%

profile of v4, /device:TPU:0, one launch (start us, length us, event | category | flops | bytes accessed | tf_op | source)
XLA Modules:
  0.0 152.8 jit_solution(4186739500355240501)
XLA Ops:
  0.7 1.4 fusion.33
  2.1 3.1 %collective-permute-start.4 = (bf16[128,2048]{1,0:T(8,128)(2,1)S(1)}, bf16[128,2048]{1,0:T(8,128)(2,1)S(1)}, u32[]{:S(2)}, u32[]{:S(2)}) collective-permute-start(bf16[128,2048]{1,0:T(8,128)(2,1)S(1)} %get-tuple-element.3), channel_id=1, source_target_pairs={{0,4},{1,12},{4,0},{5,8},{8,5},{9,13},{12,1},{13,9},{2,6},{3,14},{... | collective-permute-start | bytes 1572872 | tf_op jit(solution)/shard_map/ppermute | solution.py:303
  5.2 1.4 collective-permute-start.6
  6.6 9.4 %collective-permute-done.4.refs_1_ = bf16[128,2048]{1,0:T(8,128)(2,1)S(1)} collective-permute-done((bf16[128,2048]{1,0:T(8,128)(2,1)S(1)}, bf16[128,2048]{1,0:T(8,128)(2,1)S(1)}, u32[]{:S(2)}, u32[]{:S(2)}) %collective-permute-start.4) | collective-permute-done | bytes 524320 | tf_op jit(solution)/shard_map/ppermute | solution.py:303
  16.0 2.4 %collective-permute-start.5 = (bf16[128,2048]{1,0:T(8,128)(2,1)S(1)}, bf16[128,2048]{1,0:T(8,128)(2,1)S(1)}, u32[]{:S(2)}, u32[]{:S(2)}) collective-permute-start(bf16[128,2048]{1,0:T(8,128)(2,1)S(1)} %collective-permute-done.4.refs_1_), channel_id=1, source_target_pairs={{0,2},{2,0},{1,3},{3,1},{4,6},{6,4},{5,7},{7,5},{8,10},{10,8},{9,1... | collective-permute-start | bytes 1572872 | tf_op jit(solution)/shard_map/ppermute | solution.py:42
  18.3 0.9 fusion.34
  19.2 3.7 %collective-permute-start = (bf16[64,3584]{1,0:T(8,128)(2,1)S(1)}, bf16[64,3584]{1,0:T(8,128)(2,1)S(1)}, u32[]{:S(2)}, u32[]{:S(2)}) collective-permute-start(bf16[64,3584]{1,0:T(8,128)(2,1)S(1)} %get-tuple-element.5), channel_id=1, source_target_pairs={{0,4},{4,8},{8,12},{1,5},{5,9},{9,13},{2,6},{6,10},{10,14},{3,7},{... | collective-permute-start | bytes 1376264 | tf_op jit(solution)/shard_map/ppermute | solution.py:22
  22.9 1.3 collective-permute-start.2
  24.2 8.8 %collective-permute-done.refs_3_.refs_1_ = bf16[64,3584]{1,0:T(8,128)(2,1)S(1)} collective-permute-done((bf16[64,3584]{1,0:T(8,128)(2,1)S(1)}, bf16[64,3584]{1,0:T(8,128)(2,1)S(1)}, u32[]{:S(2)}, u32[]{:S(2)}) %collective-permute-start) | collective-permute-done | bytes 458784 | tf_op jit(solution)/shard_map/ppermute | solution.py:22
  33.0 7.0 %collective-permute-done.2.refs_4_.refs_2_.refs_5_ = bf16[64,3584]{1,0:T(8,128)(2,1)S(1)} collective-permute-done((bf16[64,3584]{1,0:T(8,128)(2,1)S(1)}, bf16[64,3584]{1,0:T(8,128)(2,1)S(1)}, u32[]{:S(2)}, u32[]{:S(2)}) %collective-permute-start.2) | collective-permute-done | bytes 458784 | tf_op jit(solution)/shard_map/ppermute | solution.py:27
  40.2 2.5 %collective-permute-start.1 = (bf16[64,3584]{1,0:T(8,128)(2,1)}, bf16[64,3584]{1,0:T(8,128)(2,1)S(1)}, u32[]{:S(2)}, u32[]{:S(2)}) collective-permute-start(bf16[64,3584]{1,0:T(8,128)(2,1)} %get-tuple-element.4), channel_id=1, source_target_pairs={{0,4},{4,8},{8,12},{1,5},{5,9},{9,13},{2,6},{6,10},{10,14},{3,7},{... | collective-permute-start | bytes 1376264 | tf_op jit(solution)/shard_map/ppermute | solution.py:22
  42.7 1.3 collective-permute-start.3
  44.4 1.5 collective-permute-start.9
  45.9 1.1 stack.249
  47.0 7.3 %fusion.4.refs_3_ = f32[2,128,3584]{2,1,0:T(8,128)S(1)} fusion(bf16[2,128,2048]{2,1,0:T(8,128)(2,1)S(1)} %stack.249, bf16[3584,2048]{1,0:T(8,128)(2,1)} %param.11), kind=kOutput, calls=%fused_computation.4 | convolution fusion | flops 3758096384 | bytes 19398656 | tf_op jit(solution)/shard_map/dot_general | solution.py:101
  54.3 3.1 %collective-permute-done.3.refs_5_.refs_2_.refs_6_ = bf16[64,3584]{1,0:T(8,128)(2,1)S(1)} collective-permute-done((bf16[64,3584]{1,0:T(8,128)(2,1)}, bf16[64,3584]{1,0:T(8,128)(2,1)S(1)}, u32[]{:S(2)}, u32[]{:S(2)}) %collective-permute-start.3) | collective-permute-done | bytes 458784 | tf_op jit(solution)/shard_map/ppermute | solution.py:27
  57.4 0.9 payload.10.refs_4_
  58.4 0.9 payload.11.refs_3_.refs_4_
  59.3 1.3 join.3.refs_5_.refs_0_
  61.2 0.6 stack.199.refs_0_
  61.8 1.7 %collective-permute-start.8 = (bf16[64,3584]{1,0:T(8,128)(2,1)}, bf16[64,3584]{1,0:T(8,128)(2,1)S(1)}, u32[]{:S(2)}, u32[]{:S(2)}) collective-permute-start(bf16[64,3584]{1,0:T(8,128)(2,1)} %copy-done.11), channel_id=1, source_target_pairs={{0,4},{2,0},{4,8},{6,2},{8,12},{10,6},{12,14},{14,10},{1,5},{3,1},... | collective-permute-start | bytes 1376264 | tf_op jit(solution)/shard_map/ppermute | solution.py:37
  63.9 2.0 %copy-done.2 = f32[2,128,3584]{2,1,0:T(8,128)S(1)} copy-done((f32[2,128,3584]{2,1,0:T(8,128)S(1)}, f32[2,128,3584]{2,1,0:T(8,128)}, u32[]{:S(2)}) %copy-start.2) | copy-done | bytes 3670040
  65.9 0.9 payload.12.refs_4_
  66.8 1.8 %collective-permute-start.10 = (bf16[64,3584]{1,0:T(8,128)(2,1)S(1)}, bf16[64,3584]{1,0:T(8,128)(2,1)S(1)}, u32[]{:S(2)}, u32[]{:S(2)}) collective-permute-start(bf16[64,3584]{1,0:T(8,128)(2,1)S(1)} %payload.12.refs_4_), channel_id=1, source_target_pairs={{0,4},{2,0},{4,8},{6,2},{8,12},{10,6},{12,14},{14,10},{1,5},{3,1},... | collective-permute-start | bytes 1376264 | tf_op jit(solution)/shard_map/ppermute | solution.py:37
  68.6 0.9 payload.13.refs_2_
  69.5 0.9 collective-permute-start.12
  70.4 1.4 stack.250
  71.8 11.3 %fusion.2.refs_2_.refs_3_.refs_15_ = f32[2,256,3584]{2,1,0:T(8,128)S(1)} fusion(bf16[2,256,2048]{2,1,0:T(8,128)(2,1)S(1)} %stack.250, bf16[3584,2048]{1,0:T(8,128)(2,1)} %param.11), kind=kOutput, calls=%fused_computation.2 | convolution fusion | flops 7516192768 | bytes 24117248 | tf_op jit(solution)/shard_map/dot_general | solution.py:101
  83.1 2.1 %payload.14.refs_3_ = bf16[64,3584]{1,0:T(8,128)(2,1)} custom-call(s32[5]{0:T(128)S(1)} %stack.218.refs_0_, bf16[64,3584]{1,0:T(8,128)(2,1)S(1)} %collective-permute-done.8.refs_1_.refs_7_, f32[2,256,3584]{2,1,0:T(8,128)S(1)} %fusion.2.refs_2_.refs_3_.refs_15_, f32[2,256,3584]{2,1,0:T(8,128)S(1)} %fusion.2.refs_2_.refs_3_.refs_15_), custom_call_target="tpu_custom_call" | custom-call | flops 1000 | bytes 1000 | tf_op jit(solution)/shard_map/payload/pallas_call | solution.py:195
  85.1 1.2 collective-permute-start.14
  86.4 1.5 %payload.15.refs_3_ = bf16[64,3584]{1,0:T(8,128)(2,1)} custom-call(s32[5]{0:T(128)S(1)} %stack.221.refs_0_, bf16[64,3584]{1,0:T(8,128)(2,1)S(1)} %collective-permute-done.11.refs_1_.refs_9_, f32[2,256,3584]{2,1,0:T(8,128)S(1)} %fusion.2.refs_2_.refs_3_.refs_15_, bf16[64,3584]{1,0:T(8,128)(2,1)} %payload.14.refs_3_), custom_call_target="tpu_custom_call" | custom-call | flops 1000 | bytes 1000 | tf_op jit(solution)/shard_map/payload/pallas_call | solution.py:195
  87.9 0.8 collective-permute-start.16
  88.7 1.5 payload.16.refs_3_
  90.2 1.2 collective-permute-start.15
  91.5 0.9 payload.17.refs_2_.after_ref
  92.4 0.9 collective-permute-start.17
  94.4 1.1 stack.251
  95.6 1.0 copy-done.18
  96.6 7.7 %fusion.refs_4_.refs_16_ = f32[2,128,3584]{2,1,0:T(8,128)S(1)} fusion(bf16[2,128,2048]{2,1,0:T(8,128)(2,1)} %copy-done.18, bf16[3584,2048]{1,0:T(8,128)(2,1)} %param.11), kind=kOutput, calls=%fused_computation | convolution fusion | flops 3758096384 | bytes 19398656 | tf_op jit(solution)/shard_map/dot_general | solution.py:101
  104.3 0.8 bitcast_select_fusion.1
  105.2 1.0 pad_maximum_fusion.3
  106.1 1.2 collective-permute-start.28
  107.3 1.5 collective-permute-start.29
  108.9 1.9 %collective-permute-start.30 = (bf16[4,4096]{1,0:T(4,128)(2,1)}, bf16[4,4096]{1,0:T(4,128)(2,1)}, u32[]{:S(2)}, u32[]{:S(2)}) collective-permute-start(bf16[4,4096]{1,0:T(4,128)(2,1)} %pad_maximum_fusion.3), channel_id=1, source_target_pairs={{0,12},{4,0},{8,4},{12,8},{1,13},{5,1},{9,5},{13,9},{2,14},{6,2},{... | collective-permute-start | bytes 98312 | tf_op jit(solution)/shard_map/ppermute | solution.py:42
  110.8 2.8 %payload.18.refs_4_ = bf16[128,3584]{1,0:T(8,128)(2,1)} custom-call(s32[5]{0:T(128)S(1)} %stack.229.refs_0_, bf16[64,3584]{1,0:T(8,128)(2,1)} %collective-permute-done.14.refs_1_.refs_11_, bf16[64,3584]{1,0:T(8,128)(2,1)} %collective-permute-done.15.refs_2_.refs_12_, f32[2,128,3584]{2,1,0:T(8,128)S(1)} %copy-done.4, f32[2,128,3584]{2,1,0:T(8,128)S(1)} %fusion.refs_4_.refs_16_), custom_call_target="tpu_custom_call" | custom-call | flops 1000 | bytes 1000 | tf_op jit(solution)/shard_map/payload/pallas_call | solution.py:195
  113.7 1.8 %payload.19.refs_17_ = bf16[128,3584]{1,0:T(8,128)(2,1)S(1)} custom-call(s32[5]{0:T(128)S(1)} %stack.225.refs_0_, bf16[64,3584]{1,0:T(8,128)(2,1)S(1)} %collective-permute-done.16.refs_1_.refs_13_, bf16[64,3584]{1,0:T(8,128)(2,1)} %collective-permute-done.17.refs_2_.refs_14_, f32[2,128,3584]{2,1,0:T(8,128)S(1)} %copy-done.4, bf16[128,3584]{1,0:T(8,128)(2,1)} %payload.18.refs_4_), custom_call_target="tpu_custom_call" | custom-call | flops 1000 | bytes 1000 | tf_op jit(solution)/shard_map/payload/pallas_call | solution.py:195
  115.6 2.0 %collective-permute-start.24 = (bf16[128,3584]{1,0:T(8,128)(2,1)S(1)}, bf16[128,3584]{1,0:T(8,128)(2,1)S(1)}, u32[]{:S(2)}, u32[]{:S(2)}) collective-permute-start(bf16[128,3584]{1,0:T(8,128)(2,1)S(1)} %payload.19.refs_17_), channel_id=1, source_target_pairs={{0,2},{2,6},{4,0},{6,10},{8,4},{10,14},{12,8},{14,12},{1,3},{3,7},... | collective-permute-start | bytes 2752520 | tf_op jit(solution)/shard_map/ppermute | solution.py:37
  117.6 10.3 %projected_first.1.after_ref = f32[4,64,128]{2,1,0:T(8,128)} custom-call(s32[8]{0:T(128)} %stack.199.refs_0_, bf16[256,3584]{1,0:T(8,128)(2,1)} %refs_1_.1, bf16[64,3584]{1,0:T(8,128)(2,1)} %bitcast.81, bf16[64,3584]{1,0:T(8,128)(2,1)} %copy-done.8, bf16[64,3584]{1,0:T(8,128)(2,1)} %copy-done.6, bf16[64,3584]{1,0:T(8,128)(2,1)} %copy-done.9, ...), custom_call_target="tpu_custom_call" | custom-call | flops 1000 | bytes 59040000 | tf_op jit(solution)/shard_map/projected_first/pallas_call | solution.py:255
  127.9 0.8 slice_bitcast_fusion.2
  128.7 1.4 collective-permute-start.20
  130.1 0.7 collective-permute-start.21
  130.8 1.2 collective-permute-start.22
  132.0 0.9 select_bitcast_fusion.3
  132.9 0.9 copy-done.17
  134.2 4.2 %collective-permute-done.20 = f32[64,128]{1,0:T(8,128)S(1)} collective-permute-done((f32[64,128]{1,0:T(8,128)S(1)}, f32[64,128]{1,0:T(8,128)S(1)}, u32[]{:S(2)}, u32[]{:S(2)}) %collective-permute-start.20) | collective-permute-done | bytes 32800 | tf_op jit(solution)/shard_map/ppermute | solution.py:42
  138.4 2.3 %collective-permute-done.21 = f32[64,128]{1,0:T(8,128)S(1)} collective-permute-done((f32[64,128]{1,0:T(8,128)S(1)}, f32[64,128]{1,0:T(8,128)S(1)}, u32[]{:S(2)}, u32[]{:S(2)}) %collective-permute-start.21) | collective-permute-done | bytes 32800 | tf_op jit(solution)/shard_map/ppermute | solution.py:42
  140.8 2.5 %fusion.16 = f32[64,128]{1,0:T(8,128)S(1)} fusion(bf16[3584,64]{0,1:T(8,128)(2,1)S(1)} %copy-done.25, f32[2,256,3584]{2,1,0:T(8,128)} %copy-done, s32[]{:T(128)S(6)} %select_n.436, s32[]{:T(128)S(6)} %add.202, bf16[128,3584]{1,0:T(8,128)(2,1)S(1)} %collective-permute-done.24, bf16[128,3584]{1,0:T(8,128)(2,1)S(1)} %collective-permute-done.23, ...), kind=kOutput, calls=%fused_computation.17 | convolution fusion | flops 179830784 | bytes 5079050 | tf_op jit(solution)/shard_map/dot_general | solution.py:421
  143.4 0.8 select_bitcast_fusion.2
  144.3 1.5 collective-permute-done.19
  145.9 0.8 collective-permute-start.26
  146.8 3.4 %collective-permute-done.26 = f32[64,256]{1,0:T(8,128)S(1)} collective-permute-done((f32[64,256]{1,0:T(8,128)S(1)}, f32[64,256]{1,0:T(8,128)S(1)}, u32[]{:S(2)}, u32[]{:S(2)}) %collective-permute-start.26) | collective-permute-done | bytes 65568 | tf_op jit(solution)/shard_map/ppermute | solution.py:59
  150.2 0.6 convolution_convert_fusion
  151.4 0.6 constant_dynamic-slice_fusion
  152.0 0.8 fusion.23
  (105 shorter events, 3.7 us)
Async XLA Ops:
  0.6 17.7 %copy-start.23 = (bf16[256,3584]{1,0:T(8,128)(2,1)S(1)}, bf16[256,3584]{1,0:T(8,128)(2,1)}, u32[]{:S(2)}) copy-start(bf16[256,3584]{1,0:T(8,128)(2,1)} %refs_1_.1) | copy-start | bytes 5505028
  2.1 13.9 %collective-permute-start.4 = (bf16[128,2048]{1,0:T(8,128)(2,1)S(1)}, bf16[128,2048]{1,0:T(8,128)(2,1)S(1)}, u32[]{:S(2)}, u32[]{:S(2)}) collective-permute-start(bf16[128,2048]{1,0:T(8,128)(2,1)S(1)} %get-tuple-element.3), channel_id=1, source_target_pairs={{0,4},{1,12},{4,0},{5,8},{8,5},{9,13},{12,1},{13,9},{2,6},{3,14},{... | collective-permute-start | bytes 1572872 | tf_op jit(solution)/shard_map/ppermute | solution.py:303
  5.2 34.9 %collective-permute-start.6 = (bf16[128,2048]{1,0:T(8,128)(2,1)S(1)}, bf16[128,2048]{1,0:T(8,128)(2,1)}, u32[]{:S(2)}, u32[]{:S(2)}) collective-permute-start(bf16[128,2048]{1,0:T(8,128)(2,1)S(1)} %get-tuple-element.2), channel_id=1, source_target_pairs={{0,0},{1,8},{4,4},{5,12},{8,1},{9,9},{12,5},{13,13},{2,2},{3,10},{... | collective-permute-start | bytes 1572872 | tf_op jit(solution)/shard_map/ppermute | solution.py:303
  16.0 24.1 %collective-permute-start.5 = (bf16[128,2048]{1,0:T(8,128)(2,1)S(1)}, bf16[128,2048]{1,0:T(8,128)(2,1)S(1)}, u32[]{:S(2)}, u32[]{:S(2)}) collective-permute-start(bf16[128,2048]{1,0:T(8,128)(2,1)S(1)} %collective-permute-done.4.refs_1_), channel_id=1, source_target_pairs={{0,2},{2,0},{1,3},{3,1},{4,6},{6,4},{5,7},{7,5},{8,10},{10,8},{9,1... | collective-permute-start | bytes 1572872 | tf_op jit(solution)/shard_map/ppermute | solution.py:42
  19.2 26.6 %copy-start.22 = (s32[256]{0:T(256)S(1)}, s32[256]{0:T(256)}, u32[]{:S(2)}) copy-start(s32[256]{0:T(256)} %refs_2_.1) | copy-start | bytes 3076
  19.2 13.8 %collective-permute-start = (bf16[64,3584]{1,0:T(8,128)(2,1)S(1)}, bf16[64,3584]{1,0:T(8,128)(2,1)S(1)}, u32[]{:S(2)}, u32[]{:S(2)}) collective-permute-start(bf16[64,3584]{1,0:T(8,128)(2,1)S(1)} %get-tuple-element.5), channel_id=1, source_target_pairs={{0,4},{4,8},{8,12},{1,5},{5,9},{9,13},{2,6},{6,10},{10,14},{3,7},{... | collective-permute-start | bytes 1376264 | tf_op jit(solution)/shard_map/ppermute | solution.py:22
  22.9 17.1 %collective-permute-start.2 = (bf16[64,3584]{1,0:T(8,128)(2,1)S(1)}, bf16[64,3584]{1,0:T(8,128)(2,1)S(1)}, u32[]{:S(2)}, u32[]{:S(2)}) collective-permute-start(bf16[64,3584]{1,0:T(8,128)(2,1)S(1)} %get-tuple-element.5), channel_id=1, source_target_pairs={{4,0},{8,4},{12,8},{5,1},{9,5},{13,9},{6,2},{10,6},{14,10},{7,3},{... | collective-permute-start | bytes 1376264 | tf_op jit(solution)/shard_map/ppermute | solution.py:27
  33.0 25.4 %copy-start.8 = (bf16[64,3584]{1,0:T(8,128)(2,1)}, bf16[64,3584]{1,0:T(8,128)(2,1)S(1)}, u32[]{:S(2)}) copy-start(bf16[64,3584]{1,0:T(8,128)(2,1)S(1)} %collective-permute-done.refs_3_.refs_1_) | copy-start | bytes 1376260
  40.0 18.3 %copy-start.9 = (bf16[64,3584]{1,0:T(8,128)(2,1)}, bf16[64,3584]{1,0:T(8,128)(2,1)S(1)}, u32[]{:S(2)}) copy-start(bf16[64,3584]{1,0:T(8,128)(2,1)S(1)} %collective-permute-done.2.refs_4_.refs_2_.refs_5_) | copy-start | bytes 1376260
  40.1 5.7 %collective-permute-start.7 = (bf16[256,2048]{1,0:T(8,128)(2,1)S(1)}, bf16[256,2048]{1,0:T(8,128)(2,1)}, u32[]{:S(2)}, u32[]{:S(2)}) collective-permute-start(bf16[256,2048]{1,0:T(8,128)(2,1)S(1)} %join.2.refs_0_), channel_id=1, source_target_pairs={{0,1},{1,0},{2,3},{3,2},{4,5},{5,4},{6,7},{7,6},{8,9},{9,8},{10,11... | collective-permute-start | bytes 3145736 | tf_op jit(solution)/shard_map/ppermute | solution.py:42
  40.2 14.1 %collective-permute-start.1 = (bf16[64,3584]{1,0:T(8,128)(2,1)}, bf16[64,3584]{1,0:T(8,128)(2,1)S(1)}, u32[]{:S(2)}, u32[]{:S(2)}) collective-permute-start(bf16[64,3584]{1,0:T(8,128)(2,1)} %get-tuple-element.4), channel_id=1, source_target_pairs={{0,4},{4,8},{8,12},{1,5},{5,9},{9,13},{2,6},{6,10},{10,14},{3,7},{... | collective-permute-start | bytes 1376264 | tf_op jit(solution)/shard_map/ppermute | solution.py:22
  42.7 14.7 %collective-permute-start.3 = (bf16[64,3584]{1,0:T(8,128)(2,1)}, bf16[64,3584]{1,0:T(8,128)(2,1)S(1)}, u32[]{:S(2)}, u32[]{:S(2)}) collective-permute-start(bf16[64,3584]{1,0:T(8,128)(2,1)} %get-tuple-element.4), channel_id=1, source_target_pairs={{4,0},{8,4},{12,8},{5,1},{9,5},{13,9},{6,2},{10,6},{14,10},{7,3},{... | collective-permute-start | bytes 1376264 | tf_op jit(solution)/shard_map/ppermute | solution.py:27
  44.4 15.0 %collective-permute-start.9 = (bf16[128,2048]{1,0:T(8,128)(2,1)}, bf16[128,2048]{1,0:T(8,128)(2,1)}, u32[]{:S(2)}, u32[]{:S(2)}) collective-permute-start(bf16[128,2048]{1,0:T(8,128)(2,1)} %collective-permute-done.6.refs_5_.refs_1_), channel_id=1, source_target_pairs={{0,2},{2,0},{1,3},{3,1},{4,6},{6,4},{5,7},{7,5},{8,10},{10,8},{9,1... | collective-permute-start | bytes 1572872 | tf_op jit(solution)/shard_map/ppermute | solution.py:42
  54.3 4.1 %copy-start.1 = (f32[2,128,3584]{2,1,0:T(8,128)}, f32[2,128,3584]{2,1,0:T(8,128)S(1)}, u32[]{:S(2)}) copy-start(f32[2,128,3584]{2,1,0:T(8,128)S(1)} %fusion.4.refs_3_) | copy-start | bytes 11010052
  54.3 14.3 %copy-start.6 = (bf16[64,3584]{1,0:T(8,128)(2,1)}, bf16[64,3584]{1,0:T(8,128)(2,1)S(1)}, u32[]{:S(2)}) copy-start(bf16[64,3584]{1,0:T(8,128)(2,1)S(1)} %collective-permute-done.1.refs_4_.refs_1_) | copy-start | bytes 1376260
  57.4 11.2 %copy-start.7 = (bf16[64,3584]{1,0:T(8,128)(2,1)}, bf16[64,3584]{1,0:T(8,128)(2,1)S(1)}, u32[]{:S(2)}) copy-start(bf16[64,3584]{1,0:T(8,128)(2,1)S(1)} %collective-permute-done.3.refs_5_.refs_2_.refs_6_) | copy-start | bytes 1376260
  58.4 0.9 copy-start.11
  60.6 9.8 %collective-permute-start.13 = (bf16[256,2048]{1,0:T(8,128)(2,1)S(1)}, bf16[256,2048]{1,0:T(8,128)(2,1)}, u32[]{:S(2)}, u32[]{:S(2)}) collective-permute-start(bf16[256,2048]{1,0:T(8,128)(2,1)S(1)} %join.3.refs_5_.refs_0_), channel_id=1, source_target_pairs={{0,1},{1,0},{2,3},{3,2},{4,5},{5,4},{6,7},{7,6},{8,9},{9,8},{10,11... | collective-permute-start | bytes 3145736 | tf_op jit(solution)/shard_map/ppermute | solution.py:42
  61.8 21.2 %collective-permute-start.8 = (bf16[64,3584]{1,0:T(8,128)(2,1)}, bf16[64,3584]{1,0:T(8,128)(2,1)S(1)}, u32[]{:S(2)}, u32[]{:S(2)}) collective-permute-start(bf16[64,3584]{1,0:T(8,128)(2,1)} %copy-done.11), channel_id=1, source_target_pairs={{0,4},{2,0},{4,8},{6,2},{8,12},{10,6},{12,14},{14,10},{1,5},{3,1},... | collective-permute-start | bytes 1376264 | tf_op jit(solution)/shard_map/ppermute | solution.py:37
  63.6 22.8 %collective-permute-start.11 = (bf16[64,3584]{1,0:T(8,128)(2,1)S(1)}, bf16[64,3584]{1,0:T(8,128)(2,1)S(1)}, u32[]{:S(2)}, u32[]{:S(2)}) collective-permute-start(bf16[64,3584]{1,0:T(8,128)(2,1)S(1)} %payload.11.refs_3_.refs_4_), channel_id=1, source_target_pairs={{0,2},{2,6},{4,0},{6,10},{8,4},{10,14},{12,8},{14,12},{1,3},{3,7},... | collective-permute-start | bytes 1376264 | tf_op jit(solution)/shard_map/ppermute | solution.py:37
  63.9 2.0 %copy-start.2 = (f32[2,128,3584]{2,1,0:T(8,128)S(1)}, f32[2,128,3584]{2,1,0:T(8,128)}, u32[]{:S(2)}) copy-start(f32[2,128,3584]{2,1,0:T(8,128)} %copy-done.1) | copy-start | bytes 11010052
  65.9 2.7 %copy-start.3 = (f32[2,128,3584]{2,1,0:T(8,128)S(1)}, f32[2,128,3584]{2,1,0:T(8,128)}, u32[]{:S(2)}) copy-start(f32[2,128,3584]{2,1,0:T(8,128)} %copy-done.1) | copy-start | bytes 11010052
  66.8 21.9 %collective-permute-start.10 = (bf16[64,3584]{1,0:T(8,128)(2,1)S(1)}, bf16[64,3584]{1,0:T(8,128)(2,1)S(1)}, u32[]{:S(2)}, u32[]{:S(2)}) collective-permute-start(bf16[64,3584]{1,0:T(8,128)(2,1)S(1)} %payload.12.refs_4_), channel_id=1, source_target_pairs={{0,4},{2,0},{4,8},{6,2},{8,12},{10,6},{12,14},{14,10},{1,5},{3,1},... | collective-permute-start | bytes 1376264 | tf_op jit(solution)/shard_map/ppermute | solution.py:37
  69.5 21.9 %collective-permute-start.12 = (bf16[64,3584]{1,0:T(8,128)(2,1)S(1)}, bf16[64,3584]{1,0:T(8,128)(2,1)S(1)}, u32[]{:S(2)}, u32[]{:S(2)}) collective-permute-start(bf16[64,3584]{1,0:T(8,128)(2,1)S(1)} %payload.13.refs_2_), channel_id=1, source_target_pairs={{0,2},{2,6},{4,0},{6,10},{8,4},{10,14},{12,8},{14,12},{1,3},{3,7},... | collective-permute-start | bytes 1376264 | tf_op jit(solution)/shard_map/ppermute | solution.py:37
  83.1 8.4 %copy-start = (f32[2,256,3584]{2,1,0:T(8,128)}, f32[2,256,3584]{2,1,0:T(8,128)S(1)}, u32[]{:S(2)}) copy-start(f32[2,256,3584]{2,1,0:T(8,128)S(1)} %fusion.2.refs_2_.refs_3_.refs_15_) | copy-start | bytes 22020100
  83.1 2.1 %copy-start.13 = (bf16[64,3584]{1,0:T(8,128)(2,1)}, bf16[64,3584]{1,0:T(8,128)(2,1)S(1)}, u32[]{:S(2)}) copy-start(bf16[64,3584]{1,0:T(8,128)(2,1)S(1)} %collective-permute-done.8.refs_1_.refs_7_) | copy-start | bytes 1376260
  85.1 23.7 %collective-permute-start.14 = (bf16[64,3584]{1,0:T(8,128)(2,1)}, bf16[64,3584]{1,0:T(8,128)(2,1)}, u32[]{:S(2)}, u32[]{:S(2)}) collective-permute-start(bf16[64,3584]{1,0:T(8,128)(2,1)} %payload.14.refs_3_), channel_id=1, source_target_pairs={{0,4},{2,0},{4,8},{6,2},{8,12},{10,6},{12,14},{14,10},{1,5},{3,1},... | collective-permute-start | bytes 1376264 | tf_op jit(solution)/shard_map/ppermute | solution.py:37
  86.4 1.5 %copy-start.14 = (bf16[64,3584]{1,0:T(8,128)(2,1)}, bf16[64,3584]{1,0:T(8,128)(2,1)S(1)}, u32[]{:S(2)}) copy-start(bf16[64,3584]{1,0:T(8,128)(2,1)S(1)} %collective-permute-done.11.refs_1_.refs_9_) | copy-start | bytes 1376260
  87.9 25.8 %collective-permute-start.16 = (bf16[64,3584]{1,0:T(8,128)(2,1)}, bf16[64,3584]{1,0:T(8,128)(2,1)S(1)}, u32[]{:S(2)}, u32[]{:S(2)}) collective-permute-start(bf16[64,3584]{1,0:T(8,128)(2,1)} %payload.15.refs_3_), channel_id=1, source_target_pairs={{0,2},{2,6},{4,0},{6,10},{8,4},{10,14},{12,8},{14,12},{1,3},{3,7},... | collective-permute-start | bytes 1376264 | tf_op jit(solution)/shard_map/ppermute | solution.py:37
  88.7 1.5 %copy-start.15 = (bf16[64,3584]{1,0:T(8,128)(2,1)}, bf16[64,3584]{1,0:T(8,128)(2,1)S(1)}, u32[]{:S(2)}) copy-start(bf16[64,3584]{1,0:T(8,128)(2,1)S(1)} %collective-permute-done.10.refs_1_.refs_8_) | copy-start | bytes 1376260
  90.2 3.0 %copy-start.21 = (bf16[1,8,2048]{2,1,0:T(8,128)(2,1)S(1)}, bf16[1,8,2048]{2,1,0:T(8,128)(2,1)}, u32[]{:S(2)}) copy-start(bf16[1,8,2048]{2,1,0:T(8,128)(2,1)} %param.14) | copy-start | bytes 98308
  90.2 17.1 %collective-permute-start.15 = (bf16[64,3584]{1,0:T(8,128)(2,1)}, bf16[64,3584]{1,0:T(8,128)(2,1)}, u32[]{:S(2)}, u32[]{:S(2)}) collective-permute-start(bf16[64,3584]{1,0:T(8,128)(2,1)} %payload.16.refs_3_), channel_id=1, source_target_pairs={{0,4},{2,0},{4,8},{6,2},{8,12},{10,6},{12,14},{14,10},{1,5},{3,1},... | collective-permute-start | bytes 1376264 | tf_op jit(solution)/shard_map/ppermute | solution.py:37
  91.5 0.9 copy-start.16
  92.4 21.2 %collective-permute-start.17 = (bf16[64,3584]{1,0:T(8,128)(2,1)S(1)}, bf16[64,3584]{1,0:T(8,128)(2,1)}, u32[]{:S(2)}, u32[]{:S(2)}) collective-permute-start(bf16[64,3584]{1,0:T(8,128)(2,1)S(1)} %payload.17.refs_2_.after_ref), channel_id=1, source_target_pairs={{0,2},{2,6},{4,0},{6,10},{8,4},{10,14},{12,8},{14,12},{1,3},{3,7},... | collective-permute-start | bytes 1376264 | tf_op jit(solution)/shard_map/ppermute | solution.py:37
  93.8 0.6 copy-start.26
  93.8 10.5 %collective-permute-start.27 = (bf16[4,2048]{1,0:T(4,128)(2,1)S(1)}, bf16[4,2048]{1,0:T(4,128)(2,1)}, u32[]{:S(2)}, u32[]{:S(2)}) collective-permute-start(bf16[4,2048]{1,0:T(4,128)(2,1)S(1)} %dynamic-slice_bitcast_fusion.1), channel_id=1, source_target_pairs={{0,1},{1,0},{2,3},{3,2},{4,5},{5,4},{6,7},{7,6},{8,9},{9,8},{10,11... | collective-permute-start | bytes 49160 | tf_op jit(solution)/shard_map/ppermute | solution.py:42
  95.5 1.0 copy-start.18
  96.6 14.2 %copy-start.4 = (f32[2,128,3584]{2,1,0:T(8,128)S(1)}, f32[2,128,3584]{2,1,0:T(8,128)}, u32[]{:S(2)}) copy-start(f32[2,128,3584]{2,1,0:T(8,128)} %copy-done.1) | copy-start | bytes 11010052
  104.3 9.3 %copy-start.5 = (f32[2,128,3584]{2,1,0:T(8,128)}, f32[2,128,3584]{2,1,0:T(8,128)S(1)}, u32[]{:S(2)}) copy-start(f32[2,128,3584]{2,1,0:T(8,128)S(1)} %fusion.refs_4_.refs_16_) | copy-start | bytes 11010052
  106.1 22.5 %collective-permute-start.28 = (bf16[4,4096]{1,0:T(4,128)(2,1)}, bf16[4,4096]{1,0:T(4,128)(2,1)}, u32[]{:S(2)}, u32[]{:S(2)}) collective-permute-start(bf16[4,4096]{1,0:T(4,128)(2,1)} %pad_maximum_fusion.3), channel_id=1, source_target_pairs={{0,4},{4,8},{8,12},{12,0},{1,5},{5,9},{9,13},{13,1},{2,6},{6,10},{... | collective-permute-start | bytes 98312 | tf_op jit(solution)/shard_map/ppermute | solution.py:42
  107.3 22.7 %collective-permute-start.29 = (bf16[4,4096]{1,0:T(4,128)(2,1)}, bf16[4,4096]{1,0:T(4,128)(2,1)}, u32[]{:S(2)}, u32[]{:S(2)}) collective-permute-start(bf16[4,4096]{1,0:T(4,128)(2,1)} %pad_maximum_fusion.3), channel_id=1, source_target_pairs={{0,8},{4,12},{8,0},{12,4},{1,9},{5,13},{9,1},{13,5},{2,10},{6,14},... | collective-permute-start | bytes 98312 | tf_op jit(solution)/shard_map/ppermute | solution.py:42
  108.9 21.9 %collective-permute-start.30 = (bf16[4,4096]{1,0:T(4,128)(2,1)}, bf16[4,4096]{1,0:T(4,128)(2,1)}, u32[]{:S(2)}, u32[]{:S(2)}) collective-permute-start(bf16[4,4096]{1,0:T(4,128)(2,1)} %pad_maximum_fusion.3), channel_id=1, source_target_pairs={{0,12},{4,0},{8,4},{12,8},{1,13},{5,1},{9,5},{13,9},{2,14},{6,2},{... | collective-permute-start | bytes 98312 | tf_op jit(solution)/shard_map/ppermute | solution.py:42
  113.6 27.3 %collective-permute-start.23 = (bf16[128,3584]{1,0:T(8,128)(2,1)}, bf16[128,3584]{1,0:T(8,128)(2,1)S(1)}, u32[]{:S(2)}, u32[]{:S(2)}) collective-permute-start(bf16[128,3584]{1,0:T(8,128)(2,1)} %payload.18.refs_4_), channel_id=1, source_target_pairs={{0,4},{2,0},{4,8},{6,2},{8,12},{10,6},{12,14},{14,10},{1,5},{3,1},... | collective-permute-start | bytes 2752520 | tf_op jit(solution)/shard_map/ppermute | solution.py:37
  113.7 1.8 %copy-start.12 = (bf16[64,3584]{1,0:T(8,128)(2,1)}, bf16[64,3584]{1,0:T(8,128)(2,1)S(1)}, u32[]{:S(2)}) copy-start(bf16[64,3584]{1,0:T(8,128)(2,1)S(1)} %collective-permute-done.16.refs_1_.refs_13_) | copy-start | bytes 1376260
  115.6 2.0 %copy-start.10 = (bf16[128,3584]{1,0:T(8,128)(2,1)}, bf16[128,3584]{1,0:T(8,128)(2,1)S(1)}, u32[]{:S(2)}) copy-start(bf16[128,3584]{1,0:T(8,128)(2,1)S(1)} %payload.19.refs_17_) | copy-start | bytes 2752516
  115.6 25.2 %collective-permute-start.24 = (bf16[128,3584]{1,0:T(8,128)(2,1)S(1)}, bf16[128,3584]{1,0:T(8,128)(2,1)S(1)}, u32[]{:S(2)}, u32[]{:S(2)}) collective-permute-start(bf16[128,3584]{1,0:T(8,128)(2,1)S(1)} %payload.19.refs_17_), channel_id=1, source_target_pairs={{0,2},{2,6},{4,0},{6,10},{8,4},{10,14},{12,8},{14,12},{1,3},{3,7},... | collective-permute-start | bytes 2752520 | tf_op jit(solution)/shard_map/ppermute | solution.py:37
  117.6 15.3 %copy-start.19 = (bf16[256,2048]{1,0:T(8,128)(2,1)S(1)}, bf16[256,2048]{1,0:T(8,128)(2,1)}, u32[]{:S(2)}) copy-start(bf16[256,2048]{1,0:T(8,128)(2,1)} %x_ref.1) | copy-start | bytes 3145732
  117.6 15.3 %copy-start.20 = (bf16[2048,64]{0,1:T(8,128)(2,1)S(1)}, bf16[2048,64]{0,1:T(8,128)(2,1)}, u32[]{:S(2)}) copy-start(bf16[2048,64]{0,1:T(8,128)(2,1)} %param.12) | copy-start | bytes 786436
  117.6 23.3 %copy-start.24 = (bf16[256,3584]{1,0:T(8,128)(2,1)S(1)}, bf16[256,3584]{1,0:T(8,128)(2,1)}, u32[]{:S(2)}) copy-start(bf16[256,3584]{1,0:T(8,128)(2,1)} %refs_1_.1) | copy-start | bytes 5505028
  117.6 23.3 %copy-start.25 = (bf16[3584,64]{0,1:T(8,128)(2,1)S(1)}, bf16[3584,64]{0,1:T(8,128)(2,1)}, u32[]{:S(2)}) copy-start(bf16[3584,64]{0,1:T(8,128)(2,1)} %param.13) | copy-start | bytes 1376260
  128.7 9.7 %collective-permute-start.20 = (f32[64,128]{1,0:T(8,128)S(1)}, f32[64,128]{1,0:T(8,128)S(1)}, u32[]{:S(2)}, u32[]{:S(2)}) collective-permute-start(f32[64,128]{1,0:T(8,128)S(1)} %get-tuple-element.9), channel_id=1, source_target_pairs={{0,12},{4,0},{8,4},{12,8},{1,13},{5,1},{9,5},{13,9},{2,14},{6,2},{... | collective-permute-start | bytes 98312 | tf_op jit(solution)/shard_map/ppermute | solution.py:42
  130.1 10.6 %collective-permute-start.21 = (f32[64,128]{1,0:T(8,128)S(1)}, f32[64,128]{1,0:T(8,128)S(1)}, u32[]{:S(2)}, u32[]{:S(2)}) collective-permute-start(f32[64,128]{1,0:T(8,128)S(1)} %get-tuple-element.11), channel_id=1, source_target_pairs={{0,8},{4,12},{8,0},{12,4},{1,9},{5,13},{9,1},{13,5},{2,10},{6,14},... | collective-permute-start | bytes 98312 | tf_op jit(solution)/shard_map/ppermute | solution.py:42
  130.8 9.9 %collective-permute-start.22 = (f32[64,128]{1,0:T(8,128)S(1)}, f32[64,128]{1,0:T(8,128)S(1)}, u32[]{:S(2)}, u32[]{:S(2)}) collective-permute-start(f32[64,128]{1,0:T(8,128)S(1)} %get-tuple-element.10), channel_id=1, source_target_pairs={{0,4},{4,8},{8,12},{12,0},{1,5},{5,9},{9,13},{13,1},{2,6},{6,10},{... | collective-permute-start | bytes 98312 | tf_op jit(solution)/shard_map/ppermute | solution.py:42
  132.9 0.9 copy-start.17
  138.4 2.3 %collective-permute-start.18 = (f32[256,64]{1,0:T(8,128)S(1)}, f32[256,64]{1,0:T(8,128)S(1)}, u32[]{:S(2)}, u32[]{:S(2)}) collective-permute-start(f32[256,64]{1,0:T(8,128)S(1)} %projected_inputs.1), channel_id=1, source_target_pairs={{0,1},{1,0},{2,3},{3,2},{4,5},{5,4},{6,7},{7,6},{8,9},{9,8},{10,11... | collective-permute-start | bytes 196616 | tf_op jit(solution)/shard_map/ppermute | solution.py:59
  140.7 5.0 %collective-permute-start.19 = (f32[256,64]{1,0:T(8,128)S(1)}, f32[256,64]{1,0:T(8,128)S(1)}, u32[]{:S(2)}, u32[]{:S(2)}) collective-permute-start(f32[256,64]{1,0:T(8,128)S(1)} %add.185), channel_id=1, source_target_pairs={{0,2},{2,0},{1,3},{3,1},{4,6},{6,4},{5,7},{7,5},{8,10},{10,8},{9,1... | collective-permute-start | bytes 196616 | tf_op jit(solution)/shard_map/ppermute | solution.py:59
  143.3 2.5 %collective-permute-start.25 = (f32[64,256]{1,0:T(8,128)S(1)}, f32[64,256]{1,0:T(8,128)S(1)}, u32[]{:S(2)}, u32[]{:S(2)}) collective-permute-start(f32[64,256]{1,0:T(8,128)S(1)} %pad_maximum_fusion.2), channel_id=1, source_target_pairs={{0,1},{1,0},{2,3},{3,2},{4,5},{5,4},{6,7},{7,6},{8,9},{9,8},{10,11... | collective-permute-start | bytes 196616 | tf_op jit(solution)/shard_map/ppermute | solution.py:59
  145.9 4.3 %collective-permute-start.26 = (f32[64,256]{1,0:T(8,128)S(1)}, f32[64,256]{1,0:T(8,128)S(1)}, u32[]{:S(2)}, u32[]{:S(2)}) collective-permute-start(f32[64,256]{1,0:T(8,128)S(1)} %fusion.32), channel_id=1, source_target_pairs={{0,2},{2,0},{1,3},{3,1},{4,6},{6,4},{5,7},{7,5},{8,10},{10,8},{9,1... | collective-permute-start | bytes 196616 | tf_op jit(solution)/shard_map/ppermute | solution.py:59

commit v5 on v4

--- a/solution.py
+++ b/solution.py
@@ -176,7 +176,7 @@
 def payload(scalars, got, parts, hidden, rows_at, *after):
     part, hid = got[0].shape
     rows = part * parts
-    step = block_of(hid, 1792)
+    step = block_of(hid, 3584)
     grid_spec = pltpu.PrefetchScalarGridSpec(
         num_scalar_prefetch=1,
         grid=(hid // step,),

time: 154 us -> 153 us (level)
  transfers between devices with their start and end apart: 31 -> 31, of which waited for: 8 -> 9; matrix products, arithmetic and copies ran while one was open for 23% -> 23% of each run, Pallas kernels for 19% -> 18%
where the time goes in v5:
time: 153 us; the launch traced here: 152 us
  waiting for transfers between devices  40.2 us (26%)
  starting transfers between devices  37 us (24%)
  matrix products  30.3 us (20%)
  Pallas kernels  29.1 us (19%)
  local copies, waits for them, and re-layouts  10.2 us (7%)
  other arithmetic  3.61 us (2%)
  between operations  1.58 us (1%)
    dot_general x3, matrix products, hidden_grad(): lax.dot_general(stacked.reshape(-1, depth), w_down, ROWS_ROWS, preferred_...  26.3 us
    pallas_call x10, Pallas kernels, payload(): pl.pallas_call(kernel, grid_spec=grid_spec, out_shape=jax.ShapeDtypeStruc...  12.9 us
    ppermute x11, starting transfers between devices, shifted(): lax.ppermute(block, axis, [(i, (i + distance) % n) for i in range(n)])  11.5 us
    ppermute x10, starting transfers between devices, onward(): return lax.ppermute(block, ('blk', 'fsdp'), route)  11.2 us
    pallas_call x1, Pallas kernels, projected_first(): pl.pallas_call(kernel, grid_spec=grid_spec, out_shape=jax.ShapeDtypeStruc...  10.3 us
    ppermute x2, waiting for transfers between devices, line_left(): return lax.ppermute(block, 'blk', [(i + 1, i) for i in range(n - 1)])  10.2 us
    ppermute x2, waiting for transfers between devices, features(): return lax.ppermute(mine, ('blk', 'sub'), route)  9.36 us
    ppermute x2, waiting for transfers between devices, line_right(): return lax.ppermute(block, 'blk', [(i, i + 1) for i in range(n - 1)])  8.79 us
  transfers between devices with their start and end apart: 31, of which 9 were waited for; matrix products, arithmetic and copies ran while one was open for 23% of the time, Pallas kernels for 18%

profile of v5, /device:TPU:0, one launch (start us, length us, event | category | flops | bytes accessed | tf_op | source)
XLA Modules:
  0.0 151.9 jit_solution(12309172544129532360)
XLA Ops:
  0.7 1.4 fusion.33
  2.1 3.1 %collective-permute-start.4 = (bf16[128,2048]{1,0:T(8,128)(2,1)S(1)}, bf16[128,2048]{1,0:T(8,128)(2,1)S(1)}, u32[]{:S(2)}, u32[]{:S(2)}) collective-permute-start(bf16[128,2048]{1,0:T(8,128)(2,1)S(1)} %get-tuple-element.3), channel_id=1, source_target_pairs={{0,4},{1,12},{4,0},{5,8},{8,5},{9,13},{12,1},{13,9},{2,6},{3,14},{... | collective-permute-start | bytes 1572872 | tf_op jit(solution)/shard_map/ppermute | solution.py:303
  5.2 1.4 collective-permute-start.6
  6.6 9.4 %collective-permute-done.4.refs_1_ = bf16[128,2048]{1,0:T(8,128)(2,1)S(1)} collective-permute-done((bf16[128,2048]{1,0:T(8,128)(2,1)S(1)}, bf16[128,2048]{1,0:T(8,128)(2,1)S(1)}, u32[]{:S(2)}, u32[]{:S(2)}) %collective-permute-start.4) | collective-permute-done | bytes 524320 | tf_op jit(solution)/shard_map/ppermute | solution.py:303
  16.0 2.4 %collective-permute-start.5 = (bf16[128,2048]{1,0:T(8,128)(2,1)S(1)}, bf16[128,2048]{1,0:T(8,128)(2,1)S(1)}, u32[]{:S(2)}, u32[]{:S(2)}) collective-permute-start(bf16[128,2048]{1,0:T(8,128)(2,1)S(1)} %collective-permute-done.4.refs_1_), channel_id=1, source_target_pairs={{0,2},{2,0},{1,3},{3,1},{4,6},{6,4},{5,7},{7,5},{8,10},{10,8},{9,1... | collective-permute-start | bytes 1572872 | tf_op jit(solution)/shard_map/ppermute | solution.py:42
  18.3 0.9 fusion.34
  19.2 3.7 %collective-permute-start = (bf16[64,3584]{1,0:T(8,128)(2,1)S(1)}, bf16[64,3584]{1,0:T(8,128)(2,1)S(1)}, u32[]{:S(2)}, u32[]{:S(2)}) collective-permute-start(bf16[64,3584]{1,0:T(8,128)(2,1)S(1)} %get-tuple-element.5), channel_id=1, source_target_pairs={{0,4},{4,8},{8,12},{1,5},{5,9},{9,13},{2,6},{6,10},{10,14},{3,7},{... | collective-permute-start | bytes 1376264 | tf_op jit(solution)/shard_map/ppermute | solution.py:22
  22.9 1.3 collective-permute-start.2
  24.2 8.8 %collective-permute-done.refs_3_.refs_1_ = bf16[64,3584]{1,0:T(8,128)(2,1)S(1)} collective-permute-done((bf16[64,3584]{1,0:T(8,128)(2,1)S(1)}, bf16[64,3584]{1,0:T(8,128)(2,1)S(1)}, u32[]{:S(2)}, u32[]{:S(2)}) %collective-permute-start) | collective-permute-done | bytes 458784 | tf_op jit(solution)/shard_map/ppermute | solution.py:22
  33.0 7.0 %collective-permute-done.2.refs_4_.refs_2_.refs_5_ = bf16[64,3584]{1,0:T(8,128)(2,1)S(1)} collective-permute-done((bf16[64,3584]{1,0:T(8,128)(2,1)S(1)}, bf16[64,3584]{1,0:T(8,128)(2,1)S(1)}, u32[]{:S(2)}, u32[]{:S(2)}) %collective-permute-start.2) | collective-permute-done | bytes 458784 | tf_op jit(solution)/shard_map/ppermute | solution.py:27
  40.2 2.5 %collective-permute-start.1 = (bf16[64,3584]{1,0:T(8,128)(2,1)}, bf16[64,3584]{1,0:T(8,128)(2,1)S(1)}, u32[]{:S(2)}, u32[]{:S(2)}) collective-permute-start(bf16[64,3584]{1,0:T(8,128)(2,1)} %get-tuple-element.4), channel_id=1, source_target_pairs={{0,4},{4,8},{8,12},{1,5},{5,9},{9,13},{2,6},{6,10},{10,14},{3,7},{... | collective-permute-start | bytes 1376264 | tf_op jit(solution)/shard_map/ppermute | solution.py:22
  42.7 1.3 collective-permute-start.3
  44.4 1.5 collective-permute-start.9
  45.9 1.1 stack.249
  47.0 7.3 %fusion.4.refs_3_ = f32[2,128,3584]{2,1,0:T(8,128)S(1)} fusion(bf16[2,128,2048]{2,1,0:T(8,128)(2,1)S(1)} %stack.249, bf16[3584,2048]{1,0:T(8,128)(2,1)} %param.11), kind=kOutput, calls=%fused_computation.4 | convolution fusion | flops 3758096384 | bytes 19398656 | tf_op jit(solution)/shard_map/dot_general | solution.py:101
  54.3 3.1 %collective-permute-done.3.refs_5_.refs_2_.refs_6_ = bf16[64,3584]{1,0:T(8,128)(2,1)S(1)} collective-permute-done((bf16[64,3584]{1,0:T(8,128)(2,1)}, bf16[64,3584]{1,0:T(8,128)(2,1)S(1)}, u32[]{:S(2)}, u32[]{:S(2)}) %collective-permute-start.3) | collective-permute-done | bytes 458784 | tf_op jit(solution)/shard_map/ppermute | solution.py:27
  57.4 0.7 payload.10.refs_4_
  58.2 0.7 payload.11.refs_3_.refs_4_
  59.0 1.3 join.3.refs_5_.refs_0_
  60.9 0.6 stack.199.refs_0_
  61.5 2.1 %collective-permute-start.8 = (bf16[64,3584]{1,0:T(8,128)(2,1)}, bf16[64,3584]{1,0:T(8,128)(2,1)S(1)}, u32[]{:S(2)}, u32[]{:S(2)}) collective-permute-start(bf16[64,3584]{1,0:T(8,128)(2,1)} %copy-done.11), channel_id=1, source_target_pairs={{0,4},{2,0},{4,8},{6,2},{8,12},{10,6},{12,14},{14,10},{1,5},{3,1},... | collective-permute-start | bytes 1376264 | tf_op jit(solution)/shard_map/ppermute | solution.py:37
  63.6 2.0 %copy-done.2 = f32[2,128,3584]{2,1,0:T(8,128)S(1)} copy-done((f32[2,128,3584]{2,1,0:T(8,128)S(1)}, f32[2,128,3584]{2,1,0:T(8,128)}, u32[]{:S(2)}) %copy-start.2) | copy-done | bytes 3670040
  65.6 0.7 payload.12.refs_4_
  66.3 2.0 %collective-permute-start.10 = (bf16[64,3584]{1,0:T(8,128)(2,1)S(1)}, bf16[64,3584]{1,0:T(8,128)(2,1)S(1)}, u32[]{:S(2)}, u32[]{:S(2)}) collective-permute-start(bf16[64,3584]{1,0:T(8,128)(2,1)S(1)} %payload.12.refs_4_), channel_id=1, source_target_pairs={{0,4},{2,0},{4,8},{6,2},{8,12},{10,6},{12,14},{14,10},{1,5},{3,1},... | collective-permute-start | bytes 1376264 | tf_op jit(solution)/shard_map/ppermute | solution.py:37
  68.4 0.7 payload.13.refs_2_
  69.0 0.9 collective-permute-start.12
  69.9 1.4 stack.250
  71.3 11.3 %fusion.2.refs_2_.refs_3_.refs_15_ = f32[2,256,3584]{2,1,0:T(8,128)S(1)} fusion(bf16[2,256,2048]{2,1,0:T(8,128)(2,1)S(1)} %stack.250, bf16[3584,2048]{1,0:T(8,128)(2,1)} %param.11), kind=kOutput, calls=%fused_computation.2 | convolution fusion | flops 7516192768 | bytes 24117248 | tf_op jit(solution)/shard_map/dot_general | solution.py:101
  82.6 1.9 %payload.14.refs_3_ = bf16[64,3584]{1,0:T(8,128)(2,1)} custom-call(s32[5]{0:T(128)S(1)} %stack.218.refs_0_, bf16[64,3584]{1,0:T(8,128)(2,1)S(1)} %collective-permute-done.8.refs_1_.refs_7_, f32[2,256,3584]{2,1,0:T(8,128)S(1)} %fusion.2.refs_2_.refs_3_.refs_15_, f32[2,256,3584]{2,1,0:T(8,128)S(1)} %fusion.2.refs_2_.refs_3_.refs_15_), custom_call_target="tpu_custom_call" | custom-call | flops 1000 | bytes 1000 | tf_op jit(solution)/shard_map/payload/pallas_call | solution.py:195
  84.5 1.2 collective-permute-start.14
  85.7 1.4 payload.15.refs_3_
  87.2 0.9 collective-permute-start.16
  88.0 1.4 payload.16.refs_3_
  89.5 1.2 collective-permute-start.15
  90.6 0.7 payload.17.refs_2_.after_ref
  91.4 0.9 collective-permute-start.17
  92.3 0.5 block_copy.1
  93.5 1.1 stack.251
  94.6 1.0 copy-done.18
  95.6 7.7 %fusion.refs_4_.refs_16_ = f32[2,128,3584]{2,1,0:T(8,128)S(1)} fusion(bf16[2,128,2048]{2,1,0:T(8,128)(2,1)} %copy-done.18, bf16[3584,2048]{1,0:T(8,128)(2,1)} %param.11), kind=kOutput, calls=%fused_computation | convolution fusion | flops 3758096384 | bytes 19398656 | tf_op jit(solution)/shard_map/dot_general | solution.py:101
  103.4 0.8 bitcast_select_fusion.1
  104.2 1.0 pad_maximum_fusion.3
  105.2 1.2 collective-permute-start.28
  106.8 1.7 %collective-permute-start.29 = (bf16[4,4096]{1,0:T(4,128)(2,1)}, bf16[4,4096]{1,0:T(4,128)(2,1)}, u32[]{:S(2)}, u32[]{:S(2)}) collective-permute-start(bf16[4,4096]{1,0:T(4,128)(2,1)} %pad_maximum_fusion.3), channel_id=1, source_target_pairs={{0,8},{4,12},{8,0},{12,4},{1,9},{5,13},{9,1},{13,5},{2,10},{6,14},... | collective-permute-start | bytes 98312 | tf_op jit(solution)/shard_map/ppermute | solution.py:42
  108.5 1.5 %collective-permute-start.30 = (bf16[4,4096]{1,0:T(4,128)(2,1)}, bf16[4,4096]{1,0:T(4,128)(2,1)}, u32[]{:S(2)}, u32[]{:S(2)}) collective-permute-start(bf16[4,4096]{1,0:T(4,128)(2,1)} %pad_maximum_fusion.3), channel_id=1, source_target_pairs={{0,12},{4,0},{8,4},{12,8},{1,13},{5,1},{9,5},{13,9},{2,14},{6,2},{... | collective-permute-start | bytes 98312 | tf_op jit(solution)/shard_map/ppermute | solution.py:42
  110.0 3.0 %payload.18.refs_4_ = bf16[128,3584]{1,0:T(8,128)(2,1)} custom-call(s32[5]{0:T(128)S(1)} %stack.229.refs_0_, bf16[64,3584]{1,0:T(8,128)(2,1)} %collective-permute-done.14.refs_1_.refs_11_, bf16[64,3584]{1,0:T(8,128)(2,1)} %collective-permute-done.15.refs_2_.refs_12_, f32[2,128,3584]{2,1,0:T(8,128)S(1)} %copy-done.4, f32[2,128,3584]{2,1,0:T(8,128)S(1)} %fusion.refs_4_.refs_16_), custom_call_target="tpu_custom_call" | custom-call | flops 1000 | bytes 1000 | tf_op jit(solution)/shard_map/payload/pallas_call | solution.py:195
  113.5 1.8 %payload.19.refs_17_ = bf16[128,3584]{1,0:T(8,128)(2,1)S(1)} custom-call(s32[5]{0:T(128)S(1)} %stack.225.refs_0_, bf16[64,3584]{1,0:T(8,128)(2,1)S(1)} %collective-permute-done.16.refs_1_.refs_13_, bf16[64,3584]{1,0:T(8,128)(2,1)} %collective-permute-done.17.refs_2_.refs_14_, f32[2,128,3584]{2,1,0:T(8,128)S(1)} %copy-done.4, bf16[128,3584]{1,0:T(8,128)(2,1)} %payload.18.refs_4_), custom_call_target="tpu_custom_call" | custom-call | flops 1000 | bytes 1000 | tf_op jit(solution)/shard_map/payload/pallas_call | solution.py:195
  115.3 1.6 %collective-permute-start.24 = (bf16[128,3584]{1,0:T(8,128)(2,1)S(1)}, bf16[128,3584]{1,0:T(8,128)(2,1)S(1)}, u32[]{:S(2)}, u32[]{:S(2)}) collective-permute-start(bf16[128,3584]{1,0:T(8,128)(2,1)S(1)} %payload.19.refs_17_), channel_id=1, source_target_pairs={{0,2},{2,6},{4,0},{6,10},{8,4},{10,14},{12,8},{14,12},{1,3},{3,7},... | collective-permute-start | bytes 2752520 | tf_op jit(solution)/shard_map/ppermute | solution.py:37
  116.9 10.3 %projected_first.1.after_ref = f32[4,64,128]{2,1,0:T(8,128)} custom-call(s32[8]{0:T(128)} %stack.199.refs_0_, bf16[256,3584]{1,0:T(8,128)(2,1)} %refs_1_.1, bf16[64,3584]{1,0:T(8,128)(2,1)} %bitcast.81, bf16[64,3584]{1,0:T(8,128)(2,1)} %copy-done.8, bf16[64,3584]{1,0:T(8,128)(2,1)} %copy-done.6, bf16[64,3584]{1,0:T(8,128)(2,1)} %copy-done.9, ...), custom_call_target="tpu_custom_call" | custom-call | flops 1000 | bytes 59040000 | tf_op jit(solution)/shard_map/projected_first/pallas_call | solution.py:255
  127.2 0.8 slice_bitcast_fusion.2
  128.0 1.8 %collective-permute-start.20 = (f32[64,128]{1,0:T(8,128)S(1)}, f32[64,128]{1,0:T(8,128)S(1)}, u32[]{:S(2)}, u32[]{:S(2)}) collective-permute-start(f32[64,128]{1,0:T(8,128)S(1)} %get-tuple-element.9), channel_id=1, source_target_pairs={{0,12},{4,0},{8,4},{12,8},{1,13},{5,1},{9,5},{13,9},{2,14},{6,2},{... | collective-permute-start | bytes 98312 | tf_op jit(solution)/shard_map/ppermute | solution.py:42
  130.0 1.1 collective-permute-start.22
  131.1 0.9 select_bitcast_fusion.3
  132.0 0.9 copy-done.17
  133.3 4.3 %collective-permute-done.20 = f32[64,128]{1,0:T(8,128)S(1)} collective-permute-done((f32[64,128]{1,0:T(8,128)S(1)}, f32[64,128]{1,0:T(8,128)S(1)}, u32[]{:S(2)}, u32[]{:S(2)}) %collective-permute-start.20) | collective-permute-done | bytes 32800 | tf_op jit(solution)/shard_map/ppermute | solution.py:42
  137.7 2.2 %collective-permute-done.21 = f32[64,128]{1,0:T(8,128)S(1)} collective-permute-done((f32[64,128]{1,0:T(8,128)S(1)}, f32[64,128]{1,0:T(8,128)S(1)}, u32[]{:S(2)}, u32[]{:S(2)}) %collective-permute-start.21) | collective-permute-done | bytes 32800 | tf_op jit(solution)/shard_map/ppermute | solution.py:42
  140.0 2.5 %fusion.16 = f32[64,128]{1,0:T(8,128)S(1)} fusion(bf16[3584,64]{0,1:T(8,128)(2,1)S(1)} %copy-done.25, f32[2,256,3584]{2,1,0:T(8,128)} %copy-done, s32[]{:T(128)S(6)} %select_n.436, s32[]{:T(128)S(6)} %add.202, bf16[128,3584]{1,0:T(8,128)(2,1)S(1)} %collective-permute-done.24, bf16[128,3584]{1,0:T(8,128)(2,1)S(1)} %collective-permute-done.23, ...), kind=kOutput, calls=%fused_computation.17 | convolution fusion | flops 179830784 | bytes 5079050 | tf_op jit(solution)/shard_map/dot_general | solution.py:421
  142.6 0.8 select_bitcast_fusion.2
  143.4 1.5 collective-permute-done.19
  145.0 0.8 collective-permute-start.26
  145.9 3.4 %collective-permute-done.26 = f32[64,256]{1,0:T(8,128)S(1)} collective-permute-done((f32[64,256]{1,0:T(8,128)S(1)}, f32[64,256]{1,0:T(8,128)S(1)}, u32[]{:S(2)}, u32[]{:S(2)}) %collective-permute-start.26) | collective-permute-done | bytes 65568 | tf_op jit(solution)/shard_map/ppermute | solution.py:59
  149.4 0.6 convolution_convert_fusion
  150.5 0.6 constant_dynamic-slice_fusion
  151.1 0.8 fusion.23
  (105 shorter events, 4.2 us)
Async XLA Ops:
  0.6 17.7 %copy-start.23 = (bf16[256,3584]{1,0:T(8,128)(2,1)S(1)}, bf16[256,3584]{1,0:T(8,128)(2,1)}, u32[]{:S(2)}) copy-start(bf16[256,3584]{1,0:T(8,128)(2,1)} %refs_1_.1) | copy-start | bytes 5505028
  2.1 13.9 %collective-permute-start.4 = (bf16[128,2048]{1,0:T(8,128)(2,1)S(1)}, bf16[128,2048]{1,0:T(8,128)(2,1)S(1)}, u32[]{:S(2)}, u32[]{:S(2)}) collective-permute-start(bf16[128,2048]{1,0:T(8,128)(2,1)S(1)} %get-tuple-element.3), channel_id=1, source_target_pairs={{0,4},{1,12},{4,0},{5,8},{8,5},{9,13},{12,1},{13,9},{2,6},{3,14},{... | collective-permute-start | bytes 1572872 | tf_op jit(solution)/shard_map/ppermute | solution.py:303
  5.2 34.9 %collective-permute-start.6 = (bf16[128,2048]{1,0:T(8,128)(2,1)S(1)}, bf16[128,2048]{1,0:T(8,128)(2,1)}, u32[]{:S(2)}, u32[]{:S(2)}) collective-permute-start(bf16[128,2048]{1,0:T(8,128)(2,1)S(1)} %get-tuple-element.2), channel_id=1, source_target_pairs={{0,0},{1,8},{4,4},{5,12},{8,1},{9,9},{12,5},{13,13},{2,2},{3,10},{... | collective-permute-start | bytes 1572872 | tf_op jit(solution)/shard_map/ppermute | solution.py:303
  16.0 24.1 %collective-permute-start.5 = (bf16[128,2048]{1,0:T(8,128)(2,1)S(1)}, bf16[128,2048]{1,0:T(8,128)(2,1)S(1)}, u32[]{:S(2)}, u32[]{:S(2)}) collective-permute-start(bf16[128,2048]{1,0:T(8,128)(2,1)S(1)} %collective-permute-done.4.refs_1_), channel_id=1, source_target_pairs={{0,2},{2,0},{1,3},{3,1},{4,6},{6,4},{5,7},{7,5},{8,10},{10,8},{9,1... | collective-permute-start | bytes 1572872 | tf_op jit(solution)/shard_map/ppermute | solution.py:42
  19.2 26.6 %copy-start.22 = (s32[256]{0:T(256)S(1)}, s32[256]{0:T(256)}, u32[]{:S(2)}) copy-start(s32[256]{0:T(256)} %refs_2_.1) | copy-start | bytes 3076
  19.2 13.8 %collective-permute-start = (bf16[64,3584]{1,0:T(8,128)(2,1)S(1)}, bf16[64,3584]{1,0:T(8,128)(2,1)S(1)}, u32[]{:S(2)}, u32[]{:S(2)}) collective-permute-start(bf16[64,3584]{1,0:T(8,128)(2,1)S(1)} %get-tuple-element.5), channel_id=1, source_target_pairs={{0,4},{4,8},{8,12},{1,5},{5,9},{9,13},{2,6},{6,10},{10,14},{3,7},{... | collective-permute-start | bytes 1376264 | tf_op jit(solution)/shard_map/ppermute | solution.py:22
  22.9 17.1 %collective-permute-start.2 = (bf16[64,3584]{1,0:T(8,128)(2,1)S(1)}, bf16[64,3584]{1,0:T(8,128)(2,1)S(1)}, u32[]{:S(2)}, u32[]{:S(2)}) collective-permute-start(bf16[64,3584]{1,0:T(8,128)(2,1)S(1)} %get-tuple-element.5), channel_id=1, source_target_pairs={{4,0},{8,4},{12,8},{5,1},{9,5},{13,9},{6,2},{10,6},{14,10},{7,3},{... | collective-permute-start | bytes 1376264 | tf_op jit(solution)/shard_map/ppermute | solution.py:27
  33.0 25.2 %copy-start.8 = (bf16[64,3584]{1,0:T(8,128)(2,1)}, bf16[64,3584]{1,0:T(8,128)(2,1)S(1)}, u32[]{:S(2)}) copy-start(bf16[64,3584]{1,0:T(8,128)(2,1)S(1)} %collective-permute-done.refs_3_.refs_1_) | copy-start | bytes 1376260
  40.0 18.1 %copy-start.9 = (bf16[64,3584]{1,0:T(8,128)(2,1)}, bf16[64,3584]{1,0:T(8,128)(2,1)S(1)}, u32[]{:S(2)}) copy-start(bf16[64,3584]{1,0:T(8,128)(2,1)S(1)} %collective-permute-done.2.refs_4_.refs_2_.refs_5_) | copy-start | bytes 1376260
  40.1 5.7 %collective-permute-start.7 = (bf16[256,2048]{1,0:T(8,128)(2,1)S(1)}, bf16[256,2048]{1,0:T(8,128)(2,1)}, u32[]{:S(2)}, u32[]{:S(2)}) collective-permute-start(bf16[256,2048]{1,0:T(8,128)(2,1)S(1)} %join.2.refs_0_), channel_id=1, source_target_pairs={{0,1},{1,0},{2,3},{3,2},{4,5},{5,4},{6,7},{7,6},{8,9},{9,8},{10,11... | collective-permute-start | bytes 3145736 | tf_op jit(solution)/shard_map/ppermute | solution.py:42
  40.2 14.1 %collective-permute-start.1 = (bf16[64,3584]{1,0:T(8,128)(2,1)}, bf16[64,3584]{1,0:T(8,128)(2,1)S(1)}, u32[]{:S(2)}, u32[]{:S(2)}) collective-permute-start(bf16[64,3584]{1,0:T(8,128)(2,1)} %get-tuple-element.4), channel_id=1, source_target_pairs={{0,4},{4,8},{8,12},{1,5},{5,9},{9,13},{2,6},{6,10},{10,14},{3,7},{... | collective-permute-start | bytes 1376264 | tf_op jit(solution)/shard_map/ppermute | solution.py:22
  42.7 14.7 %collective-permute-start.3 = (bf16[64,3584]{1,0:T(8,128)(2,1)}, bf16[64,3584]{1,0:T(8,128)(2,1)S(1)}, u32[]{:S(2)}, u32[]{:S(2)}) collective-permute-start(bf16[64,3584]{1,0:T(8,128)(2,1)} %get-tuple-element.4), channel_id=1, source_target_pairs={{4,0},{8,4},{12,8},{5,1},{9,5},{13,9},{6,2},{10,6},{14,10},{7,3},{... | collective-permute-start | bytes 1376264 | tf_op jit(solution)/shard_map/ppermute | solution.py:27
  44.4 14.6 %collective-permute-start.9 = (bf16[128,2048]{1,0:T(8,128)(2,1)}, bf16[128,2048]{1,0:T(8,128)(2,1)}, u32[]{:S(2)}, u32[]{:S(2)}) collective-permute-start(bf16[128,2048]{1,0:T(8,128)(2,1)} %collective-permute-done.6.refs_5_.refs_1_), channel_id=1, source_target_pairs={{0,2},{2,0},{1,3},{3,1},{4,6},{6,4},{5,7},{7,5},{8,10},{10,8},{9,1... | collective-permute-start | bytes 1572872 | tf_op jit(solution)/shard_map/ppermute | solution.py:42
  54.3 3.9 %copy-start.1 = (f32[2,128,3584]{2,1,0:T(8,128)}, f32[2,128,3584]{2,1,0:T(8,128)S(1)}, u32[]{:S(2)}) copy-start(f32[2,128,3584]{2,1,0:T(8,128)S(1)} %fusion.4.refs_3_) | copy-start | bytes 11010052
  54.3 14.1 %copy-start.6 = (bf16[64,3584]{1,0:T(8,128)(2,1)}, bf16[64,3584]{1,0:T(8,128)(2,1)S(1)}, u32[]{:S(2)}) copy-start(bf16[64,3584]{1,0:T(8,128)(2,1)S(1)} %collective-permute-done.1.refs_4_.refs_1_) | copy-start | bytes 1376260
  57.4 10.9 %copy-start.7 = (bf16[64,3584]{1,0:T(8,128)(2,1)}, bf16[64,3584]{1,0:T(8,128)(2,1)S(1)}, u32[]{:S(2)}) copy-start(bf16[64,3584]{1,0:T(8,128)(2,1)S(1)} %collective-permute-done.3.refs_5_.refs_2_.refs_6_) | copy-start | bytes 1376260
  58.2 0.8 copy-start.11
  60.3 9.6 %collective-permute-start.13 = (bf16[256,2048]{1,0:T(8,128)(2,1)S(1)}, bf16[256,2048]{1,0:T(8,128)(2,1)}, u32[]{:S(2)}, u32[]{:S(2)}) collective-permute-start(bf16[256,2048]{1,0:T(8,128)(2,1)S(1)} %join.3.refs_5_.refs_0_), channel_id=1, source_target_pairs={{0,1},{1,0},{2,3},{3,2},{4,5},{5,4},{6,7},{7,6},{8,9},{9,8},{10,11... | collective-permute-start | bytes 3145736 | tf_op jit(solution)/shard_map/ppermute | solution.py:42
  61.5 21.1 %collective-permute-start.8 = (bf16[64,3584]{1,0:T(8,128)(2,1)}, bf16[64,3584]{1,0:T(8,128)(2,1)S(1)}, u32[]{:S(2)}, u32[]{:S(2)}) collective-permute-start(bf16[64,3584]{1,0:T(8,128)(2,1)} %copy-done.11), channel_id=1, source_target_pairs={{0,4},{2,0},{4,8},{6,2},{8,12},{10,6},{12,14},{14,10},{1,5},{3,1},... | collective-permute-start | bytes 1376264 | tf_op jit(solution)/shard_map/ppermute | solution.py:37
  63.6 22.2 %collective-permute-start.11 = (bf16[64,3584]{1,0:T(8,128)(2,1)S(1)}, bf16[64,3584]{1,0:T(8,128)(2,1)S(1)}, u32[]{:S(2)}, u32[]{:S(2)}) collective-permute-start(bf16[64,3584]{1,0:T(8,128)(2,1)S(1)} %payload.11.refs_3_.refs_4_), channel_id=1, source_target_pairs={{0,2},{2,6},{4,0},{6,10},{8,4},{10,14},{12,8},{14,12},{1,3},{3,7},... | collective-permute-start | bytes 1376264 | tf_op jit(solution)/shard_map/ppermute | solution.py:37
  63.6 2.0 %copy-start.2 = (f32[2,128,3584]{2,1,0:T(8,128)S(1)}, f32[2,128,3584]{2,1,0:T(8,128)}, u32[]{:S(2)}) copy-start(f32[2,128,3584]{2,1,0:T(8,128)} %copy-done.1) | copy-start | bytes 11010052
  65.6 2.8 %copy-start.3 = (f32[2,128,3584]{2,1,0:T(8,128)S(1)}, f32[2,128,3584]{2,1,0:T(8,128)}, u32[]{:S(2)}) copy-start(f32[2,128,3584]{2,1,0:T(8,128)} %copy-done.1) | copy-start | bytes 11010052
  66.3 21.7 %collective-permute-start.10 = (bf16[64,3584]{1,0:T(8,128)(2,1)S(1)}, bf16[64,3584]{1,0:T(8,128)(2,1)S(1)}, u32[]{:S(2)}, u32[]{:S(2)}) collective-permute-start(bf16[64,3584]{1,0:T(8,128)(2,1)S(1)} %payload.12.refs_4_), channel_id=1, source_target_pairs={{0,4},{2,0},{4,8},{6,2},{8,12},{10,6},{12,14},{14,10},{1,5},{3,1},... | collective-permute-start | bytes 1376264 | tf_op jit(solution)/shard_map/ppermute | solution.py:37
  69.0 21.6 %collective-permute-start.12 = (bf16[64,3584]{1,0:T(8,128)(2,1)S(1)}, bf16[64,3584]{1,0:T(8,128)(2,1)S(1)}, u32[]{:S(2)}, u32[]{:S(2)}) collective-permute-start(bf16[64,3584]{1,0:T(8,128)(2,1)S(1)} %payload.13.refs_2_), channel_id=1, source_target_pairs={{0,2},{2,6},{4,0},{6,10},{8,4},{10,14},{12,8},{14,12},{1,3},{3,7},... | collective-permute-start | bytes 1376264 | tf_op jit(solution)/shard_map/ppermute | solution.py:37
  82.6 8.0 %copy-start = (f32[2,256,3584]{2,1,0:T(8,128)}, f32[2,256,3584]{2,1,0:T(8,128)S(1)}, u32[]{:S(2)}) copy-start(f32[2,256,3584]{2,1,0:T(8,128)S(1)} %fusion.2.refs_2_.refs_3_.refs_15_) | copy-start | bytes 22020100
  82.6 1.9 %copy-start.13 = (bf16[64,3584]{1,0:T(8,128)(2,1)}, bf16[64,3584]{1,0:T(8,128)(2,1)S(1)}, u32[]{:S(2)}) copy-start(bf16[64,3584]{1,0:T(8,128)(2,1)S(1)} %collective-permute-done.8.refs_1_.refs_7_) | copy-start | bytes 1376260
  84.5 24.0 %collective-permute-start.14 = (bf16[64,3584]{1,0:T(8,128)(2,1)}, bf16[64,3584]{1,0:T(8,128)(2,1)}, u32[]{:S(2)}, u32[]{:S(2)}) collective-permute-start(bf16[64,3584]{1,0:T(8,128)(2,1)} %payload.14.refs_3_), channel_id=1, source_target_pairs={{0,4},{2,0},{4,8},{6,2},{8,12},{10,6},{12,14},{14,10},{1,5},{3,1},... | collective-permute-start | bytes 1376264 | tf_op jit(solution)/shard_map/ppermute | solution.py:37
  85.7 1.4 copy-start.14
  87.2 26.3 %collective-permute-start.16 = (bf16[64,3584]{1,0:T(8,128)(2,1)}, bf16[64,3584]{1,0:T(8,128)(2,1)S(1)}, u32[]{:S(2)}, u32[]{:S(2)}) collective-permute-start(bf16[64,3584]{1,0:T(8,128)(2,1)} %payload.15.refs_3_), channel_id=1, source_target_pairs={{0,2},{2,6},{4,0},{6,10},{8,4},{10,14},{12,8},{14,12},{1,3},{3,7},... | collective-permute-start | bytes 1376264 | tf_op jit(solution)/shard_map/ppermute | solution.py:37
  88.0 1.4 copy-start.15
  89.5 2.8 %copy-start.21 = (bf16[1,8,2048]{2,1,0:T(8,128)(2,1)S(1)}, bf16[1,8,2048]{2,1,0:T(8,128)(2,1)}, u32[]{:S(2)}) copy-start(bf16[1,8,2048]{2,1,0:T(8,128)(2,1)} %param.14) | copy-start | bytes 98308
  89.5 17.4 %collective-permute-start.15 = (bf16[64,3584]{1,0:T(8,128)(2,1)}, bf16[64,3584]{1,0:T(8,128)(2,1)}, u32[]{:S(2)}, u32[]{:S(2)}) collective-permute-start(bf16[64,3584]{1,0:T(8,128)(2,1)} %payload.16.refs_3_), channel_id=1, source_target_pairs={{0,4},{2,0},{4,8},{6,2},{8,12},{10,6},{12,14},{14,10},{1,5},{3,1},... | collective-permute-start | bytes 1376264 | tf_op jit(solution)/shard_map/ppermute | solution.py:37
  90.6 0.8 copy-start.16
  91.4 21.6 %collective-permute-start.17 = (bf16[64,3584]{1,0:T(8,128)(2,1)S(1)}, bf16[64,3584]{1,0:T(8,128)(2,1)}, u32[]{:S(2)}, u32[]{:S(2)}) collective-permute-start(bf16[64,3584]{1,0:T(8,128)(2,1)S(1)} %payload.17.refs_2_.after_ref), channel_id=1, source_target_pairs={{0,2},{2,6},{4,0},{6,10},{8,4},{10,14},{12,8},{14,12},{1,3},{3,7},... | collective-permute-start | bytes 1376264 | tf_op jit(solution)/shard_map/ppermute | solution.py:37
  92.9 0.6 copy-start.26
  92.9 10.5 %collective-permute-start.27 = (bf16[4,2048]{1,0:T(4,128)(2,1)S(1)}, bf16[4,2048]{1,0:T(4,128)(2,1)}, u32[]{:S(2)}, u32[]{:S(2)}) collective-permute-start(bf16[4,2048]{1,0:T(4,128)(2,1)S(1)} %dynamic-slice_bitcast_fusion.1), channel_id=1, source_target_pairs={{0,1},{1,0},{2,3},{3,2},{4,5},{5,4},{6,7},{7,6},{8,9},{9,8},{10,11... | collective-permute-start | bytes 49160 | tf_op jit(solution)/shard_map/ppermute | solution.py:42
  94.6 1.0 copy-start.18
  95.6 14.4 %copy-start.4 = (f32[2,128,3584]{2,1,0:T(8,128)S(1)}, f32[2,128,3584]{2,1,0:T(8,128)}, u32[]{:S(2)}) copy-start(f32[2,128,3584]{2,1,0:T(8,128)} %copy-done.1) | copy-start | bytes 11010052
  103.4 9.6 %copy-start.5 = (f32[2,128,3584]{2,1,0:T(8,128)}, f32[2,128,3584]{2,1,0:T(8,128)S(1)}, u32[]{:S(2)}) copy-start(f32[2,128,3584]{2,1,0:T(8,128)S(1)} %fusion.refs_4_.refs_16_) | copy-start | bytes 11010052
  105.2 22.8 %collective-permute-start.28 = (bf16[4,4096]{1,0:T(4,128)(2,1)}, bf16[4,4096]{1,0:T(4,128)(2,1)}, u32[]{:S(2)}, u32[]{:S(2)}) collective-permute-start(bf16[4,4096]{1,0:T(4,128)(2,1)} %pad_maximum_fusion.3), channel_id=1, source_target_pairs={{0,4},{4,8},{8,12},{12,0},{1,5},{5,9},{9,13},{13,1},{2,6},{6,10},{... | collective-permute-start | bytes 98312 | tf_op jit(solution)/shard_map/ppermute | solution.py:42
  106.8 23.0 %collective-permute-start.29 = (bf16[4,4096]{1,0:T(4,128)(2,1)}, bf16[4,4096]{1,0:T(4,128)(2,1)}, u32[]{:S(2)}, u32[]{:S(2)}) collective-permute-start(bf16[4,4096]{1,0:T(4,128)(2,1)} %pad_maximum_fusion.3), channel_id=1, source_target_pairs={{0,8},{4,12},{8,0},{12,4},{1,9},{5,13},{9,1},{13,5},{2,10},{6,14},... | collective-permute-start | bytes 98312 | tf_op jit(solution)/shard_map/ppermute | solution.py:42
  108.5 21.5 %collective-permute-start.30 = (bf16[4,4096]{1,0:T(4,128)(2,1)}, bf16[4,4096]{1,0:T(4,128)(2,1)}, u32[]{:S(2)}, u32[]{:S(2)}) collective-permute-start(bf16[4,4096]{1,0:T(4,128)(2,1)} %pad_maximum_fusion.3), channel_id=1, source_target_pairs={{0,12},{4,0},{8,4},{12,8},{1,13},{5,1},{9,5},{13,9},{2,14},{6,2},{... | collective-permute-start | bytes 98312 | tf_op jit(solution)/shard_map/ppermute | solution.py:42
  113.0 27.0 %collective-permute-start.23 = (bf16[128,3584]{1,0:T(8,128)(2,1)}, bf16[128,3584]{1,0:T(8,128)(2,1)S(1)}, u32[]{:S(2)}, u32[]{:S(2)}) collective-permute-start(bf16[128,3584]{1,0:T(8,128)(2,1)} %payload.18.refs_4_), channel_id=1, source_target_pairs={{0,4},{2,0},{4,8},{6,2},{8,12},{10,6},{12,14},{14,10},{1,5},{3,1},... | collective-permute-start | bytes 2752520 | tf_op jit(solution)/shard_map/ppermute | solution.py:37
  113.5 1.8 %copy-start.12 = (bf16[64,3584]{1,0:T(8,128)(2,1)}, bf16[64,3584]{1,0:T(8,128)(2,1)S(1)}, u32[]{:S(2)}) copy-start(bf16[64,3584]{1,0:T(8,128)(2,1)S(1)} %collective-permute-done.16.refs_1_.refs_13_) | copy-start | bytes 1376260
  115.3 1.6 %copy-start.10 = (bf16[128,3584]{1,0:T(8,128)(2,1)}, bf16[128,3584]{1,0:T(8,128)(2,1)S(1)}, u32[]{:S(2)}) copy-start(bf16[128,3584]{1,0:T(8,128)(2,1)S(1)} %payload.19.refs_17_) | copy-start | bytes 2752516
  115.3 24.7 %collective-permute-start.24 = (bf16[128,3584]{1,0:T(8,128)(2,1)S(1)}, bf16[128,3584]{1,0:T(8,128)(2,1)S(1)}, u32[]{:S(2)}, u32[]{:S(2)}) collective-permute-start(bf16[128,3584]{1,0:T(8,128)(2,1)S(1)} %payload.19.refs_17_), channel_id=1, source_target_pairs={{0,2},{2,6},{4,0},{6,10},{8,4},{10,14},{12,8},{14,12},{1,3},{3,7},... | collective-permute-start | bytes 2752520 | tf_op jit(solution)/shard_map/ppermute | solution.py:37
  116.9 15.1 %copy-start.19 = (bf16[256,2048]{1,0:T(8,128)(2,1)S(1)}, bf16[256,2048]{1,0:T(8,128)(2,1)}, u32[]{:S(2)}) copy-start(bf16[256,2048]{1,0:T(8,128)(2,1)} %x_ref.1) | copy-start | bytes 3145732
  116.9 15.1 %copy-start.20 = (bf16[2048,64]{0,1:T(8,128)(2,1)S(1)}, bf16[2048,64]{0,1:T(8,128)(2,1)}, u32[]{:S(2)}) copy-start(bf16[2048,64]{0,1:T(8,128)(2,1)} %param.12) | copy-start | bytes 786436
  116.9 23.1 %copy-start.24 = (bf16[256,3584]{1,0:T(8,128)(2,1)S(1)}, bf16[256,3584]{1,0:T(8,128)(2,1)}, u32[]{:S(2)}) copy-start(bf16[256,3584]{1,0:T(8,128)(2,1)} %refs_1_.1) | copy-start | bytes 5505028
  116.9 23.1 %copy-start.25 = (bf16[3584,64]{0,1:T(8,128)(2,1)S(1)}, bf16[3584,64]{0,1:T(8,128)(2,1)}, u32[]{:S(2)}) copy-start(bf16[3584,64]{0,1:T(8,128)(2,1)} %param.13) | copy-start | bytes 1376260
  128.0 9.7 %collective-permute-start.20 = (f32[64,128]{1,0:T(8,128)S(1)}, f32[64,128]{1,0:T(8,128)S(1)}, u32[]{:S(2)}, u32[]{:S(2)}) collective-permute-start(f32[64,128]{1,0:T(8,128)S(1)} %get-tuple-element.9), channel_id=1, source_target_pairs={{0,12},{4,0},{8,4},{12,8},{1,13},{5,1},{9,5},{13,9},{2,14},{6,2},{... | collective-permute-start | bytes 98312 | tf_op jit(solution)/shard_map/ppermute | solution.py:42
  129.8 10.0 %collective-permute-start.21 = (f32[64,128]{1,0:T(8,128)S(1)}, f32[64,128]{1,0:T(8,128)S(1)}, u32[]{:S(2)}, u32[]{:S(2)}) collective-permute-start(f32[64,128]{1,0:T(8,128)S(1)} %get-tuple-element.11), channel_id=1, source_target_pairs={{0,8},{4,12},{8,0},{12,4},{1,9},{5,13},{9,1},{13,5},{2,10},{6,14},... | collective-permute-start | bytes 98312 | tf_op jit(solution)/shard_map/ppermute | solution.py:42
  130.0 9.8 %collective-permute-start.22 = (f32[64,128]{1,0:T(8,128)S(1)}, f32[64,128]{1,0:T(8,128)S(1)}, u32[]{:S(2)}, u32[]{:S(2)}) collective-permute-start(f32[64,128]{1,0:T(8,128)S(1)} %get-tuple-element.10), channel_id=1, source_target_pairs={{0,4},{4,8},{8,12},{12,0},{1,5},{5,9},{9,13},{13,1},{2,6},{6,10},{... | collective-permute-start | bytes 98312 | tf_op jit(solution)/shard_map/ppermute | solution.py:42
  132.0 0.9 copy-start.17
  137.7 2.2 %collective-permute-start.18 = (f32[256,64]{1,0:T(8,128)S(1)}, f32[256,64]{1,0:T(8,128)S(1)}, u32[]{:S(2)}, u32[]{:S(2)}) collective-permute-start(f32[256,64]{1,0:T(8,128)S(1)} %projected_inputs.1), channel_id=1, source_target_pairs={{0,1},{1,0},{2,3},{3,2},{4,5},{5,4},{6,7},{7,6},{8,9},{9,8},{10,11... | collective-permute-start | bytes 196616 | tf_op jit(solution)/shard_map/ppermute | solution.py:59
  139.9 5.0 %collective-permute-start.19 = (f32[256,64]{1,0:T(8,128)S(1)}, f32[256,64]{1,0:T(8,128)S(1)}, u32[]{:S(2)}, u32[]{:S(2)}) collective-permute-start(f32[256,64]{1,0:T(8,128)S(1)} %add.185), channel_id=1, source_target_pairs={{0,2},{2,0},{1,3},{3,1},{4,6},{6,4},{5,7},{7,5},{8,10},{10,8},{9,1... | collective-permute-start | bytes 196616 | tf_op jit(solution)/shard_map/ppermute | solution.py:59
  142.5 2.5 %collective-permute-start.25 = (f32[64,256]{1,0:T(8,128)S(1)}, f32[64,256]{1,0:T(8,128)S(1)}, u32[]{:S(2)}, u32[]{:S(2)}) collective-permute-start(f32[64,256]{1,0:T(8,128)S(1)} %pad_maximum_fusion.2), channel_id=1, source_target_pairs={{0,1},{1,0},{2,3},{3,2},{4,5},{5,4},{6,7},{7,6},{8,9},{9,8},{10,11... | collective-permute-start | bytes 196616 | tf_op jit(solution)/shard_map/ppermute | solution.py:59
  145.0 4.3 %collective-permute-start.26 = (f32[64,256]{1,0:T(8,128)S(1)}, f32[64,256]{1,0:T(8,128)S(1)}, u32[]{:S(2)}, u32[]{:S(2)}) collective-permute-start(f32[64,256]{1,0:T(8,128)S(1)} %fusion.32), channel_id=1, source_target_pairs={{0,2},{2,0},{1,3},{3,1},{4,6},{6,4},{5,7},{7,5},{8,10},{10,8},{9,1... | collective-permute-start | bytes 196616 | tf_op jit(solution)/shard_map/ppermute | solution.py:59
